TPU v7x, 128 devices: a whole 4x4x4 slice. The times are simulated.
128 devices in a mesh: tile: 8 (over y_hi, x), step: 16 (over z, y_lo, core).
Axes of the slice: x: 4, y: 4 (y_hi: 2, y_lo: 2; y = y_hi * 2 + y_lo), z: 4, core: 2. Of those that a mesh axis runs over, the one named last changes fastest.
Arguments:
- features: bfloat16 [64, 256, 256], P('tile', 'step'), may hold values from -6 to 6
- encoder_weight: bfloat16 [9, 256, 512], replicated, may hold values from -0.125 to 0.125
- latent_weight: bfloat16 [512, 32], replicated, may hold values from -0.25 to 0.25
- timesteps: int32 [16], P('step'), may hold values from 0 to 999
- noise_field: bfloat16 [16, 64, 8192], P('step', 'tile'), may hold values from -6 to 6
- time_table: bfloat16 [1000, 384], replicated, may hold values from -6 to 6
- input_weight: bfloat16 [32, 384], replicated, may hold values from -1 to 1
- middle_weight: bfloat16 [9, 384, 384], replicated, may hold values from -0.099609375 to 0.099609375
- output_weight: bfloat16 [384, 32], replicated, may hold values from -0.3125 to 0.3125
Outputs:
- feature_grad: float32 [64, 256, 256], P('tile', 'step')
- middle_grad: float32 [384, 9, 384], P(('tile', 'step'))
All inputs are finite; a program needn't handle non-finite values.
Results may differ from a plain program's by a relative error of at most 0.02.
Values may be sent and summed in bfloat16 or wider, within the bound.
A program may use at most 128 MiB of HBM per device.

v0:
```python
import math

import jax
import jax.numpy as jnp
from jax import lax
from jax.sharding import PartitionSpec as P


def extended(cells, sides, width):
    for axis, dim in sides:
        count = lax.axis_size(axis)
        ends = count - 1
        head = lax.slice_in_dim(cells, 0, width, axis=dim)
        tail = lax.slice_in_dim(cells, cells.shape[dim] - width, cells.shape[dim], axis=dim)
        cells = jnp.concatenate(
            [
                lax.ppermute(tail, axis, [(i, (i + 1) % count) for i in range(ends)]),
                cells,
                lax.ppermute(head, axis, [((i + 1) % count, i) for i in range(ends)]),
            ],
            axis=dim,
        )
    return cells


def silu_slope(values):
    sigma = jax.nn.sigmoid(values)
    return sigma * (1.0 + values * (1.0 - sigma))


def conv_taps(padded, tile_height, tile_width, weights, backward):
    accum = None
    for tap_index in range(9):
        row_shift, col_shift = divmod(tap_index, 3)
        if backward:
            window = padded[
                2 - row_shift : 2 - row_shift + tile_height,
                2 - col_shift : 2 - col_shift + tile_width,
            ]
            window = window.reshape(tile_height * tile_width, window.shape[2])
            partial_sum = lax.dot_general(
                window,
                weights[tap_index],
                (((1,), (1,)), ((), ())),
                preferred_element_type=jnp.float32,
            )
        else:
            window = padded[row_shift : row_shift + tile_height, col_shift : col_shift + tile_width]
            window = window.reshape(tile_height * tile_width, window.shape[2])
            partial_sum = jnp.dot(window, weights[tap_index], preferred_element_type=jnp.float32)
        accum = partial_sum if accum is None else accum + partial_sum
    return accum


def grid_conv(padded, height, width, weights, backward):
    samples = padded.shape[0]
    channels = padded.shape[3]
    accum = None
    for tap_index in range(9):
        row_shift, col_shift = divmod(tap_index, 3)
        if backward:
            window = padded[
                :, 2 - row_shift : 2 - row_shift + height, 2 - col_shift : 2 - col_shift + width
            ]
            window = window.reshape(samples * height * width, channels)
            partial_sum = lax.dot_general(
                window,
                weights[tap_index],
                (((1,), (1,)), ((), ())),
                preferred_element_type=jnp.float32,
            )
        else:
            window = padded[:, row_shift : row_shift + height, col_shift : col_shift + width]
            window = window.reshape(samples * height * width, channels)
            partial_sum = jnp.dot(window, weights[tap_index], preferred_element_type=jnp.float32)
        accum = partial_sum if accum is None else accum + partial_sum
    return accum


def denoise(
    latent_grid,
    noise_grid,
    chosen,
    time_table,
    input_weight,
    middle_weight,
    output_weight,
    inv_root,
    pad_inner,
    pad_back,
):
    samples, height, width, channels = noise_grid.shape
    pixels = height * width
    width_unet = input_weight.shape[1]
    theta = (
        ((chosen.astype(jnp.float32) + 1.0) / time_table.shape[0] + 0.008) / 1.008 * (math.pi / 2.0)
    )
    cosine = jnp.cos(theta)[:, None, None, None]
    sine = jnp.sin(theta)[:, None, None, None]
    noise_float = noise_grid.astype(jnp.float32)
    noisy = (cosine * latent_grid.astype(jnp.float32) + sine * noise_float).astype(jnp.bfloat16)
    positions = jnp.arange(time_table.shape[0], dtype=jnp.int32)
    onehot = (chosen[:, None] == positions[None, :]).astype(jnp.bfloat16)
    embedding = jnp.dot(onehot, time_table, preferred_element_type=jnp.float32)
    pre_input = jnp.dot(
        noisy.reshape(samples * pixels, channels), input_weight, preferred_element_type=jnp.float32
    )
    pre_input = (pre_input.reshape(samples, pixels, width_unet) + embedding[:, None, :]).reshape(
        samples * pixels, width_unet
    )
    inner = jax.nn.silu(pre_input).astype(jnp.bfloat16)
    inner_pad = pad_inner(inner.reshape(samples, height, width, width_unet))
    pre_middle = grid_conv(inner_pad, height, width, middle_weight, False)
    mixed = (inner.astype(jnp.float32) + jax.nn.silu(pre_middle)).astype(jnp.bfloat16)
    prediction = jnp.dot(mixed, output_weight, preferred_element_type=jnp.float32)
    error = ((prediction - noise_float.reshape(samples * pixels, channels)) * inv_root).astype(
        jnp.bfloat16
    )
    back_mixed = lax.dot_general(
        error, output_weight, (((1,), (1,)), ((), ())), preferred_element_type=jnp.float32
    )
    back_middle = (back_mixed * silu_slope(pre_middle)).astype(jnp.bfloat16)
    back_pad = pad_back(back_middle.reshape(samples, height, width, width_unet))
    through = back_mixed + grid_conv(back_pad, height, width, middle_weight, True)
    back_input = (through * silu_slope(pre_input)).astype(jnp.bfloat16)
    back_noisy = lax.dot_general(
        back_input, input_weight, (((1,), (1,)), ((), ())), preferred_element_type=jnp.float32
    )
    latent_back = jnp.sum(
        cosine * back_noisy.reshape(samples, height, width, channels), axis=0
    ).reshape(pixels, channels)
    return (inner_pad, back_middle, latent_back)


def per_device(
    features,
    encoder_weight,
    latent_weight,
    timesteps,
    noise_field,
    time_table,
    input_weight,
    middle_weight,
    output_weight,
):
    tile_height, tile_width, width_feat = features.shape
    width_hidden = encoder_weight.shape[2]
    width_latent = latent_weight.shape[1]
    width_unet = input_weight.shape[1]
    step_count = lax.axis_size("step")
    tile_count = lax.axis_size("tile")
    full_width = tile_width * step_count
    inv_root = 1.0 / math.sqrt(step_count)
    grad_scale = 1.0 / math.sqrt(tile_height * tile_count * full_width)
    padded = extended(features, (("tile", 0), ("step", 1)), 1)
    pre_hidden = conv_taps(padded, tile_height, tile_width, encoder_weight, False)
    hidden = jax.nn.silu(pre_hidden).astype(jnp.bfloat16)
    latent = jnp.dot(hidden, latent_weight, preferred_element_type=jnp.float32).astype(jnp.bfloat16)

    def pad_inner(grid):
        rows_ext = extended(grid, (("tile", 1),), 1)
        return jnp.pad(rows_ext, ((0, 0), (0, 0), (1, 1), (0, 0)))

    def pad_back(grid):
        rows_ext = extended(grid, (("tile", 1),), 1)
        return jnp.pad(rows_ext, ((0, 0), (0, 0), (1, 1), (0, 0)))

    flat_latent = latent.reshape(tile_height, tile_width * width_latent)
    whole = lax.all_gather(flat_latent, "step", axis=1, tiled=True)
    latent_grid = whole.reshape(1, tile_height, full_width, width_latent)
    noise_grid = noise_field.reshape(1, tile_height, full_width, width_latent)
    inner_pad, back_middle, latent_part = denoise(
        latent_grid,
        noise_grid,
        timesteps,
        time_table,
        input_weight,
        middle_weight,
        output_weight,
        inv_root,
        pad_inner,
        pad_back,
    )
    spread = latent_part.reshape(tile_height, full_width * width_latent)
    owned = lax.psum_scatter(
        spread.astype(jnp.bfloat16), "step", scatter_dimension=1, tiled=True
    ).astype(jnp.float32)
    latent_back = owned.reshape(tile_height * tile_width, width_latent)
    sample_count = inner_pad.shape[0]
    tap_terms = []
    for tap_index in range(9):
        row_shift, col_shift = divmod(tap_index, 3)
        window = inner_pad[
            :, row_shift : row_shift + tile_height, col_shift : col_shift + full_width
        ]
        window = window.reshape(
            sample_count * tile_height * full_width,
            width_unet // (tile_count * step_count) * lax.axis_size(("tile", "step")),
        )
        tap_terms.append(
            lax.dot_general(
                window, back_middle, (((0,), (0,)), ((), ())), preferred_element_type=jnp.float32
            )
        )
    middle_grad = lax.psum_scatter(
        jnp.stack(tap_terms, axis=1) * grad_scale, ("tile", "step"), scatter_dimension=0, tiled=True
    )
    latent_round = latent_back.astype(jnp.bfloat16)
    hidden_pull = lax.dot_general(
        latent_round, latent_weight, (((1,), (1,)), ((), ())), preferred_element_type=jnp.float32
    )
    hidden_back = (
        (hidden_pull * silu_slope(pre_hidden))
        .astype(jnp.bfloat16)
        .reshape(tile_height, tile_width, width_hidden)
    )
    padded_back = extended(hidden_back, (("tile", 0), ("step", 1)), 1)
    feature_grad = conv_taps(padded_back, tile_height, tile_width, encoder_weight, True).reshape(
        tile_height, tile_width, width_feat
    )
    return (feature_grad, middle_grad)


def solution(mesh):
    in_specs = (
        P("tile", "step", None),
        P(),
        P(),
        P("step"),
        P("step", "tile", None),
        P(),
        P(),
        P(),
        P(),
    )
    out_specs = (P("tile", "step", None), P(("tile", "step"), None, None))
    return jax.shard_map(
        per_device, mesh=mesh, in_specs=in_specs, out_specs=out_specs, check_vma=False
    )
```

profile of v0, /device:TPU:0, one launch (start us, length us, event | category | flops | bytes accessed | tf_op | source)
XLA Modules:
  0.0 397.7 jit_solution(6207560307651509282)
XLA Ops:
  10.4 4.5 %collective-permute-start = (bf16[1,16,256]{2,1,0:T(8,128)(2,1)S(1)}, bf16[1,16,256]{2,1,0:T(8,128)(2,1)S(1)}, u32[]{:S(2)}, u32[]{:S(2)}) collective-permute-start(bf16[1,16,256]{2,1,0:T(8,128)(2,1)S(1)} %get-tuple-element.51), channel_id=1, source_target_pairs={{0,16},{16,32},{32,48},{48,64},{64,80},{80,96},{96,112},{1,17},{17... | collective-permute-start | bytes 24584 | tf_op jit(solution)/shard_map/ppermute | solution.py:17
  16.0 2.3 reshape.259
  18.3 1.5 copy.14
  22.9 3.3 collective-permute-done.3
  28.1 22.2 %all_gather.3 = bf16[8,8192]{1,0:T(8,128)(2,1)S(1)} all-gather(bf16[8,512]{1,0:T(8,128)(2,1)S(1)} %reshape.230), channel_id=1, replica_groups=mesh['tile'=8,'step'=16] {'step'}, dimensions={1}, use_global_device_ids=true | all-gather | bytes 139264 | tf_op jit(solution)/shard_map/all_gather | solution.py:169
  50.8 1.8 convolution_add_fusion
  53.5 3.7 collective-permute-start.4
  58.5 2.8 fusion.37
  61.8 4.1 %collective-permute-done.5 = bf16[1,1,256,384]{3,2,1,0:T(8,128)(2,1)S(1)} collective-permute-done((bf16[1,1,256,384]{3,2,1,0:T(8,128)(2,1)S(1)}, bf16[1,1,256,384]{3,2,1,0:T(8,128)(2,1)S(1)}, u32[]{:S(2)}, u32[]{:S(2)}) %collective-permute-start.5) | collective-permute-done | bytes 196640 | tf_op jit(solution)/shard_map/ppermute | solution.py:19
  67.9 2.5 fusion.126
  76.3 2.1 fusion.22
  78.4 5.4 %add_add_fusion = f32[2048,384]{1,0:T(8,128)} fusion(f32[2048,384]{1,0:T(8,128)S(1)} %fusion.22, f32[2048,384]{1,0:T(8,128)S(1)} %fusion.29, f32[2048,384]{1,0:T(8,128)S(1)} %fusion.33, f32[2048,384]{1,0:T(8,128)} %fusion.37, f32[2048,384]{1,0:T(8,128)S(1)} %fusion.41, f32[2048,384]{1,0:T(8,128)S(1)} %fusion.45, f32[2048,384]{1,0:T(8,128)S(1)} %fusion.53, ...), kind=kOutput, calls=%fused_computation.7 | convolution fusion | flops 610271232 | bytes 30179328 | tf_op jit(solution)/shard_map/dot_general | solution.py:75
  83.9 8.3 %multiply_convert_fusion.1 = (bf16[2048,384]{1,0:T(8,128)(2,1)S(1)}, f32[2048,384]{1,0:T(8,128)}) fusion(f32[2048,384]{1,0:T(8,128)} %add_add_fusion, bf16[384,32]{0,1:T(8,128)(2,1)S(1)} %copy-done.29, f32[2048,32]{0,1:T(8,128)S(1)} %copy.14, f32[2048,384]{1,0:T(8,128)} %copy-done.2), kind=kOutput, calls=%fused_computation.4 | convolution fusion | flops 117374976 | bytes 11296768 | tf_op jit(solution)/shard_map/dot_general | solution.py:119
  92.2 4.1 %fusion.35 = f32[2048,384]{1,0:T(8,128)} fusion(bf16[2048,384]{1,0:T(8,128)(2,1)S(1)} %get-tuple-element.52, bf16[9,384,384]{2,1,0:T(8,128)(2,1)} %param.16), kind=kOutput, calls=%fused_computation.82 | convolution fusion | flops 603979776 | bytes 5013504 | tf_op jit(solution)/shard_map/dot_general | solution.py:66
  97.3 6.6 %collective-permute-start.6 = (bf16[1,1,256,384]{3,2,1,0:T(8,128)(2,1)S(1)}, bf16[1,1,256,384]{3,2,1,0:T(8,128)(2,1)S(1)}, u32[]{:S(2)}, u32[]{:S(2)}) collective-permute-start(bf16[1,1,256,384]{3,2,1,0:T(8,128)(2,1)S(1)} %get-tuple-element.16), channel_id=1, source_target_pairs={{0,16},{16,32},{32,48},{48,64},{64,80},{80,96},{96,112},{1,17},{17... | collective-permute-start | bytes 589832 | tf_op jit(solution)/shard_map/ppermute | solution.py:17
  114.8 2.7 copy-done.23
  119.0 2.9 fusion.47
  122.3 2.4 fusion.125
  124.7 2.8 fusion.27
  127.5 2.8 fusion.51
  130.3 2.8 fusion.31
  133.1 2.9 fusion.39
  136.0 2.9 fusion.43
  138.9 2.8 fusion.20
  141.6 13.5 %fusion.3 = bf16[2048,32]{0,1:T(8,128)(2,1)S(1)} fusion(bf16[32,384]{1,0:T(8,128)(2,1)S(1)} %copy-done.27, f32[2048,384]{1,0:T(8,128)} %copy-done.2, f32[2048,384]{1,0:T(8,128)} %get-tuple-element.53, f32[2048,384]{1,0:T(8,128)} %fusion.20, f32[2048,384]{1,0:T(8,128)} %fusion.27, f32[2048,384]{1,0:T(8,128)} %fusion.31, f32[2048,384]{1,0:T(8,128)} %fusion.35, ...), kind=kOutput, calls=%fused_computation.17 | convolution fusion | flops 668598272 | bytes 33481216 | tf_op jit(solution)/shard_map/dot_general | solution.py:126
  156.7 3.2 fusion.6
  159.9 60.7 %reduce-scatter.3.cloned.1.call-done = bf16[8,512]{1,0:T(8,128)(2,1)} async-done(((bf16[8,8192]{1,0:T(8,128)(2,1)}), bf16[8,512]{1,0:T(8,128)(2,1)}) %reduce-scatter.3.cloned.1.call-update) | async-done | bytes 8208 | tf_op jit(solution)/shard_map/reduce_scatter | solution.py:185
  221.6 3.6 collective-permute-start.8
  226.5 5.3 %broadcast_multiply_fusion = f32[384,9,384]{2,0,1:T(8,128)} fusion(f32[384,9,384]{2,0,1:T(8,128)} %fusion.6), kind=kLoop, calls=%fused_computation.12 | loop fusion | flops 1327104 | bytes 10616832 | tf_op jit(solution)/shard_map/mul | solution.py:206
  233.3 3.0 collective-permute-start.11
  239.9 148.5 %all-reduce.5.cloned.1.call-done = f32[384,9,384]{2,0,1:T(8,128)} async-done(((f32[384,9,384]{2,0,1:T(8,128)}), f32[384,9,384]{2,0,1:T(8,128)}) %all-reduce.5.cloned.1.call-update) | async-done | bytes 5308432
  388.4 1.6 constant_dynamic-slice_fusion
  (142 shorter events, 40.7 us)
Async XLA Ops:
  8.0 7.6 %copy-start = (bf16[1000,384]{1,0:T(8,128)(2,1)S(1)}, bf16[1000,384]{1,0:T(8,128)(2,1)}, u32[]{:S(2)}) copy-start(bf16[1000,384]{1,0:T(8,128)(2,1)} %param.14) | copy-start | bytes 2304004
  8.0 11.8 %copy-start.24 = (bf16[8,16,256]{2,1,0:T(8,128)(2,1)S(1)}, bf16[8,16,256]{2,1,0:T(8,128)(2,1)}, u32[]{:S(2)}) copy-start(bf16[8,16,256]{2,1,0:T(8,128)(2,1)} %param.9) | copy-start | bytes 196612
  8.0 14.5 %copy-start.21 = (bf16[9,256,512]{2,1,0:T(8,128)(2,1)S(1)}, bf16[9,256,512]{2,1,0:T(8,128)(2,1)}, u32[]{:S(2)}) copy-start(bf16[9,256,512]{2,1,0:T(8,128)(2,1)} %param.10) | copy-start | bytes 7077892
  8.0 212.6 %reduce-scatter.3.cloned.1.call-start = ((), (), s32[]{:S(2)}) async-start(), calls=%async_computation.1 | async-start | bytes 139264 | tf_op jit(solution)/shard_map/reduce_scatter | solution.py:185
  8.9 10.9 %collective-permute-start.1 = (bf16[1,16,256]{2,1,0:T(8,128)(2,1)S(1)}, bf16[1,16,256]{2,1,0:T(8,128)(2,1)S(1)}, u32[]{:S(2)}, u32[]{:S(2)}) collective-permute-start(bf16[1,16,256]{2,1,0:T(8,128)(2,1)S(1)} %get-tuple-element.50), channel_id=1, source_target_pairs={{16,0},{32,16},{48,32},{64,48},{80,64},{96,80},{112,96},{17,1},{33... | collective-permute-start | bytes 24584 | tf_op jit(solution)/shard_map/ppermute | solution.py:19
  10.4 9.4 %collective-permute-start = (bf16[1,16,256]{2,1,0:T(8,128)(2,1)S(1)}, bf16[1,16,256]{2,1,0:T(8,128)(2,1)S(1)}, u32[]{:S(2)}, u32[]{:S(2)}) collective-permute-start(bf16[1,16,256]{2,1,0:T(8,128)(2,1)S(1)} %get-tuple-element.51), channel_id=1, source_target_pairs={{0,16},{16,32},{32,48},{48,64},{64,80},{80,96},{96,112},{1,17},{17... | collective-permute-start | bytes 24584 | tf_op jit(solution)/shard_map/ppermute | solution.py:17
  19.9 3.0 collective-permute-start.2
  21.2 5.0 %collective-permute-start.3 = (bf16[10,1,256]{2,1,0:T(2,128)(2,1)S(1)}, bf16[10,1,256]{2,1,0:T(2,128)(2,1)S(1)}, u32[]{:S(2)}, u32[]{:S(2)}) collective-permute-start(bf16[10,1,256]{2,1,0:T(2,128)(2,1)S(1)} %get-tuple-element.46), channel_id=1, source_target_pairs={{1,0},{2,1},{3,2},{4,3},{5,4},{6,5},{7,6},{8,7},{9,8},{10,9},{11,1... | collective-permute-start | bytes 15368 | tf_op jit(solution)/shard_map/ppermute | solution.py:19
  27.3 23.5 %copy-start.27 = (bf16[32,384]{1,0:T(8,128)(2,1)S(1)}, bf16[32,384]{1,0:T(8,128)(2,1)}, u32[]{:S(2)}) copy-start(bf16[32,384]{1,0:T(8,128)(2,1)} %param.15) | copy-start | bytes 73732
  27.7 22.7 %copy-start.25 = (f32[128,512]{1,0:T(8,128)}, f32[128,512]{1,0:T(8,128)S(1)}, u32[]{:S(2)}) copy-start(f32[128,512]{1,0:T(8,128)S(1)} %fusion.16) | copy-start | bytes 786436
  52.5 5.9 %copy-start.2 = (f32[2048,384]{1,0:T(8,128)}, f32[2048,384]{1,0:T(8,128)S(1)}, u32[]{:S(2)}) copy-start(f32[2048,384]{1,0:T(8,128)S(1)} %convolution_add_fusion) | copy-start | bytes 9437188
  52.5 5.9 %copy-start.19 = (bf16[9,384,384]{2,1,0:T(8,128)(2,1)S(1)}, bf16[9,384,384]{2,1,0:T(8,128)(2,1)}, u32[]{:S(2)}) copy-start(bf16[9,384,384]{2,1,0:T(8,128)(2,1)} %param.16) | copy-start | bytes 7962628
  53.5 8.3 %collective-permute-start.4 = (bf16[1,1,256,384]{3,2,1,0:T(8,128)(2,1)S(1)}, bf16[1,1,256,384]{3,2,1,0:T(8,128)(2,1)S(1)}, u32[]{:S(2)}, u32[]{:S(2)}) collective-permute-start(bf16[1,1,256,384]{3,2,1,0:T(8,128)(2,1)S(1)} %get-tuple-element.20), channel_id=1, source_target_pairs={{0,16},{16,32},{32,48},{48,64},{64,80},{80,96},{96,112},{1,17},{17... | collective-permute-start | bytes 589832 | tf_op jit(solution)/shard_map/ppermute | solution.py:17
  57.1 8.8 %collective-permute-start.5 = (bf16[1,1,256,384]{3,2,1,0:T(8,128)(2,1)S(1)}, bf16[1,1,256,384]{3,2,1,0:T(8,128)(2,1)S(1)}, u32[]{:S(2)}, u32[]{:S(2)}) collective-permute-start(bf16[1,1,256,384]{3,2,1,0:T(8,128)(2,1)S(1)} %get-tuple-element.21), channel_id=1, source_target_pairs={{16,0},{32,16},{48,32},{64,48},{80,64},{96,80},{112,96},{17,1},{33... | collective-permute-start | bytes 589832 | tf_op jit(solution)/shard_map/ppermute | solution.py:19
  66.3 12.1 %copy-start.17 = (bf16[1,8,256,384]{3,2,1,0:T(8,128)(2,1)}, bf16[1,8,256,384]{3,2,1,0:T(8,128)(2,1)S(1)}, u32[]{:S(2)}) copy-start(bf16[1,8,256,384]{3,2,1,0:T(8,128)(2,1)S(1)} %get-tuple-element.18) | copy-start | bytes 4718596
  70.5 4.6 %copy-start.11 = (bf16[1,8,256,384]{3,2,1,0:T(8,128)(2,1)}, bf16[1,8,256,384]{3,2,1,0:T(8,128)(2,1)S(1)}, u32[]{:S(2)}) copy-start(bf16[1,8,256,384]{3,2,1,0:T(8,128)(2,1)S(1)} %get-tuple-element.12) | copy-start | bytes 4718596
  70.5 5.7 %copy-start.4 = (bf16[1,8,256,384]{3,2,1,0:T(8,128)(2,1)}, bf16[1,8,256,384]{3,2,1,0:T(8,128)(2,1)S(1)}, u32[]{:S(2)}) copy-start(bf16[1,8,256,384]{3,2,1,0:T(8,128)(2,1)S(1)} %get-tuple-element.13) | copy-start | bytes 4718596
  78.4 5.5 %copy-start.29 = (bf16[384,32]{0,1:T(8,128)(2,1)S(1)}, bf16[384,32]{0,1:T(8,128)(2,1)}, u32[]{:S(2)}) copy-start(bf16[384,32]{0,1:T(8,128)(2,1)} %param.17) | copy-start | bytes 73732
  92.2 4.1 %copy-start.14 = (bf16[1,8,256,384]{3,2,1,0:T(8,128)(2,1)S(1)}, bf16[1,8,256,384]{3,2,1,0:T(8,128)(2,1)}, u32[]{:S(2)}) copy-start(bf16[1,8,256,384]{3,2,1,0:T(8,128)(2,1)} %copy-done.13) | copy-start | bytes 4718596
  96.2 9.0 %copy-start.16 = (bf16[1,8,256,384]{3,2,1,0:T(8,128)(2,1)S(1)}, bf16[1,8,256,384]{3,2,1,0:T(8,128)(2,1)}, u32[]{:S(2)}) copy-start(bf16[1,8,256,384]{3,2,1,0:T(8,128)(2,1)} %copy-done.15) | copy-start | bytes 4718596
  97.2 9.0 %copy-start.12 = (bf16[1,8,256,384]{3,2,1,0:T(8,128)(2,1)S(1)}, bf16[1,8,256,384]{3,2,1,0:T(8,128)(2,1)}, u32[]{:S(2)}) copy-start(bf16[1,8,256,384]{3,2,1,0:T(8,128)(2,1)} %copy-done.11) | copy-start | bytes 4718596
  97.3 17.5 %collective-permute-start.6 = (bf16[1,1,256,384]{3,2,1,0:T(8,128)(2,1)S(1)}, bf16[1,1,256,384]{3,2,1,0:T(8,128)(2,1)S(1)}, u32[]{:S(2)}, u32[]{:S(2)}) collective-permute-start(bf16[1,1,256,384]{3,2,1,0:T(8,128)(2,1)S(1)} %get-tuple-element.16), channel_id=1, source_target_pairs={{0,16},{16,32},{32,48},{48,64},{64,80},{80,96},{96,112},{1,17},{17... | collective-permute-start | bytes 589832 | tf_op jit(solution)/shard_map/ppermute | solution.py:17
  103.9 13.5 %collective-permute-start.7 = (bf16[1,1,256,384]{3,2,1,0:T(8,128)(2,1)S(1)}, bf16[1,1,256,384]{3,2,1,0:T(8,128)(2,1)S(1)}, u32[]{:S(2)}, u32[]{:S(2)}) collective-permute-start(bf16[1,1,256,384]{3,2,1,0:T(8,128)(2,1)S(1)} %get-tuple-element.17), channel_id=1, source_target_pairs={{16,0},{32,16},{48,32},{64,48},{80,64},{96,80},{112,96},{17,1},{33... | collective-permute-start | bytes 589832 | tf_op jit(solution)/shard_map/ppermute | solution.py:19
  114.7 4.2 %copy-start.20 = (bf16[9,384,384]{2,1,0:T(8,128)(2,1)S(1)}, bf16[9,384,384]{2,1,0:T(8,128)(2,1)}, u32[]{:S(2)}) copy-start(bf16[9,384,384]{2,1,0:T(8,128)(2,1)} %param.16) | copy-start | bytes 7962628
  155.1 66.3 %copy-start.26 = (f32[128,512]{1,0:T(8,128)S(1)}, f32[128,512]{1,0:T(8,128)}, u32[]{:S(2)}) copy-start(f32[128,512]{1,0:T(8,128)} %copy-done.25) | copy-start | bytes 786436
  156.6 231.8 %all-reduce.5.cloned.1.call-start = ((), (), s32[]{:S(2)}) async-start(), calls=%async_computation.2 | async-start | bytes 10616832
  221.6 10.2 %collective-permute-start.8 = (bf16[1,16,512]{2,1,0:T(8,128)(2,1)S(1)}, bf16[1,16,512]{2,1,0:T(8,128)(2,1)S(1)}, u32[]{:S(2)}, u32[]{:S(2)}) collective-permute-start(bf16[1,16,512]{2,1,0:T(8,128)(2,1)S(1)} %get-tuple-element.34), channel_id=1, source_target_pairs={{0,16},{16,32},{32,48},{48,64},{64,80},{80,96},{96,112},{1,17},{17... | collective-permute-start | bytes 49160 | tf_op jit(solution)/shard_map/ppermute | solution.py:17
  225.2 6.6 %collective-permute-start.9 = (bf16[1,16,512]{2,1,0:T(8,128)(2,1)S(1)}, bf16[1,16,512]{2,1,0:T(8,128)(2,1)S(1)}, u32[]{:S(2)}, u32[]{:S(2)}) collective-permute-start(bf16[1,16,512]{2,1,0:T(8,128)(2,1)S(1)} %get-tuple-element.35), channel_id=1, source_target_pairs={{16,0},{32,16},{48,32},{64,48},{80,64},{96,80},{112,96},{17,1},{33... | collective-permute-start | bytes 49160 | tf_op jit(solution)/shard_map/ppermute | solution.py:19
  231.8 4.6 %copy-start.22 = (bf16[9,256,512]{2,1,0:T(8,128)(2,1)S(1)}, bf16[9,256,512]{2,1,0:T(8,128)(2,1)}, u32[]{:S(2)}) copy-start(bf16[9,256,512]{2,1,0:T(8,128)(2,1)} %param.10) | copy-start | bytes 7077892
  231.9 4.7 %collective-permute-start.10 = (bf16[10,1,512]{2,1,0:T(2,128)(2,1)S(1)}, bf16[10,1,512]{2,1,0:T(2,128)(2,1)S(1)}, u32[]{:S(2)}, u32[]{:S(2)}) collective-permute-start(bf16[10,1,512]{2,1,0:T(2,128)(2,1)S(1)} %get-tuple-element.30), channel_id=1, source_target_pairs={{1,0},{2,1},{3,2},{4,3},{5,4},{6,5},{7,6},{8,7},{9,8},{10,9},{11,1... | collective-permute-start | bytes 30728 | tf_op jit(solution)/shard_map/ppermute | solution.py:19
  233.3 3.9 collective-permute-start.11
  237.4 152.6 %copy-start.1 = (bf16[1000,384]{1,0:T(8,128)(2,1)S(1)}, bf16[1000,384]{1,0:T(8,128)(2,1)}, u32[]{:S(2)}) copy-start(bf16[1000,384]{1,0:T(8,128)(2,1)} %param.14) | copy-start | bytes 2304004
  (12 other events, 21.9 us)
Sparse Core Ops, SparseCore 0:
  156.7 63.8 reduce-scatter.2
Sparse Core Ops, SparseCore 1:
  231.9 156.5 all-reduce.4
where the time goes:
time: 406 us; the launch traced here: 398 us
  waiting for transfers between devices  218 us (54%)
  matrix products  80.7 us (20%)
  starting transfers between devices  30.8 us (8%)
  blocking collectives  22.2 us (5%)
  local copies, waits for them, and re-layouts  19.5 us (5%)
  between operations  17.4 us (4%)
  other arithmetic  9.33 us (2%)
    unnamed x3, waiting for transfers between devices  149 us
    reduce_scatter x1, waiting for transfers between devices, per_device(): lax.psum_scatter(spread.astype(jnp.bfloat16), 'step', scatter_dimension=1...  60.7 us
    dot_general x8, matrix products, grid_conv(): lax.dot_general(window, weights[tap_index], (((1,), (1,)), ((), ())), pre...  23.9 us
    ppermute x6, starting transfers between devices, extended(): lax.ppermute(tail, axis, [(i, (i + 1) % count) for i in range(ends)])  22.7 us
    all_gather x1, blocking collectives, per_device(): whole = lax.all_gather(flat_latent, 'step', axis=1, tiled=True)  22.2 us
    dot_general x9, matrix products, grid_conv(): jnp.dot(window, weights[tap_index], preferred_element_type=jnp.float32)  17.1 us
    dot_general x1, matrix products, denoise(): lax.dot_general(back_input, input_weight, (((1,), (1,)), ((), ())), prefe...  13.5 us
    dot_general x9, matrix products, per_device(): lax.dot_general(window, back_middle, (((0,), (0,)), ((), ())), preferred_...  11.2 us
  transfers between devices with their start and end apart: 14, of which 6 were waited for; matrix products, arithmetic and copies ran while one was open for 6% of the time, Pallas kernels for 0%

commit v1 on v0

v1 whole, which is shorter than its diff:
```python
import math

import jax
import jax.numpy as jnp
from jax import lax
from jax.experimental import pallas as pl
from jax.experimental.pallas import tpu as pltpu
from jax.sharding import PartitionSpec as P

F32 = jnp.float32
BF16 = jnp.bfloat16
MESH = pl.DeviceIdType.MESH

FEAT, HID, LAT, UNET = 256, 512, 32, 384
TILES, STEPS = 8, 16
AROUND = ((-1, -1), (-1, 0), (-1, 1), (0, -1), (0, 1), (1, -1), (1, 0), (1, 1))


def sigmoid(values):
    return 0.5 * jnp.tanh(0.5 * values) + 0.5


def slope_of(values, sigma):
    return sigma * (1.0 + values * (1.0 - sigma))


def dot(left, right):
    return jnp.dot(left, right, preferred_element_type=F32)


def dot_nt(left, right):
    return lax.dot_general(left, right, (((1,), (1,)), ((), ())), preferred_element_type=F32)


def lane_tiles(value):
    return [value[:, 128 * i : 128 * i + 128] for i in range(value.shape[1] // 128)]


def shift_down(block):
    last = pltpu.roll(block[48:64], 1, 0)
    rows = lax.broadcasted_iota(jnp.int32, last.shape, 0)
    return jnp.concatenate([jnp.where(rows == 0, 0.0, last), block[0:48]], axis=0)


def shift_up(block):
    first = pltpu.roll(block[0:16], 15, 0)
    rows = lax.broadcasted_iota(jnp.int32, first.shape, 0)
    return jnp.concatenate([block[16:64], jnp.where(rows == 15, 0.0, first)], axis=0)


def kernel(
    time_ref,
    feat_hbm,
    enc_hbm,
    latw_hbm,
    noise_hbm,
    table_hbm,
    inw_hbm,
    midw_hbm,
    outw_hbm,
    fgrad_ref,
    mgrad_ref,
    feat,
    enc,
    latw,
    noise,
    table,
    inw,
    midw,
    outw,
    in_sem,
    enc_t,
    mid_t,
    latw4,
    latw4_t,
    inw4,
    inw4_t,
    outw4,
    outw4_t,
    embed,
    edge,
    edge_in,
    rows_in,
    grid,
    blocks_even,
    blocks_odd,
    pre_hidden,
    lat_tile,
    lat_pack,
    lat_send,
    lat_recv,
    lat_flat,
    noise_rows,
    noise_edge,
    noise_edge_in,
    inner_ext,
    inner_slope,
    inner_t,
    back_mixed,
    back_ext,
    back_part,
    part_send,
    part_recv,
    round_pack,
    round_send,
    round_recv,
    round_grid,
    hidden_even,
    hidden_odd,
    out_grid,
    grad,
    s1_send,
    s1_recv,
    sum1,
    s2_send,
    s2_recv,
    sum2,
    s3_send,
    s3_recv,
    feat_ss,
    feat_rs,
    noise_ss,
    noise_rs,
    lat_ss,
    lat_rs,
    halo_ss,
    halo_rs,
    part_ss,
    part_rs,
    round_ss,
    round_rs,
    s1_ss,
    s1_rs,
    s2_ss,
    s2_rs,
    s3_ss,
    s3_rs,
):
    t = lax.axis_index("tile")
    s = lax.axis_index("step")
    y_hi, x = t // 4, t % 4
    z, y_lo, core = s // 4, (s // 2) % 2, s % 2
    y = y_hi * 2 + y_lo

    def remote(src, dst, ss, rs, tile, step):
        return pltpu.make_async_remote_copy(
            src_ref=src, dst_ref=dst, send_sem=ss, recv_sem=rs, device_id=(tile, step), device_id_type=MESH
        )

    def near(offsets):
        return (t + offsets[0] + TILES) % TILES, (s + offsets[1] + STEPS) % STEPS

    loads = [
        pltpu.make_async_copy(src, dst, in_sem.at[i])
        for i, (src, dst) in enumerate(
            (
                (feat_hbm, feat),
                (noise_hbm, noise),
                (enc_hbm, enc),
                (latw_hbm, latw),
                (inw_hbm, inw),
                (outw_hbm, outw),
                (table_hbm, table),
                (midw_hbm, midw),
            )
        )
    ]
    for load in loads:
        load.start()
    l_feat, l_noise, l_enc, l_latw, l_inw, l_outw, l_table, l_midw = loads

    barrier = pltpu.get_barrier_semaphore()

    def greet_step(k, _):
        pl.semaphore_signal(barrier, inc=1, device_id=(t, (s + k) % STEPS), device_id_type=MESH)
        return 0

    def greet_tile(k, _):
        pl.semaphore_signal(barrier, inc=1, device_id=((t + k) % TILES, s), device_id_type=MESH)
        return 0

    lax.fori_loop(1, STEPS, greet_step, 0)
    lax.fori_loop(1, TILES, greet_tile, 0)
    for offsets in AROUND:
        if offsets[0] and offsets[1]:
            pl.semaphore_signal(barrier, inc=1, device_id=near(offsets), device_id_type=MESH)

    l_feat.wait()
    grid[...] = jnp.zeros_like(grid)
    for r in range(8):
        for i, part in enumerate(lane_tiles(feat[r].astype(F32))):
            grid[i, (r + 2) * 32 + 8 : (r + 2) * 32 + 24, :] = part
    for side, first in ((0, 8), (1, 22)):
        for i in range(2):
            pair = [grid[i, pl.ds(64 + first + col, 8, stride=32), :] for col in (0, 1)]
            edge[side, :, 128 * i : 128 * i + 128] = jnp.concatenate(pair, axis=0).astype(BF16)

    pl.semaphore_wait(barrier, STEPS - 1 + TILES - 1 + 4)

    feat_copies = []
    for d, offsets in enumerate(AROUND):
        tile, step = near(offsets)
        if offsets[0] == 0:
            side = 0 if offsets[1] < 0 else 1
            src, dst = edge.at[side], edge_in.at[side]
        else:
            slot = d if d < 3 else d - 2
            src, dst = feat.at[pl.ds(0 if offsets[0] < 0 else 6, 2)], rows_in.at[slot]
        copy = remote(src, dst, feat_ss.at[d], feat_rs.at[d], tile, step)
        copy.start()
        feat_copies.append(copy)

    l_noise.wait()
    for q in range(64):
        piece = noise[0, :, 128 * q : 128 * q + 128].astype(F32)
        noise_rows[pl.ds(64 + (q % 4) * 16 + q // 4, 8, stride=64), :] = piece
    noise_edge[0] = noise_rows[64:128, :].astype(BF16)
    noise_edge[1] = noise_rows[512:576, :].astype(BF16)
    noise_copies = []
    for side, offset in ((0, -1), (1, 1)):
        tile, step = near((offset, 0))
        copy = remote(noise_edge.at[side], noise_edge_in.at[side], noise_ss.at[side], noise_rs.at[side], tile, step)
        copy.start()
        noise_copies.append(copy)

    def spread(j):
        row = lax.broadcasted_iota(jnp.int32, (LAT, 128), 0)
        lane = lax.broadcasted_iota(jnp.int32, (LAT, 128), 1)
        return (lane == row + LAT * j).astype(F32).astype(BF16)

    def spread_t(j):
        row = lax.broadcasted_iota(jnp.int32, (128, LAT), 0)
        lane = lax.broadcasted_iota(jnp.int32, (128, LAT), 1)
        return (row == lane + LAT * j).astype(F32).astype(BF16)

    l_latw.wait()
    for j in range(4):
        latw4[HID * j : HID * j + HID, :] = dot(latw[...], spread(j)).astype(BF16)
        latw4_t[:, HID * j : HID * j + HID] = dot_nt(spread_t(j), latw[...]).astype(BF16)
    l_inw.wait()
    inw4[...] = jnp.zeros_like(inw4)
    for j in range(4):
        inw4[LAT * j : LAT * j + LAT, UNET * j : UNET * j + UNET] = inw[...]
    for j in range(4):
        part = inw4[:, UNET * j : UNET * j + UNET].astype(F32)
        inw4_t[UNET * j : UNET * j + UNET, :] = jnp.transpose(part).astype(BF16)
    l_outw.wait()
    for j in range(4):
        outw4[UNET * j : UNET * j + UNET, :] = dot(outw[...], spread(j)).astype(BF16)
        outw4_t[:, UNET * j : UNET * j + UNET] = dot_nt(spread_t(j), outw[...]).astype(BF16)

    chosen = time_ref[0]
    angle = ((jnp.full((8, 128), chosen, jnp.int32).astype(F32) + 1.0) / 1000.0 + 0.008) / 1.008 * (math.pi / 2.0)
    cosine = jnp.cos(angle)[0:1, :]
    sine = jnp.sin(angle)[0:1, :]
    l_table.wait()
    onehot = (lax.broadcasted_iota(jnp.int32, (16, table.shape[0]), 1) == chosen).astype(F32).astype(BF16)
    embed[...] = dot(onehot, table[...])[0:8]

    l_enc.wait()

    for d, copy in enumerate(feat_copies):
        copy.wait()
    for d, offsets in enumerate(AROUND):
        dt, ds = offsets
        valid = jnp.bool_(True)
        if dt:
            valid = (t < TILES - 1) if dt < 0 else (t > 0)
        if ds:
            beside = (s < STEPS - 1) if ds < 0 else (s > 0)
            valid = jnp.logical_and(valid, beside) if dt else beside
        if dt == 0:
            side = 0 if ds < 0 else 1
            taken = jnp.where(valid, edge_in[side].astype(F32), 0.0)
            first = 24 if ds < 0 else 6
            for i, part in enumerate(lane_tiles(taken)):
                for col in (0, 1):
                    grid[i, pl.ds(64 + first + col, 8, stride=32), :] = part[8 * col : 8 * col + 8]
        else:
            slot = d if d < 3 else d - 2
            for r in range(2):
                taken = jnp.where(valid, rows_in[slot, r].astype(F32), 0.0)
                row = (10 + r if dt < 0 else r) * 32
                for i, part in enumerate(lane_tiles(taken)):
                    if ds == 0:
                        grid[i, row + 8 : row + 24, :] = part
                    elif ds < 0:
                        grid[i, row + 24 : row + 32, :] = part[0:8]
                    else:
                        grid[i, row : row + 8, :] = part[8:16]

    def put_blocks(even, odd, index, value):
        even[index] = value.astype(BF16)
        odd[index] = value[8:].astype(BF16)

    for j in range(4):
        value = jnp.concatenate([grid[i, pl.ds(j, 96, stride=4), :] for i in range(2)], axis=1)
        put_blocks(blocks_even, blocks_odd, 1 + j, value)
        if j == 0:
            put_blocks(blocks_even, blocks_odd, 5, pltpu.roll(value, 95, 0))
        if j == 3:
            put_blocks(blocks_even, blocks_odd, 0, pltpu.roll(value, 1, 0))
    pieces = []
    for a in range(3):
        for b in range(3):
            if a == 1:
                window = blocks_odd[b : b + 4, 0:80, :]
            else:
                window = blocks_even[b : b + 4, 8 * a : 8 * a + 80, :]
            pieces.append(window.reshape(320, FEAT))
    pre = dot(jnp.concatenate(pieces, axis=1), enc[...].reshape(9 * FEAT, HID))
    pre_hidden[...] = pre
    hidden = (pre * sigmoid(pre)).astype(BF16)
    hidden = jnp.concatenate([hidden[80 * j : 80 * j + 80] for j in range(4)], axis=1)
    lat_tile[...] = dot(hidden, latw4[...])
    lat_pack[...] = jnp.zeros_like(lat_pack)
    for q in range(4):
        lat_pack[pl.ds(q, 10, stride=4), :] = lat_tile[pl.ds(2 + q, 10, stride=8), :]
    lat_send[...] = lat_pack[...].astype(BF16)

    def lat_copy(k):
        return remote(lat_send, lat_recv.at[k - 1], lat_ss.at[k - 1], lat_rs.at[k - 1], t, (s + k) % STEPS)

    def lat_start(k, _):
        lat_copy(k).start()
        return 0

    lax.fori_loop(1, STEPS, lat_start, 0)

    l_midw.wait()

    def flip_mid(k, _):
        mid_t[k] = jnp.transpose(midw[k])
        return 0

    lax.fori_loop(0, 9, flip_mid, 0)

    def flip_enc(k, _):
        enc_t[k] = jnp.transpose(enc[k])
        return 0

    lax.fori_loop(0, 9, flip_enc, 0)

    for side in (0, 1):
        noise_copies[side].wait()
    noise_rows[576:640, :] = noise_edge_in[0].astype(F32)
    noise_rows[0:64, :] = noise_edge_in[1].astype(F32)

    lat_flat[pl.ds(pl.multiple_of(s * 48, 16), 48), :] = lat_pack[...].astype(BF16).astype(F32)

    def lat_take(k, _):
        lat_copy(k).wait()
        source = (s - k + STEPS) % STEPS
        lat_flat[pl.ds(pl.multiple_of(source * 48, 16), 48), :] = lat_recv[k - 1].astype(F32)
        return 0

    lax.fori_loop(1, STEPS, lat_take, 0)

    def input_rows(r, _):
        latent = jnp.concatenate([lat_flat[pl.ds(r * 4 + q, 16, stride=48), :] for q in range(4)], axis=0)
        noisy = (cosine * latent + sine * noise_rows[pl.ds(pl.multiple_of(r * 64, 64), 64), :]).astype(BF16)
        shown = jnp.logical_and(jnp.logical_or(r > 0, t > 0), jnp.logical_or(r < 9, t < TILES - 1))
        gate = jnp.where(shown, 1.0, 0.0)
        for j in range(4):
            pre = dot(noisy, inw4[:, UNET * j : UNET * j + UNET]) + embed[0:1, :]
            sigma = sigmoid(pre)
            inner = pre * sigma * gate
            inner_slope[r, 64 * j : 64 * j + 64, :] = slope_of(pre, sigma)
            inner_ext[r, 64 + 64 * j : 128 + 64 * j, :] = inner.astype(BF16)
            if j == 0:
                inner_ext[r, 320:384, :] = shift_up(inner).astype(BF16)
            if j == 3:
                inner_ext[r, 0:64, :] = shift_down(inner).astype(BF16)
        for b in range(3):
            flipped = jnp.transpose(inner_ext[r, 64 * b : 64 * b + 256, :])
            inner_t[UNET * b : UNET * b + UNET, pl.ds(pl.multiple_of(r * 256, 256), 256)] = flipped
        return 0

    lax.fori_loop(0, 10, input_rows, 0)

    def by_class(value):
        rows = value.shape[0] // 256
        return jnp.concatenate(
            [
                jnp.concatenate([value[256 * r + 64 * j : 256 * r + 64 * j + 64] for j in range(4)], axis=1)
                for r in range(rows)
            ],
            axis=0,
        )

    def by_position(value):
        rows = value.shape[0] // 64
        return jnp.concatenate(
            [value[64 * r : 64 * r + 64, UNET * j : UNET * j + UNET] for r in range(rows) for j in range(4)], axis=0
        )

    def forward_rows(i, _):
        r = 2 * i
        windows = [
            inner_ext[pl.ds(r + a, 2), 64 * b : 64 * b + 256, :].reshape(512, UNET)
            for a in range(3)
            for b in range(3)
        ]
        pre = dot(jnp.concatenate(windows, axis=1), midw[...].reshape(9 * UNET, UNET))
        sigma = sigmoid(pre)
        mixed = (windows[4].astype(F32) + pre * sigma).astype(BF16)
        prediction = dot(by_class(mixed), outw4[...])
        own_noise = noise_rows[pl.ds(pl.multiple_of(64 + r * 64, 64), 128), :]
        error = ((prediction - own_noise) * (1.0 / math.sqrt(STEPS))).astype(BF16)
        pulled = by_position(dot(error, outw4_t[...]))
        back_mixed[pl.ds(pl.multiple_of(r * 256, 256), 512), :] = pulled
        back = pulled * slope_of(pre, sigma)
        for row in range(2):
            own = back[256 * row : 256 * row + 256]
            back_ext[r + 1 + row, 64:320, :] = own.astype(BF16)
            back_ext[r + 1 + row, 320:384, :] = shift_up(own[0:64]).astype(BF16)
            back_ext[r + 1 + row, 0:64, :] = shift_down(own[192:256]).astype(BF16)
        return 0

    lax.fori_loop(0, 4, forward_rows, 0)

    halo_copies = []
    for side, offset in ((0, -1), (1, 1)):
        tile, step = near((offset, 0))
        src, dst = (1, 9) if side == 0 else (8, 0)
        copy = remote(back_ext.at[src], back_ext.at[dst], halo_ss.at[side], halo_rs.at[side], tile, step)
        copy.start()
        halo_copies.append(copy)

    def s1_copy(a):
        return remote(s1_send.at[a], s1_recv.at[a], s1_ss.at[a], s1_rs.at[a], t, s + 1 - 2 * core)

    def s1_start(a):
        def pack(n, _):
            first = (n // 3) * UNET + n % 3 + 3 * (1 - core)
            block = jnp.concatenate([grad[a * 3 + i, pl.ds(first, 64, stride=6), :] for i in range(3)], axis=1)
            s1_send[a, pl.ds(pl.multiple_of(n * 64, 64), 64), :] = block.astype(BF16)
            return 0

        lax.fori_loop(0, 9, pack, 0)
        s1_copy(a).start()

    def axis_peer(a, k):
        if a == 0:
            there = (z + k) % 4
            return there, t, there * 4 + s % 4
        if a == 1:
            there = (x + k) % 4
            return there, y_hi * 4 + there, s
        there = (y + k) % 4
        return there, (there // 2) * 4 + x, z * 4 + (there % 2) * 2 + core

    def plane_rows(a, n, there):
        base = n * 64
        parts = []
        for i in range(3):
            if a == 0:
                half = [sum1[a * 3 + i, pl.ds(base + 2 * there + low, 8, stride=8), :] for low in (0, 1)]
                parts.append(jnp.concatenate(half, axis=0))
            elif a == 1:
                half = [
                    sum1[a * 3 + i, pl.ds(pl.multiple_of(base + high * 32 + there * 8, 8), 8), :] for high in (0, 1)
                ]
                parts.append(jnp.concatenate(half, axis=0))
            else:
                first = base + (there // 2) * 32 + there % 2
                parts.append(sum1[a * 3 + i, pl.ds(first, 16, stride=2), :])
        return jnp.concatenate(parts, axis=1)

    def s2_copy(a, k):
        _, tile, step = axis_peer(a, k)
        index = a * 3 + k - 1
        return remote(s2_send.at[index], s2_recv.at[index], s2_ss.at[index], s2_rs.at[index], tile, step)

    def s2_start(a):
        s1_copy(a).wait()

        def add(n, _):
            first = (n // 3) * UNET + n % 3 + 3 * core
            rows = pl.ds(pl.multiple_of(n * 64, 64), 64)
            got = s1_recv[a, rows, :].astype(F32)
            for i in range(3):
                own = grad[a * 3 + i, pl.ds(first, 64, stride=6), :]
                sum1[a * 3 + i, rows, :] = own + got[:, 128 * i : 128 * i + 128]
            return 0

        lax.fori_loop(0, 9, add, 0)
        for k in range(1, 4):
            there = axis_peer(a, k)[0]

            def pack(n, _, there=there, k=k):
                rows = pl.ds(pl.multiple_of(n * 16, 16), 16)
                s2_send[a * 3 + k - 1, rows, :] = plane_rows(a, n, there).astype(BF16)
                return 0

            lax.fori_loop(0, 9, pack, 0)
            s2_copy(a, k).start()

    def plane_peer(a, k):
        if a == 0:
            mine = y_lo * 8 + t
            there = (mine + k) % 16
            return mine, there, there % 8, z * 4 + (there // 8) * 2 + core
        if a == 1:
            mine = y_hi * 8 + s // 2
            there = (mine + k) % 16
            return mine, there, (there // 8) * 4 + x, (there % 8) * 2 + core
        mine = x * 4 + z
        there = (mine + k) % 16
        return mine, there, y_hi * 4 + there // 4, (there % 4) * 4 + s % 4

    def s3_copy(a, k):
        _, _, tile, step = plane_peer(a, k)
        index = a * 15 + k - 1
        return remote(s3_send.at[index], s3_recv.at[index], s3_ss.at[index], s3_rs.at[index], tile, step)

    def s3_start(a):
        for k in range(1, 4):
            s2_copy(a, k).wait()
        mine = axis_peer(a, 0)[0]

        def add(n, _):
            rows = pl.ds(pl.multiple_of(n * 16, 16), 16)
            total = plane_rows(a, n, mine)
            for k in range(3):
                total = total + s2_recv[a * 3 + k, rows, :].astype(F32)
            for i, part in enumerate(lane_tiles(total)):
                sum2[a * 3 + i, rows, :] = part
            return 0

        lax.fori_loop(0, 9, add, 0)

        def send(k, _):
            there = plane_peer(a, k)[1]
            block = jnp.concatenate([sum2[a * 3 + i, pl.ds(there, 16, stride=16), :] for i in range(3)], axis=1)
            s3_send[a * 15 + k - 1] = block.astype(BF16)
            s3_copy(a, k).start()
            return 0

        lax.fori_loop(1, 16, send, 0)

    def finish(a):
        mine = plane_peer(a, 0)[0]
        own = jnp.concatenate([sum2[a * 3 + i, pl.ds(mine, 16, stride=16), :] for i in range(3)], axis=1)

        def add(k, total):
            s3_copy(a, k).wait()
            return total + s3_recv[a * 15 + k - 1].astype(F32)

        total = lax.fori_loop(1, 16, add, own) * (1.0 / math.sqrt(64 * 256))
        for b in range(3):
            for i in range(3):
                mgrad_ref[i, 3 * a + b : 3 * a + b + 1, :] = total[3 * b + i : 3 * b + i + 1]

    sum2[...] = jnp.zeros_like(sum2)
    for a in range(3):
        result = dot(inner_t[:, 256 * a : 256 * a + 2048], back_ext[1:9, 64:320, :].reshape(2048, UNET))
        for i, part in enumerate(lane_tiles(result)):
            grad[a * 3 + i] = part
        s1_start(a)
        if a:
            s2_start(a - 1)

    for side in (0, 1):
        halo_copies[side].wait()

    @pl.when(t == 0)
    def _():
        back_ext[0] = jnp.zeros_like(back_ext[0])

    @pl.when(t == TILES - 1)
    def _():
        back_ext[9] = jnp.zeros_like(back_ext[9])

    def backward_rows(i, _):
        r = 2 * i
        windows = [
            back_ext[pl.ds(r + 2 - a, 2), 64 * (2 - b) : 64 * (2 - b) + 256, :].reshape(512, UNET)
            for a in range(3)
            for b in range(3)
        ]
        through = dot(jnp.concatenate(windows, axis=1), mid_t[...].reshape(9 * UNET, UNET))
        through = through + back_mixed[pl.ds(pl.multiple_of(r * 256, 256), 512), :]
        back = (through * inner_slope[pl.ds(r + 1, 2)].reshape(512, UNET)).astype(BF16)
        back_part[pl.ds(pl.multiple_of(r * 64, 64), 128), :] = cosine * dot(by_class(back), inw4_t[...])
        return 0

    lax.fori_loop(0, 2, backward_rows, 0)
    s2_start(2)
    lax.fori_loop(2, 4, backward_rows, 0)

    def part_copy(k):
        return remote(
            part_send.at[k - 1], part_recv.at[k - 1], part_ss.at[k - 1], part_rs.at[k - 1], t, (s + k) % STEPS
        )

    def part_start(k, _):
        part_send[k - 1] = back_part[pl.ds((s + k) % STEPS, 32, stride=16), :].astype(BF16)
        part_copy(k).start()
        return 0

    lax.fori_loop(1, STEPS, part_start, 0)

    for a in range(3):
        s3_start(a)

    def part_add(k, total):
        part_copy(k).wait()
        return total + part_recv[k - 1].astype(F32)

    latent_round = lax.fori_loop(1, STEPS, part_add, back_part[pl.ds(s, 32, stride=16), :])
    round_send[...] = latent_round.astype(BF16)
    round_copies = []
    for d, offsets in enumerate(AROUND):
        tile, step = near(offsets)
        copy = remote(round_send, round_recv.at[d], round_ss.at[d], round_rs.at[d], tile, step)
        copy.start()
        round_copies.append(copy)

    round_grid[...] = jnp.zeros_like(round_grid)
    round_pack[...] = round_send[...].astype(F32)
    for q in range(4):
        round_grid[pl.ds(10 + q, 8, stride=8), :] = round_pack[pl.ds(q, 8, stride=4), :]
    for d, (dt, ds) in enumerate(AROUND):
        round_copies[d].wait()
        valid = jnp.bool_(True)
        if dt:
            valid = (t < TILES - 1) if dt < 0 else (t > 0)
        if ds:
            beside = (s < STEPS - 1) if ds < 0 else (s > 0)
            valid = jnp.logical_and(valid, beside) if dt else beside
        round_pack[...] = jnp.where(valid, round_recv[d].astype(F32), 0.0)
        if dt == 0:
            q, place = (0, 6) if ds < 0 else (3, 1)
            round_grid[pl.ds(8 + place, 8, stride=8), :] = round_pack[pl.ds(q, 8, stride=4), :]
        else:
            source, row = (0, 72) if dt < 0 else (28, 0)
            if ds == 0:
                round_grid[row + 2 : row + 6, :] = round_pack[source : source + 4, :]
            else:
                q, place = (0, 6) if ds < 0 else (3, 1)
                round_grid[row + place : row + place + 1, :] = round_pack[source + q : source + q + 1, :]
    pulled = dot(round_grid[...].astype(BF16), latw4_t[...])
    for j in range(4):
        pre = pre_hidden[80 * j : 80 * j + 80, :]
        value = pulled[:, HID * j : HID * j + HID] * slope_of(pre, sigmoid(pre))
        put_blocks(hidden_even, hidden_odd, 1 + j, value)
        if j == 0:
            put_blocks(hidden_even, hidden_odd, 5, pltpu.roll(value, 79, 0))
        if j == 3:
            put_blocks(hidden_even, hidden_odd, 0, pltpu.roll(value, 1, 0))
    pieces = []
    for a in range(3):
        for b in range(3):
            if a == 1:
                window = hidden_odd[2 - b : 6 - b, 0:64, :]
            else:
                window = hidden_even[2 - b : 6 - b, 8 * (2 - a) : 8 * (2 - a) + 64, :]
            pieces.append(window.reshape(256, HID))
    result = dot(jnp.concatenate(pieces, axis=1), enc_t[...].reshape(9 * HID, FEAT))
    for j in range(4):
        for i, part in enumerate(lane_tiles(result[64 * j : 64 * j + 64])):
            out_grid[i, pl.ds(j, 64, stride=4), :] = part
    for r in range(8):
        for i in range(2):
            fgrad_ref[r, :, 128 * i : 128 * i + 128] = out_grid[i, r * 32 + 8 : r * 32 + 24, :]

    for a in range(3):
        finish(a)


def per_device(
    features,
    encoder_weight,
    latent_weight,
    timesteps,
    noise_field,
    time_table,
    input_weight,
    middle_weight,
    output_weight,
):
    hbm = pl.BlockSpec(memory_space=pl.ANY)
    vmem = pl.BlockSpec(memory_space=pltpu.VMEM)
    dma = pltpu.SemaphoreType.DMA
    operands = (
        features,
        encoder_weight,
        latent_weight,
        noise_field,
        time_table,
        input_weight,
        middle_weight,
        output_weight,
    )
    scratch = [
        pltpu.VMEM((8, 16, FEAT), BF16),
        pltpu.VMEM((9, FEAT, HID), BF16),
        pltpu.VMEM((HID, LAT), BF16),
        pltpu.VMEM(noise_field.shape, BF16),
        pltpu.VMEM(time_table.shape, BF16),
        pltpu.VMEM((LAT, UNET), BF16),
        pltpu.VMEM((9, UNET, UNET), BF16),
        pltpu.VMEM((UNET, LAT), BF16),
        dma((8,)),
        pltpu.VMEM((9, HID, FEAT), BF16),
        pltpu.VMEM((9, UNET, UNET), BF16),
        pltpu.VMEM((4 * HID, 128), BF16),
        pltpu.VMEM((128, 4 * HID), BF16),
        pltpu.VMEM((128, 4 * UNET), BF16),
        pltpu.VMEM((4 * UNET, 128), BF16),
        pltpu.VMEM((4 * UNET, 128), BF16),
        pltpu.VMEM((128, 4 * UNET), BF16),
        pltpu.VMEM((8, UNET), F32),
        pltpu.VMEM((2, 16, FEAT), BF16),
        pltpu.VMEM((2, 16, FEAT), BF16),
        pltpu.VMEM((6, 2, 16, FEAT), BF16),
        pltpu.VMEM((2, 12 * 32, 128), F32),
        pltpu.VMEM((6, 96, FEAT), BF16),
        pltpu.VMEM((6, 88, FEAT), BF16),
        pltpu.VMEM((320, HID), F32),
        pltpu.VMEM((80, 128), F32),
        pltpu.VMEM((48, 128), F32),
        pltpu.VMEM((48, 128), BF16),
        pltpu.VMEM((15, 48, 128), BF16),
        pltpu.VMEM((16 * 48, 128), F32),
        pltpu.VMEM((640, 128), F32),
        pltpu.VMEM((2, 64, 128), BF16),
        pltpu.VMEM((2, 64, 128), BF16),
        pltpu.VMEM((10, 384, UNET), BF16),
        pltpu.VMEM((10, 256, UNET), F32),
        pltpu.VMEM((3 * UNET, 2560), BF16),
        pltpu.VMEM((2048, UNET), F32),
        pltpu.VMEM((10, 384, UNET), BF16),
        pltpu.VMEM((512, 128), F32),
        pltpu.VMEM((15, 32, 128), BF16),
        pltpu.VMEM((15, 32, 128), BF16),
        pltpu.VMEM((32, 128), F32),
        pltpu.VMEM((32, 128), BF16),
        pltpu.VMEM((8, 32, 128), BF16),
        pltpu.VMEM((80, 128), F32),
        pltpu.VMEM((6, 80, HID), BF16),
        pltpu.VMEM((6, 72, HID), BF16),
        pltpu.VMEM((2, 256, 128), F32),
        pltpu.VMEM((9, 3 * UNET, 128), F32),
        pltpu.VMEM((3, 576, UNET), BF16),
        pltpu.VMEM((3, 576, UNET), BF16),
        pltpu.VMEM((9, 576, 128), F32),
        pltpu.VMEM((9, 144, UNET), BF16),
        pltpu.VMEM((9, 144, UNET), BF16),
        pltpu.VMEM((9, 256, 128), F32),
        pltpu.VMEM((45, 16, UNET), BF16),
        pltpu.VMEM((45, 16, UNET), BF16),
        dma((8,)),
        dma((8,)),
        dma((2,)),
        dma((2,)),
        dma((15,)),
        dma((15,)),
        dma((2,)),
        dma((2,)),
        dma((15,)),
        dma((15,)),
        dma((8,)),
        dma((8,)),
        dma((3,)),
        dma((3,)),
        dma((9,)),
        dma((9,)),
        dma((45,)),
        dma((45,)),
    ]
    return pl.pallas_call(
        kernel,
        out_shape=(
            jax.ShapeDtypeStruct((8, 16, FEAT), F32),
            jax.ShapeDtypeStruct((3, 9, UNET), F32),
        ),
        in_specs=[pl.BlockSpec(memory_space=pltpu.SMEM)] + [hbm] * 8,
        out_specs=(vmem, vmem),
        scratch_shapes=scratch,
        compiler_params=pltpu.CompilerParams(
            collective_id=0, has_side_effects=True, vmem_limit_bytes=60 * 1024 * 1024
        ),
        cost_estimate=pl.CostEstimate(flops=18_000_000_000, bytes_accessed=8_000_000, transcendentals=3_000_000),
    )(timesteps, *operands)


def solution(mesh):
    in_specs = (
        P("tile", "step", None),
        P(),
        P(),
        P("step"),
        P("step", "tile", None),
        P(),
        P(),
        P(),
        P(),
    )
    out_specs = (P("tile", "step", None), P(("tile", "step"), None, None))
    return jax.shard_map(per_device, mesh=mesh, in_specs=in_specs, out_specs=out_specs, check_vma=False)
```

time: 406 us -> 76.7 us (0.19); the launches traced: 398 us -> 75.7 us
  waiting for transfers between devices: 218 us -> 0 us
  matrix products: 80.7 us -> 0 us
  Pallas kernels: 0 us -> 68.4 us
  starting transfers between devices: 30.8 us -> 0 us
  blocking collectives: 22.2 us -> 0 us
  between operations: 17.4 us -> 1.29 us
  local copies, waits for them, and re-layouts: 19.5 us -> 6.09 us
  other arithmetic: 9.33 us -> 0 us
    unnamed x3 -> x0, waiting for transfers between devices: 149 us -> none
    dot_general x50 -> x0, matrix products: 80.7 us -> none  [the longest x8 23.9 us: grid_conv(): lax.dot_general(window, weights[tap_index], (((1,), (1,)), ((), ())), pre...]
    pallas_call x0 -> x1, Pallas kernels: none -> 68.4 us  [per_device(): pl.pallas_call(kernel, out_shape=(jax.ShapeDtypeStruct((8, 16, FEAT), F32...]
    reduce_scatter x1 -> x0, waiting for transfers between devices: 60.7 us -> none  [per_device(): lax.psum_scatter(spread.astype(jnp.bfloat16), 'step', scatter_dimension=1...]
    ppermute x12 -> x0, starting transfers between devices: 30.7 us -> none  [the longest x6 22.7 us: extended(): lax.ppermute(tail, axis, [(i, (i + 1) % count) for i in range(ends)])]
    all_gather x1 -> x0, blocking collectives: 22.2 us -> none  [per_device(): whole = lax.all_gather(flat_latent, 'step', axis=1, tiled=True)]
    ppermute x12 -> x0, waiting for transfers between devices: 8.46 us -> none  [the longest x6 7.4 us: extended(): lax.ppermute(head, axis, [((i + 1) % count, i) for i in range(ends)])]
    convert_element_type x6 -> x0, local copies, waits for them, and re-layouts: 6.18 us -> none  [the longest x2 3.79 us: denoise(): noise_float = noise_grid.astype(jnp.float32)]
  transfers between devices with their start and end apart: 14 -> 0, of which waited for: 6 -> 0; matrix products, arithmetic and copies ran while one was open for 6% -> 0% of each run, Pallas kernels for 0% -> 0%
where the time goes in v1:
time: 76.7 us; the launch traced here: 75.7 us
  Pallas kernels  68.4 us (89%)
  local copies, waits for them, and re-layouts  6.09 us (8%)
  between operations  1.29 us (2%)
    pallas_call x1, Pallas kernels, per_device(): pl.pallas_call(kernel, out_shape=(jax.ShapeDtypeStruct((8, 16, FEAT), F32...  68.4 us
    unnamed x3, local copies, waits for them, and re-layouts  4.56 us

profile of v1, /device:TPU:0, one launch (start us, length us, event | category | flops | bytes accessed | tf_op | source)
XLA Modules:
  0.0 75.7 jit_solution(11327563699989014661)
XLA Ops:
  1.3 1.5 %copy.12.outw_hbm = bf16[384,32]{1,0:T(8,128)(2,1)} copy(bf16[384,32]{0,1:T(8,128)(2,1)} %param.17) | data formatting | bytes 49152 | tf_op args[8]
  2.8 1.5 %copy.11.latw_hbm = bf16[512,32]{1,0:T(8,128)(2,1)} copy(bf16[512,32]{0,1:T(8,128)(2,1)} %param.11) | data formatting | bytes 65536 | tf_op args[2]
  4.3 68.4 %shard_map.104 = (f32[8,16,256]{2,1,0:T(8,128)}, f32[3,9,384]{2,1,0:T(8,128)}) custom-call(s32[1]{0:T(128)S(6)} %copy.15.time_ref, bf16[8,16,256]{2,1,0:T(8,128)(2,1)} %feat_hbm.1, bf16[9,256,512]{2,1,0:T(8,128)(2,1)} %enc_hbm.1, bf16[512,32]{1,0:T(8,128)(2,1)} %copy.11.latw_hbm, bf16[1,8,8192]{2,1,0:T(8,128)(2,1)} %noise_hbm.1, ...), custom_call_target="tpu_custom_call" | custom-call | flops 17999998976 | bytes 8000000 | tf_op jit(solution)/shard_map/pallas_call | solution.py:773
  72.6 1.5 %copy.13 = f32[3,9,384]{2,0,1:T(4,128)} copy(f32[3,9,384]{2,1,0:T(8,128)} %get-tuple-element.3) | data formatting | bytes 82944 | tf_op jit(solution)/shard_map/pallas_call | solution.py:773
  74.2 1.6 %copy.16 = f32[8,16,256]{2,1,0:T(8,128)} copy(f32[8,16,256]{2,1,0:T(8,128)} %get-tuple-element.6) | data formatting | bytes 262144

commit v2 on v1

--- a/solution.py
+++ b/solution.py
@@ -69,13 +69,8 @@
     midw,
     outw,
     in_sem,
-    enc_t,
-    mid_t,
-    latw4,
     latw4_t,
     inw4,
-    inw4_t,
-    outw4,
     outw4_t,
     embed,
     edge,
@@ -96,6 +91,8 @@
     inner_ext,
     inner_slope,
     inner_t,
+    inner_tm,
+    pre_middle,
     back_mixed,
     back_ext,
     back_part,
@@ -223,31 +220,12 @@
         copy.start()
         noise_copies.append(copy)
 
-    def spread(j):
-        row = lax.broadcasted_iota(jnp.int32, (LAT, 128), 0)
-        lane = lax.broadcasted_iota(jnp.int32, (LAT, 128), 1)
-        return (lane == row + LAT * j).astype(F32).astype(BF16)
-
-    def spread_t(j):
-        row = lax.broadcasted_iota(jnp.int32, (128, LAT), 0)
-        lane = lax.broadcasted_iota(jnp.int32, (128, LAT), 1)
-        return (row == lane + LAT * j).astype(F32).astype(BF16)
-
-    l_latw.wait()
-    for j in range(4):
-        latw4[HID * j : HID * j + HID, :] = dot(latw[...], spread(j)).astype(BF16)
-        latw4_t[:, HID * j : HID * j + HID] = dot_nt(spread_t(j), latw[...]).astype(BF16)
-    l_inw.wait()
-    inw4[...] = jnp.zeros_like(inw4)
-    for j in range(4):
-        inw4[LAT * j : LAT * j + LAT, UNET * j : UNET * j + UNET] = inw[...]
-    for j in range(4):
-        part = inw4[:, UNET * j : UNET * j + UNET].astype(F32)
-        inw4_t[UNET * j : UNET * j + UNET, :] = jnp.transpose(part).astype(BF16)
-    l_outw.wait()
-    for j in range(4):
-        outw4[UNET * j : UNET * j + UNET, :] = dot(outw[...], spread(j)).astype(BF16)
-        outw4_t[:, UNET * j : UNET * j + UNET] = dot_nt(spread_t(j), outw[...]).astype(BF16)
+    for load, weight, wide in ((l_latw, latw, latw4_t), (l_inw, inw, inw4), (l_outw, outw, outw4_t)):
+        load.wait()
+        columns = weight.shape[1]
+        wide[...] = jnp.zeros_like(wide)
+        for j in range(4):
+            wide[LAT * j : LAT * j + LAT, columns * j : columns * j + columns] = weight[...]
 
     chosen = time_ref[0]
     angle = ((jnp.full((8, 128), chosen, jnp.int32).astype(F32) + 1.0) / 1000.0 + 0.008) / 1.008 * (math.pi / 2.0)
@@ -312,7 +290,7 @@
     pre_hidden[...] = pre
     hidden = (pre * sigmoid(pre)).astype(BF16)
     hidden = jnp.concatenate([hidden[80 * j : 80 * j + 80] for j in range(4)], axis=1)
-    lat_tile[...] = dot(hidden, latw4[...])
+    lat_tile[...] = dot_nt(hidden, latw4_t[...])
     lat_pack[...] = jnp.zeros_like(lat_pack)
     for q in range(4):
         lat_pack[pl.ds(q, 10, stride=4), :] = lat_tile[pl.ds(2 + q, 10, stride=8), :]
@@ -328,19 +306,6 @@
     lax.fori_loop(1, STEPS, lat_start, 0)
 
     l_midw.wait()
-
-    def flip_mid(k, _):
-        mid_t[k] = jnp.transpose(midw[k])
-        return 0
-
-    lax.fori_loop(0, 9, flip_mid, 0)
-
-    def flip_enc(k, _):
-        enc_t[k] = jnp.transpose(enc[k])
-        return 0
-
-    lax.fori_loop(0, 9, flip_enc, 0)
-
     for side in (0, 1):
         noise_copies[side].wait()
     noise_rows[576:640, :] = noise_edge_in[0].astype(F32)
@@ -356,27 +321,36 @@
 
     lax.fori_loop(1, STEPS, lat_take, 0)
 
-    def input_rows(r, _):
-        latent = jnp.concatenate([lat_flat[pl.ds(r * 4 + q, 16, stride=48), :] for q in range(4)], axis=0)
-        noisy = (cosine * latent + sine * noise_rows[pl.ds(pl.multiple_of(r * 64, 64), 64), :]).astype(BF16)
-        shown = jnp.logical_and(jnp.logical_or(r > 0, t > 0), jnp.logical_or(r < 9, t < TILES - 1))
-        gate = jnp.where(shown, 1.0, 0.0)
+    def input_rows(pair):
+        first = 2 * pair
+        latent = [lat_flat[pl.ds((first + r) * 4 + q, 16, stride=48), :] for r in range(2) for q in range(4)]
+        noisy = cosine * jnp.concatenate(latent, axis=0) + sine * noise_rows[64 * first : 64 * first + 128, :]
+        noisy = noisy.astype(BF16)
         for j in range(4):
             pre = dot(noisy, inw4[:, UNET * j : UNET * j + UNET]) + embed[0:1, :]
             sigma = sigmoid(pre)
-            inner = pre * sigma * gate
-            inner_slope[r, 64 * j : 64 * j + 64, :] = slope_of(pre, sigma)
-            inner_ext[r, 64 + 64 * j : 128 + 64 * j, :] = inner.astype(BF16)
-            if j == 0:
-                inner_ext[r, 320:384, :] = shift_up(inner).astype(BF16)
-            if j == 3:
-                inner_ext[r, 0:64, :] = shift_down(inner).astype(BF16)
-        for b in range(3):
-            flipped = jnp.transpose(inner_ext[r, 64 * b : 64 * b + 256, :])
-            inner_t[UNET * b : UNET * b + UNET, pl.ds(pl.multiple_of(r * 256, 256), 256)] = flipped
-        return 0
-
-    lax.fori_loop(0, 10, input_rows, 0)
+            inner = pre * sigma
+            slope = slope_of(pre, sigma)
+            for r in range(2):
+                row = first + r
+                own = inner[64 * r : 64 * r + 64]
+                if row == 0:
+                    own = own * jnp.where(t > 0, 1.0, 0.0)
+                if row == 9:
+                    own = own * jnp.where(t < TILES - 1, 1.0, 0.0)
+                inner_ext[row, 64 + 64 * j : 128 + 64 * j, :] = own.astype(BF16)
+                if j == 0:
+                    inner_ext[row, 320:384, :] = shift_up(own).astype(BF16)
+                if j == 3:
+                    inner_ext[row, 0:64, :] = shift_down(own).astype(BF16)
+                if 0 < row < 9:
+                    inner_slope[row - 1, 64 * j : 64 * j + 64, :] = slope[64 * r : 64 * r + 64]
+
+    def flip_rows(pair):
+        for row in (2 * pair, 2 * pair + 1):
+            flipped = jnp.transpose(inner_ext[row])
+            inner_t[row] = flipped
+            inner_tm[row] = flipped[:, 64:320]
 
     def by_class(value):
         rows = value.shape[0] // 256
@@ -394,30 +368,43 @@
             [value[64 * r : 64 * r + 64, UNET * j : UNET * j + UNET] for r in range(rows) for j in range(4)], axis=0
         )
 
-    def forward_rows(i, _):
-        r = 2 * i
+    def forward_conv(i):
         windows = [
-            inner_ext[pl.ds(r + a, 2), 64 * b : 64 * b + 256, :].reshape(512, UNET)
+            inner_ext[2 * i + a : 2 * i + a + 2, 64 * b : 64 * b + 256, :].reshape(512, UNET)
             for a in range(3)
             for b in range(3)
         ]
-        pre = dot(jnp.concatenate(windows, axis=1), midw[...].reshape(9 * UNET, UNET))
+        pre_middle[i % 2] = dot(jnp.concatenate(windows, axis=1), midw[...].reshape(9 * UNET, UNET))
+
+    def forward_after(i):
+        r = 2 * i
+        pre = pre_middle[i % 2]
         sigma = sigmoid(pre)
-        mixed = (windows[4].astype(F32) + pre * sigma).astype(BF16)
-        prediction = dot(by_class(mixed), outw4[...])
-        own_noise = noise_rows[pl.ds(pl.multiple_of(64 + r * 64, 64), 128), :]
+        own = inner_ext[r + 1 : r + 3, 64:320, :].reshape(512, UNET)
+        mixed = (own.astype(F32) + pre * sigma).astype(BF16)
+        prediction = dot_nt(by_class(mixed), outw4_t[...])
+        own_noise = noise_rows[64 + r * 64 : 192 + r * 64, :]
         error = ((prediction - own_noise) * (1.0 / math.sqrt(STEPS))).astype(BF16)
         pulled = by_position(dot(error, outw4_t[...]))
-        back_mixed[pl.ds(pl.multiple_of(r * 256, 256), 512), :] = pulled
+        back_mixed[256 * r : 256 * r + 512, :] = pulled
         back = pulled * slope_of(pre, sigma)
         for row in range(2):
             own = back[256 * row : 256 * row + 256]
             back_ext[r + 1 + row, 64:320, :] = own.astype(BF16)
             back_ext[r + 1 + row, 320:384, :] = shift_up(own[0:64]).astype(BF16)
             back_ext[r + 1 + row, 0:64, :] = shift_down(own[192:256]).astype(BF16)
-        return 0
-
-    lax.fori_loop(0, 4, forward_rows, 0)
+
+    input_rows(0)
+    input_rows(1)
+    for i in range(4):
+        forward_conv(i)
+        if i < 3:
+            input_rows(i + 2)
+        flip_rows(i)
+        if i:
+            forward_after(i - 1)
+    flip_rows(4)
+    forward_after(3)
 
     halo_copies = []
     for side, offset in ((0, -1), (1, 1)):
@@ -431,13 +418,10 @@
         return remote(s1_send.at[a], s1_recv.at[a], s1_ss.at[a], s1_rs.at[a], t, s + 1 - 2 * core)
 
     def s1_start(a):
-        def pack(n, _):
+        for n in range(9):
             first = (n // 3) * UNET + n % 3 + 3 * (1 - core)
             block = jnp.concatenate([grad[a * 3 + i, pl.ds(first, 64, stride=6), :] for i in range(3)], axis=1)
-            s1_send[a, pl.ds(pl.multiple_of(n * 64, 64), 64), :] = block.astype(BF16)
-            return 0
-
-        lax.fori_loop(0, 9, pack, 0)
+            s1_send[a, 64 * n : 64 * n + 64, :] = block.astype(BF16)
         s1_copy(a).start()
 
     def axis_peer(a, k):
@@ -459,7 +443,7 @@
                 parts.append(jnp.concatenate(half, axis=0))
             elif a == 1:
                 half = [
-                    sum1[a * 3 + i, pl.ds(pl.multiple_of(base + high * 32 + there * 8, 8), 8), :] for high in (0, 1)
+                    sum1[a * 3 + i, pl.ds(base + high * 32 + pl.multiple_of(there * 8, 8), 8), :] for high in (0, 1)
                 ]
                 parts.append(jnp.concatenate(half, axis=0))
             else:
@@ -475,25 +459,16 @@
     def s2_start(a):
         s1_copy(a).wait()
 
-        def add(n, _):
+        for n in range(9):
             first = (n // 3) * UNET + n % 3 + 3 * core
-            rows = pl.ds(pl.multiple_of(n * 64, 64), 64)
-            got = s1_recv[a, rows, :].astype(F32)
+            got = s1_recv[a, 64 * n : 64 * n + 64, :].astype(F32)
             for i in range(3):
                 own = grad[a * 3 + i, pl.ds(first, 64, stride=6), :]
-                sum1[a * 3 + i, rows, :] = own + got[:, 128 * i : 128 * i + 128]
-            return 0
-
-        lax.fori_loop(0, 9, add, 0)
-        for k in range(1, 4):
+                sum1[a * 3 + i, 64 * n : 64 * n + 64, :] = own + got[:, 128 * i : 128 * i + 128]
+        for k in (2, 1, 3):
             there = axis_peer(a, k)[0]
-
-            def pack(n, _, there=there, k=k):
-                rows = pl.ds(pl.multiple_of(n * 16, 16), 16)
-                s2_send[a * 3 + k - 1, rows, :] = plane_rows(a, n, there).astype(BF16)
-                return 0
-
-            lax.fori_loop(0, 9, pack, 0)
+            for n in range(9):
+                s2_send[a * 3 + k - 1, 16 * n : 16 * n + 16, :] = plane_rows(a, n, there).astype(BF16)
             s2_copy(a, k).start()
 
     def plane_peer(a, k):
@@ -519,16 +494,12 @@
             s2_copy(a, k).wait()
         mine = axis_peer(a, 0)[0]
 
-        def add(n, _):
-            rows = pl.ds(pl.multiple_of(n * 16, 16), 16)
+        for n in range(9):
             total = plane_rows(a, n, mine)
             for k in range(3):
-                total = total + s2_recv[a * 3 + k, rows, :].astype(F32)
+                total = total + s2_recv[a * 3 + k, 16 * n : 16 * n + 16, :].astype(F32)
             for i, part in enumerate(lane_tiles(total)):
-                sum2[a * 3 + i, rows, :] = part
-            return 0
-
-        lax.fori_loop(0, 9, add, 0)
+                sum2[a * 3 + i, 16 * n : 16 * n + 16, :] = part
 
         def send(k, _):
             there = plane_peer(a, k)[1]
@@ -549,12 +520,16 @@
 
         total = lax.fori_loop(1, 16, add, own) * (1.0 / math.sqrt(64 * 256))
         for b in range(3):
-            for i in range(3):
-                mgrad_ref[i, 3 * a + b : 3 * a + b + 1, :] = total[3 * b + i : 3 * b + i + 1]
+            mgrad_ref[3 * a + b] = total[3 * b : 3 * b + 3]
 
     sum2[...] = jnp.zeros_like(sum2)
     for a in range(3):
-        result = dot(inner_t[:, 256 * a : 256 * a + 2048], back_ext[1:9, 64:320, :].reshape(2048, UNET))
+        taps = [
+            jnp.concatenate([inner_t[r + a, :, 0:256] for r in range(8)], axis=1),
+            jnp.concatenate([inner_tm[r + a] for r in range(8)], axis=1),
+            jnp.concatenate([inner_t[r + a, :, 128:384] for r in range(8)], axis=1),
+        ]
+        result = dot(jnp.concatenate(taps, axis=0), back_ext[1:9, 64:320, :].reshape(2048, UNET))
         for i, part in enumerate(lane_tiles(result)):
             grad[a * 3 + i] = part
         s1_start(a)
@@ -572,22 +547,24 @@
     def _():
         back_ext[9] = jnp.zeros_like(back_ext[9])
 
-    def backward_rows(i, _):
+    def backward_rows(i):
         r = 2 * i
         windows = [
-            back_ext[pl.ds(r + 2 - a, 2), 64 * (2 - b) : 64 * (2 - b) + 256, :].reshape(512, UNET)
+            back_ext[r + 2 - a : r + 4 - a, 64 * (2 - b) : 64 * (2 - b) + 256, :].reshape(512, UNET)
             for a in range(3)
             for b in range(3)
         ]
-        through = dot(jnp.concatenate(windows, axis=1), mid_t[...].reshape(9 * UNET, UNET))
-        through = through + back_mixed[pl.ds(pl.multiple_of(r * 256, 256), 512), :]
-        back = (through * inner_slope[pl.ds(r + 1, 2)].reshape(512, UNET)).astype(BF16)
-        back_part[pl.ds(pl.multiple_of(r * 64, 64), 128), :] = cosine * dot(by_class(back), inw4_t[...])
-        return 0
-
-    lax.fori_loop(0, 2, backward_rows, 0)
+        weights = jnp.concatenate([midw[k] for k in range(9)], axis=1)
+        through = dot_nt(jnp.concatenate(windows, axis=1), weights) + back_mixed[256 * r : 256 * r + 512, :]
+        back = (through * inner_slope[r : r + 2].reshape(512, UNET)).astype(BF16)
+        back_part[64 * r : 64 * r + 128, :] = cosine * dot_nt(by_class(back), inw4[...])
+
+    backward_rows(0)
     s2_start(2)
-    lax.fori_loop(2, 4, backward_rows, 0)
+    backward_rows(1)
+    backward_rows(2)
+    s3_start(0)
+    backward_rows(3)
 
     def part_copy(k):
         return remote(
@@ -601,8 +578,7 @@
 
     lax.fori_loop(1, STEPS, part_start, 0)
 
-    for a in range(3):
-        s3_start(a)
+    s3_start(1)
 
     def part_add(k, total):
         part_copy(k).wait()
@@ -616,6 +592,8 @@
         copy = remote(round_send, round_recv.at[d], round_ss.at[d], round_rs.at[d], tile, step)
         copy.start()
         round_copies.append(copy)
+
+    s3_start(2)
 
     round_grid[...] = jnp.zeros_like(round_grid)
     round_pack[...] = round_send[...].astype(F32)
@@ -657,7 +635,7 @@
             else:
                 window = hidden_even[2 - b : 6 - b, 8 * (2 - a) : 8 * (2 - a) + 64, :]
             pieces.append(window.reshape(256, HID))
-    result = dot(jnp.concatenate(pieces, axis=1), enc_t[...].reshape(9 * HID, FEAT))
+    result = dot_nt(jnp.concatenate(pieces, axis=1), jnp.concatenate([enc[k] for k in range(9)], axis=1))
     for j in range(4):
         for i, part in enumerate(lane_tiles(result[64 * j : 64 * j + 64])):
             out_grid[i, pl.ds(j, 64, stride=4), :] = part
@@ -667,6 +645,15 @@
 
     for a in range(3):
         finish(a)
+
+
+def hand_over(fgrad_ref, mgrad_ref, fgrad_out, mgrad_out, sem):
+    first = pltpu.make_async_copy(fgrad_ref, fgrad_out, sem.at[0])
+    second = pltpu.make_async_copy(mgrad_ref, mgrad_out, sem.at[1])
+    first.start()
+    second.start()
+    first.wait()
+    second.wait()
 
 
 def per_device(
@@ -686,30 +673,25 @@
     operands = (
         features,
         encoder_weight,
-        latent_weight,
+        latent_weight.T,
         noise_field,
         time_table,
         input_weight,
         middle_weight,
-        output_weight,
+        output_weight.T,
     )
     scratch = [
         pltpu.VMEM((8, 16, FEAT), BF16),
         pltpu.VMEM((9, FEAT, HID), BF16),
-        pltpu.VMEM((HID, LAT), BF16),
+        pltpu.VMEM((LAT, HID), BF16),
         pltpu.VMEM(noise_field.shape, BF16),
         pltpu.VMEM(time_table.shape, BF16),
         pltpu.VMEM((LAT, UNET), BF16),
         pltpu.VMEM((9, UNET, UNET), BF16),
-        pltpu.VMEM((UNET, LAT), BF16),
+        pltpu.VMEM((LAT, UNET), BF16),
         dma((8,)),
-        pltpu.VMEM((9, HID, FEAT), BF16),
-        pltpu.VMEM((9, UNET, UNET), BF16),
-        pltpu.VMEM((4 * HID, 128), BF16),
         pltpu.VMEM((128, 4 * HID), BF16),
         pltpu.VMEM((128, 4 * UNET), BF16),
-        pltpu.VMEM((4 * UNET, 128), BF16),
-        pltpu.VMEM((4 * UNET, 128), BF16),
         pltpu.VMEM((128, 4 * UNET), BF16),
         pltpu.VMEM((8, UNET), F32),
         pltpu.VMEM((2, 16, FEAT), BF16),
@@ -728,8 +710,10 @@
         pltpu.VMEM((2, 64, 128), BF16),
         pltpu.VMEM((2, 64, 128), BF16),
         pltpu.VMEM((10, 384, UNET), BF16),
-        pltpu.VMEM((10, 256, UNET), F32),
-        pltpu.VMEM((3 * UNET, 2560), BF16),
+        pltpu.VMEM((8, 256, UNET), F32),
+        pltpu.VMEM((10, UNET, 384), BF16),
+        pltpu.VMEM((10, UNET, 256), BF16),
+        pltpu.VMEM((2, 512, UNET), F32),
         pltpu.VMEM((2048, UNET), F32),
         pltpu.VMEM((10, 384, UNET), BF16),
         pltpu.VMEM((512, 128), F32),
@@ -770,12 +754,13 @@
         dma((45,)),
         dma((45,)),
     ]
-    return pl.pallas_call(
+    shapes = (
+        jax.ShapeDtypeStruct((8, 16, FEAT), F32),
+        jax.ShapeDtypeStruct((9, 3, UNET), F32),
+    )
+    results = pl.pallas_call(
         kernel,
-        out_shape=(
-            jax.ShapeDtypeStruct((8, 16, FEAT), F32),
-            jax.ShapeDtypeStruct((3, 9, UNET), F32),
-        ),
+        out_shape=shapes,
         in_specs=[pl.BlockSpec(memory_space=pltpu.SMEM)] + [hbm] * 8,
         out_specs=(vmem, vmem),
         scratch_shapes=scratch,
@@ -784,6 +769,14 @@
         ),
         cost_estimate=pl.CostEstimate(flops=18_000_000_000, bytes_accessed=8_000_000, transcendentals=3_000_000),
     )(timesteps, *operands)
+    feature_grad, middle_grad = pl.pallas_call(
+        hand_over,
+        out_shape=shapes,
+        in_specs=[hbm, hbm],
+        out_specs=(hbm, hbm),
+        scratch_shapes=[dma((2,))],
+    )(*results)
+    return feature_grad, jnp.transpose(middle_grad, (1, 0, 2))
 
 
 def solution(mesh):

time: 76.7 us -> 73.7 us (0.961)
  the two profiles are of different devices: /device:TPU:0 before, /device:TPU:1 now
where the time goes in v2:
time: 73.7 us; the launch traced here: 73.6 us
  Pallas kernels  72.2 us (98%)
  between operations  1.45 us (2%)
    pallas_call x1, Pallas kernels, per_device(): pl.pallas_call(kernel, out_shape=shapes, in_specs=[pl.BlockSpec(memory_sp...  65.4 us
    pallas_call x1, Pallas kernels, per_device(): pl.pallas_call(hand_over, out_shape=shapes, in_specs=[hbm, hbm], out_spec...  6.77 us

profile of v2, /device:TPU:1, one launch (start us, length us, event | category | flops | bytes accessed | tf_op | source)
XLA Modules:
  0.0 73.6 jit_solution(5237808499528026526)
XLA Ops:
  1.3 65.4 %shard_map.104 = (f32[8,16,256]{2,1,0:T(8,128)}, f32[9,3,384]{2,1,0:T(4,128)}) custom-call(s32[1]{0:T(128)S(6)} %copy.11.time_ref, bf16[8,16,256]{2,1,0:T(8,128)(2,1)} %feat_hbm.1, bf16[9,256,512]{2,1,0:T(8,128)(2,1)} %enc_hbm.1, bf16[32,512]{1,0:T(8,128)(2,1)} %bitcast.4, bf16[1,8,8192]{2,1,0:T(8,128)(2,1)} %noise_hbm.1, bf16[1000,384]{1,0:T(8,128)(2,1)} %table_hbm.1, ...), custom_call_target="tpu_custom_call" | custom-call | flops 17999998976 | bytes 8000000 | tf_op jit(solution)/shard_map/pallas_call | solution.py:761
  66.7 6.8 %shard_map.105 = (f32[8,16,256]{2,1,0:T(8,128)}, f32[9,3,384]{2,1,0:T(4,128)}) custom-call(f32[8,16,256]{2,1,0:T(8,128)} %get-tuple-element.6.fgrad_ref, f32[9,3,384]{2,1,0:T(4,128)} %get-tuple-element.7.mgrad_ref), custom_call_target="tpu_custom_call" | custom-call | tf_op jit(solution)/shard_map/pallas_call | solution.py:772

commit v3 on v2

--- a/solution.py
+++ b/solution.py
@@ -26,10 +26,6 @@
 
 def dot(left, right):
     return jnp.dot(left, right, preferred_element_type=F32)
-
-
-def dot_nt(left, right):
-    return lax.dot_general(left, right, (((1,), (1,)), ((), ())), preferred_element_type=F32)
 
 
 def lane_tiles(value):
@@ -69,8 +65,13 @@
     midw,
     outw,
     in_sem,
+    enc_t,
+    mid_t,
+    latw4,
     latw4_t,
     inw4,
+    inw4_t,
+    outw4,
     outw4_t,
     embed,
     edge,
@@ -220,12 +221,17 @@
         copy.start()
         noise_copies.append(copy)
 
-    for load, weight, wide in ((l_latw, latw, latw4_t), (l_inw, inw, inw4), (l_outw, outw, outw4_t)):
+    for load, weight, wide, flipped in (
+        (l_latw, latw, latw4_t, latw4),
+        (l_inw, inw, inw4, inw4_t),
+        (l_outw, outw, outw4_t, outw4),
+    ):
         load.wait()
         columns = weight.shape[1]
         wide[...] = jnp.zeros_like(wide)
         for j in range(4):
             wide[LAT * j : LAT * j + LAT, columns * j : columns * j + columns] = weight[...]
+        flipped[...] = jnp.transpose(wide[...])
 
     chosen = time_ref[0]
     angle = ((jnp.full((8, 128), chosen, jnp.int32).astype(F32) + 1.0) / 1000.0 + 0.008) / 1.008 * (math.pi / 2.0)
@@ -290,7 +296,7 @@
     pre_hidden[...] = pre
     hidden = (pre * sigmoid(pre)).astype(BF16)
     hidden = jnp.concatenate([hidden[80 * j : 80 * j + 80] for j in range(4)], axis=1)
-    lat_tile[...] = dot_nt(hidden, latw4_t[...])
+    lat_tile[...] = dot(hidden, latw4[...])
     lat_pack[...] = jnp.zeros_like(lat_pack)
     for q in range(4):
         lat_pack[pl.ds(q, 10, stride=4), :] = lat_tile[pl.ds(2 + q, 10, stride=8), :]
@@ -306,6 +312,12 @@
     lax.fori_loop(1, STEPS, lat_start, 0)
 
     l_midw.wait()
+
+    def flip_mid(k, _):
+        mid_t[k] = jnp.transpose(midw[k])
+        return 0
+
+    lax.fori_loop(0, 9, flip_mid, 0)
     for side in (0, 1):
         noise_copies[side].wait()
     noise_rows[576:640, :] = noise_edge_in[0].astype(F32)
@@ -382,7 +394,7 @@
         sigma = sigmoid(pre)
         own = inner_ext[r + 1 : r + 3, 64:320, :].reshape(512, UNET)
         mixed = (own.astype(F32) + pre * sigma).astype(BF16)
-        prediction = dot_nt(by_class(mixed), outw4_t[...])
+        prediction = dot(by_class(mixed), outw4[...])
         own_noise = noise_rows[64 + r * 64 : 192 + r * 64, :]
         error = ((prediction - own_noise) * (1.0 / math.sqrt(STEPS))).astype(BF16)
         pulled = by_position(dot(error, outw4_t[...]))
@@ -410,7 +422,8 @@
     for side, offset in ((0, -1), (1, 1)):
         tile, step = near((offset, 0))
         src, dst = (1, 9) if side == 0 else (8, 0)
-        copy = remote(back_ext.at[src], back_ext.at[dst], halo_ss.at[side], halo_rs.at[side], tile, step)
+        src, dst = back_ext.at[src, pl.ds(64, 256)], back_ext.at[dst, pl.ds(64, 256)]
+        copy = remote(src, dst, halo_ss.at[side], halo_rs.at[side], tile, step)
         copy.start()
         halo_copies.append(copy)
 
@@ -532,12 +545,16 @@
         result = dot(jnp.concatenate(taps, axis=0), back_ext[1:9, 64:320, :].reshape(2048, UNET))
         for i, part in enumerate(lane_tiles(result)):
             grad[a * 3 + i] = part
+        for k in range(3 * a, 3 * a + 3):
+            enc_t[k] = jnp.transpose(enc[k])
         s1_start(a)
         if a:
             s2_start(a - 1)
 
-    for side in (0, 1):
-        halo_copies[side].wait()
+    for row, copy in ((9, halo_copies[0]), (0, halo_copies[1])):
+        copy.wait()
+        back_ext[row, 320:384, :] = shift_up(back_ext[row, 64:128, :].astype(F32)).astype(BF16)
+        back_ext[row, 0:64, :] = shift_down(back_ext[row, 256:320, :].astype(F32)).astype(BF16)
 
     @pl.when(t == 0)
     def _():
@@ -554,10 +571,10 @@
             for a in range(3)
             for b in range(3)
         ]
-        weights = jnp.concatenate([midw[k] for k in range(9)], axis=1)
-        through = dot_nt(jnp.concatenate(windows, axis=1), weights) + back_mixed[256 * r : 256 * r + 512, :]
+        through = dot(jnp.concatenate(windows, axis=1), mid_t[...].reshape(9 * UNET, UNET))
+        through = through + back_mixed[256 * r : 256 * r + 512, :]
         back = (through * inner_slope[r : r + 2].reshape(512, UNET)).astype(BF16)
-        back_part[64 * r : 64 * r + 128, :] = cosine * dot_nt(by_class(back), inw4[...])
+        back_part[64 * r : 64 * r + 128, :] = cosine * dot(by_class(back), inw4_t[...])
 
     backward_rows(0)
     s2_start(2)
@@ -635,7 +652,7 @@
             else:
                 window = hidden_even[2 - b : 6 - b, 8 * (2 - a) : 8 * (2 - a) + 64, :]
             pieces.append(window.reshape(256, HID))
-    result = dot_nt(jnp.concatenate(pieces, axis=1), jnp.concatenate([enc[k] for k in range(9)], axis=1))
+    result = dot(jnp.concatenate(pieces, axis=1), enc_t[...].reshape(9 * HID, FEAT))
     for j in range(4):
         for i, part in enumerate(lane_tiles(result[64 * j : 64 * j + 64])):
             out_grid[i, pl.ds(j, 64, stride=4), :] = part
@@ -647,13 +664,9 @@
         finish(a)
 
 
-def hand_over(fgrad_ref, mgrad_ref, fgrad_out, mgrad_out, sem):
-    first = pltpu.make_async_copy(fgrad_ref, fgrad_out, sem.at[0])
-    second = pltpu.make_async_copy(mgrad_ref, mgrad_out, sem.at[1])
-    first.start()
-    second.start()
-    first.wait()
-    second.wait()
+def hand_over(fgrad_ref, mgrad_ref, fgrad_out, mgrad_out):
+    fgrad_out[...] = fgrad_ref[...]
+    mgrad_out[...] = mgrad_ref[...]
 
 
 def per_device(
@@ -690,8 +703,13 @@
         pltpu.VMEM((9, UNET, UNET), BF16),
         pltpu.VMEM((LAT, UNET), BF16),
         dma((8,)),
+        pltpu.VMEM((9, HID, FEAT), BF16),
+        pltpu.VMEM((9, UNET, UNET), BF16),
+        pltpu.VMEM((4 * HID, 128), BF16),
         pltpu.VMEM((128, 4 * HID), BF16),
         pltpu.VMEM((128, 4 * UNET), BF16),
+        pltpu.VMEM((4 * UNET, 128), BF16),
+        pltpu.VMEM((4 * UNET, 128), BF16),
         pltpu.VMEM((128, 4 * UNET), BF16),
         pltpu.VMEM((8, UNET), F32),
         pltpu.VMEM((2, 16, FEAT), BF16),
@@ -772,9 +790,8 @@
     feature_grad, middle_grad = pl.pallas_call(
         hand_over,
         out_shape=shapes,
-        in_specs=[hbm, hbm],
-        out_specs=(hbm, hbm),
-        scratch_shapes=[dma((2,))],
+        in_specs=[vmem, vmem],
+        out_specs=(vmem, vmem),
     )(*results)
     return feature_grad, jnp.transpose(middle_grad, (1, 0, 2))
 

time: 73.7 us -> 68.5 us (0.929)
  the two profiles are of different devices: /device:TPU:1 before, /device:TPU:0 now
where the time goes in v3:
time: 68.5 us; the launch traced here: 67.4 us
  Pallas kernels  66.1 us (96%)
  between operations  1.29 us (2%)
    pallas_call x1, Pallas kernels, per_device(): pl.pallas_call(kernel, out_shape=shapes, in_specs=[pl.BlockSpec(memory_sp...  64.5 us
    pallas_call x1, Pallas kernels, per_device(): pl.pallas_call(hand_over, out_shape=shapes, in_specs=[vmem, vmem], out_sp...  1.59 us

profile of v3, /device:TPU:0, one launch (start us, length us, event | category | flops | bytes accessed | tf_op | source)
XLA Modules:
  0.0 67.4 jit_solution(16963072340238745226)
XLA Ops:
  1.3 64.5 %shard_map.104 = (f32[8,16,256]{2,1,0:T(8,128)}, f32[9,3,384]{2,1,0:T(4,128)}) custom-call(s32[1]{0:T(128)S(6)} %copy.11.time_ref, bf16[8,16,256]{2,1,0:T(8,128)(2,1)} %feat_hbm.1, bf16[9,256,512]{2,1,0:T(8,128)(2,1)} %enc_hbm.1, bf16[32,512]{1,0:T(8,128)(2,1)} %bitcast.4, bf16[1,8,8192]{2,1,0:T(8,128)(2,1)} %noise_hbm.1, bf16[1000,384]{1,0:T(8,128)(2,1)} %table_hbm.1, ...), custom_call_target="tpu_custom_call" | custom-call | flops 17999998976 | bytes 8000000 | tf_op jit(solution)/shard_map/pallas_call | solution.py:779
  65.8 1.6 %shard_map.105 = (f32[8,16,256]{2,1,0:T(8,128)}, f32[9,3,384]{2,1,0:T(4,128)}) custom-call(f32[8,16,256]{2,1,0:T(8,128)} %get-tuple-element.6.fgrad_ref, f32[9,3,384]{2,1,0:T(4,128)} %get-tuple-element.7.mgrad_ref), custom_call_target="tpu_custom_call" | custom-call | tf_op jit(solution)/shard_map/pallas_call | solution.py:790

commit v4 on v3

--- a/solution.py
+++ b/solution.py
@@ -333,33 +333,35 @@
 
     lax.fori_loop(1, STEPS, lat_take, 0)
 
-    def input_rows(pair):
+    def input_rows(pair, _):
         first = 2 * pair
         latent = [lat_flat[pl.ds((first + r) * 4 + q, 16, stride=48), :] for r in range(2) for q in range(4)]
-        noisy = cosine * jnp.concatenate(latent, axis=0) + sine * noise_rows[64 * first : 64 * first + 128, :]
-        noisy = noisy.astype(BF16)
+        noisy = sine * noise_rows[pl.ds(pl.multiple_of(64 * first, 128), 128), :]
+        noisy = (cosine * jnp.concatenate(latent, axis=0) + noisy).astype(BF16)
+        gates = [
+            jnp.where(jnp.logical_or(pair > 0, t > 0), 1.0, 0.0),
+            jnp.where(jnp.logical_or(pair < 4, t < TILES - 1), 1.0, 0.0),
+        ]
         for j in range(4):
             pre = dot(noisy, inw4[:, UNET * j : UNET * j + UNET]) + embed[0:1, :]
             sigma = sigmoid(pre)
             inner = pre * sigma
             slope = slope_of(pre, sigma)
             for r in range(2):
-                row = first + r
-                own = inner[64 * r : 64 * r + 64]
-                if row == 0:
-                    own = own * jnp.where(t > 0, 1.0, 0.0)
-                if row == 9:
-                    own = own * jnp.where(t < TILES - 1, 1.0, 0.0)
-                inner_ext[row, 64 + 64 * j : 128 + 64 * j, :] = own.astype(BF16)
+                own = inner[64 * r : 64 * r + 64] * gates[r]
+                inner_ext[first + r, 64 + 64 * j : 128 + 64 * j, :] = own.astype(BF16)
                 if j == 0:
-                    inner_ext[row, 320:384, :] = shift_up(own).astype(BF16)
+                    inner_ext[first + r, 320:384, :] = shift_up(own).astype(BF16)
                 if j == 3:
-                    inner_ext[row, 0:64, :] = shift_down(own).astype(BF16)
-                if 0 < row < 9:
-                    inner_slope[row - 1, 64 * j : 64 * j + 64, :] = slope[64 * r : 64 * r + 64]
+                    inner_ext[first + r, 0:64, :] = shift_down(own).astype(BF16)
+                inner_slope[first + r, 64 * j : 64 * j + 64, :] = slope[64 * r : 64 * r + 64]
+        return 0
+
+    lax.fori_loop(0, 5, input_rows, 0)
 
     def flip_rows(pair):
-        for row in (2 * pair, 2 * pair + 1):
+        for r in range(2):
+            row = 2 * pair + r
             flipped = jnp.transpose(inner_ext[row])
             inner_t[row] = flipped
             inner_tm[row] = flipped[:, 64:320]
@@ -382,23 +384,23 @@
 
     def forward_conv(i):
         windows = [
-            inner_ext[2 * i + a : 2 * i + a + 2, 64 * b : 64 * b + 256, :].reshape(512, UNET)
+            inner_ext[pl.ds(2 * i + a, 2), 64 * b : 64 * b + 256, :].reshape(512, UNET)
             for a in range(3)
             for b in range(3)
         ]
-        pre_middle[i % 2] = dot(jnp.concatenate(windows, axis=1), midw[...].reshape(9 * UNET, UNET))
+        pre_middle[...] = dot(jnp.concatenate(windows, axis=1), midw[...].reshape(9 * UNET, UNET))
 
     def forward_after(i):
         r = 2 * i
-        pre = pre_middle[i % 2]
+        pre = pre_middle[...]
         sigma = sigmoid(pre)
-        own = inner_ext[r + 1 : r + 3, 64:320, :].reshape(512, UNET)
+        own = inner_ext[pl.ds(r + 1, 2), 64:320, :].reshape(512, UNET)
         mixed = (own.astype(F32) + pre * sigma).astype(BF16)
         prediction = dot(by_class(mixed), outw4[...])
-        own_noise = noise_rows[64 + r * 64 : 192 + r * 64, :]
+        own_noise = noise_rows[pl.ds(pl.multiple_of(64 + r * 64, 64), 128), :]
         error = ((prediction - own_noise) * (1.0 / math.sqrt(STEPS))).astype(BF16)
         pulled = by_position(dot(error, outw4_t[...]))
-        back_mixed[256 * r : 256 * r + 512, :] = pulled
+        back_mixed[pl.ds(pl.multiple_of(256 * r, 512), 512), :] = pulled
         back = pulled * slope_of(pre, sigma)
         for row in range(2):
             own = back[256 * row : 256 * row + 256]
@@ -406,15 +408,14 @@
             back_ext[r + 1 + row, 320:384, :] = shift_up(own[0:64]).astype(BF16)
             back_ext[r + 1 + row, 0:64, :] = shift_down(own[192:256]).astype(BF16)
 
-    input_rows(0)
-    input_rows(1)
-    for i in range(4):
+    def forward_rows(i, _):
+        forward_after((i + 3) % 4)
         forward_conv(i)
-        if i < 3:
-            input_rows(i + 2)
         flip_rows(i)
-        if i:
-            forward_after(i - 1)
+        return 0
+
+    pre_middle[...] = jnp.zeros_like(pre_middle)
+    lax.fori_loop(0, 4, forward_rows, 0)
     flip_rows(4)
     forward_after(3)
 
@@ -456,7 +457,7 @@
                 parts.append(jnp.concatenate(half, axis=0))
             elif a == 1:
                 half = [
-                    sum1[a * 3 + i, pl.ds(base + high * 32 + pl.multiple_of(there * 8, 8), 8), :] for high in (0, 1)
+                    sum1[a * 3 + i, pl.ds(pl.multiple_of(base + high * 32 + there * 8, 8), 8), :] for high in (0, 1)
                 ]
                 parts.append(jnp.concatenate(half, axis=0))
             else:
@@ -472,16 +473,25 @@
     def s2_start(a):
         s1_copy(a).wait()
 
-        for n in range(9):
+        def add(n, _):
             first = (n // 3) * UNET + n % 3 + 3 * core
-            got = s1_recv[a, 64 * n : 64 * n + 64, :].astype(F32)
+            rows = pl.ds(pl.multiple_of(64 * n, 64), 64)
+            got = s1_recv[a, rows, :].astype(F32)
             for i in range(3):
                 own = grad[a * 3 + i, pl.ds(first, 64, stride=6), :]
-                sum1[a * 3 + i, 64 * n : 64 * n + 64, :] = own + got[:, 128 * i : 128 * i + 128]
+                sum1[a * 3 + i, rows, :] = own + got[:, 128 * i : 128 * i + 128]
+            return 0
+
+        lax.fori_loop(0, 9, add, 0)
+
+        def pack(n, _):
+            for k in (1, 2, 3):
+                rows = pl.ds(pl.multiple_of(16 * n, 16), 16)
+                s2_send[a * 3 + k - 1, rows, :] = plane_rows(a, n, axis_peer(a, k)[0]).astype(BF16)
+            return 0
+
+        lax.fori_loop(0, 9, pack, 0)
         for k in (2, 1, 3):
-            there = axis_peer(a, k)[0]
-            for n in range(9):
-                s2_send[a * 3 + k - 1, 16 * n : 16 * n + 16, :] = plane_rows(a, n, there).astype(BF16)
             s2_copy(a, k).start()
 
     def plane_peer(a, k):
@@ -507,12 +517,16 @@
             s2_copy(a, k).wait()
         mine = axis_peer(a, 0)[0]
 
-        for n in range(9):
+        def add(n, _):
+            rows = pl.ds(pl.multiple_of(16 * n, 16), 16)
             total = plane_rows(a, n, mine)
             for k in range(3):
-                total = total + s2_recv[a * 3 + k, 16 * n : 16 * n + 16, :].astype(F32)
+                total = total + s2_recv[a * 3 + k, rows, :].astype(F32)
             for i, part in enumerate(lane_tiles(total)):
-                sum2[a * 3 + i, 16 * n : 16 * n + 16, :] = part
+                sum2[a * 3 + i, rows, :] = part
+            return 0
+
+        lax.fori_loop(0, 9, add, 0)
 
         def send(k, _):
             there = plane_peer(a, k)[1]
@@ -536,7 +550,7 @@
             mgrad_ref[3 * a + b] = total[3 * b : 3 * b + 3]
 
     sum2[...] = jnp.zeros_like(sum2)
-    for a in range(3):
+    def weight_rows(a, _):
         taps = [
             jnp.concatenate([inner_t[r + a, :, 0:256] for r in range(8)], axis=1),
             jnp.concatenate([inner_tm[r + a] for r in range(8)], axis=1),
@@ -545,11 +559,21 @@
         result = dot(jnp.concatenate(taps, axis=0), back_ext[1:9, 64:320, :].reshape(2048, UNET))
         for i, part in enumerate(lane_tiles(result)):
             grad[a * 3 + i] = part
-        for k in range(3 * a, 3 * a + 3):
-            enc_t[k] = jnp.transpose(enc[k])
+        for k in range(3):
+            enc_t[3 * a + k] = jnp.transpose(enc[3 * a + k])
         s1_start(a)
-        if a:
-            s2_start(a - 1)
+
+        @pl.when(a == 1)
+        def _():
+            s2_start(0)
+
+        @pl.when(a == 2)
+        def _():
+            s2_start(1)
+
+        return 0
+
+    lax.fori_loop(0, 3, weight_rows, 0)
 
     for row, copy in ((9, halo_copies[0]), (0, halo_copies[1])):
         copy.wait()
@@ -564,24 +588,33 @@
     def _():
         back_ext[9] = jnp.zeros_like(back_ext[9])
 
-    def backward_rows(i):
+    def backward_after(i):
         r = 2 * i
+        through = pre_middle[...] + back_mixed[pl.ds(pl.multiple_of(256 * r, 512), 512), :]
+        back = (through * inner_slope[pl.ds(r + 1, 2)].reshape(512, UNET)).astype(BF16)
+        back_part[pl.ds(pl.multiple_of(64 * r, 128), 128), :] = cosine * dot(by_class(back), inw4_t[...])
+
+    def backward_rows(i, _):
+        backward_after((i + 3) % 4)
         windows = [
-            back_ext[r + 2 - a : r + 4 - a, 64 * (2 - b) : 64 * (2 - b) + 256, :].reshape(512, UNET)
+            back_ext[pl.ds(2 * i + 2 - a, 2), 64 * (2 - b) : 64 * (2 - b) + 256, :].reshape(512, UNET)
             for a in range(3)
             for b in range(3)
         ]
-        through = dot(jnp.concatenate(windows, axis=1), mid_t[...].reshape(9 * UNET, UNET))
-        through = through + back_mixed[256 * r : 256 * r + 512, :]
-        back = (through * inner_slope[r : r + 2].reshape(512, UNET)).astype(BF16)
-        back_part[64 * r : 64 * r + 128, :] = cosine * dot(by_class(back), inw4_t[...])
-
-    backward_rows(0)
-    s2_start(2)
-    backward_rows(1)
-    backward_rows(2)
-    s3_start(0)
-    backward_rows(3)
+        pre_middle[...] = dot(jnp.concatenate(windows, axis=1), mid_t[...].reshape(9 * UNET, UNET))
+
+        @pl.when(i == 0)
+        def _():
+            s2_start(2)
+
+        @pl.when(i == 2)
+        def _():
+            s3_start(0)
+
+        return 0
+
+    lax.fori_loop(0, 4, backward_rows, 0)
+    backward_after(3)
 
     def part_copy(k):
         return remote(
@@ -728,10 +761,10 @@
         pltpu.VMEM((2, 64, 128), BF16),
         pltpu.VMEM((2, 64, 128), BF16),
         pltpu.VMEM((10, 384, UNET), BF16),
-        pltpu.VMEM((8, 256, UNET), F32),
+        pltpu.VMEM((10, 256, UNET), F32),
         pltpu.VMEM((10, UNET, 384), BF16),
         pltpu.VMEM((10, UNET, 256), BF16),
-        pltpu.VMEM((2, 512, UNET), F32),
+        pltpu.VMEM((512, UNET), F32),
         pltpu.VMEM((2048, UNET), F32),
         pltpu.VMEM((10, 384, UNET), BF16),
         pltpu.VMEM((512, 128), F32),

time: 68.5 us -> 70.4 us (1.028)
  Pallas kernels: 66.1 us -> 67.9 us
    pallas_call x1, Pallas kernels: 64.5 us -> 66.3 us  [per_device(): pl.pallas_call(kernel, out_shape=shapes, in_specs=[pl.BlockSpec(memory_sp...]
where the time goes in v4:
time: 70.4 us; the launch traced here: 69.2 us
  Pallas kernels  67.9 us (96%)
  between operations  1.29 us (2%)
    pallas_call x1, Pallas kernels, per_device(): pl.pallas_call(kernel, out_shape=shapes, in_specs=[pl.BlockSpec(memory_sp...  66.3 us
    pallas_call x1, Pallas kernels, per_device(): pl.pallas_call(hand_over, out_shape=shapes, in_specs=[vmem, vmem], out_sp...  1.59 us

profile of v4, /device:TPU:0, one launch (start us, length us, event | category | flops | bytes accessed | tf_op | source)
XLA Modules:
  0.0 69.2 jit_solution(2015381060785625158)
XLA Ops:
  1.3 66.3 %shard_map.104 = (f32[8,16,256]{2,1,0:T(8,128)}, f32[9,3,384]{2,1,0:T(4,128)}) custom-call(s32[1]{0:T(128)S(6)} %copy.11.time_ref, bf16[8,16,256]{2,1,0:T(8,128)(2,1)} %feat_hbm.1, bf16[9,256,512]{2,1,0:T(8,128)(2,1)} %enc_hbm.1, bf16[32,512]{1,0:T(8,128)(2,1)} %bitcast.4, bf16[1,8,8192]{2,1,0:T(8,128)(2,1)} %noise_hbm.1, bf16[1000,384]{1,0:T(8,128)(2,1)} %table_hbm.1, ...), custom_call_target="tpu_custom_call" | custom-call | flops 17999998976 | bytes 8000000 | tf_op jit(solution)/shard_map/pallas_call | solution.py:812
  67.6 1.6 %shard_map.105 = (f32[8,16,256]{2,1,0:T(8,128)}, f32[9,3,384]{2,1,0:T(4,128)}) custom-call(f32[8,16,256]{2,1,0:T(8,128)} %get-tuple-element.6.fgrad_ref, f32[9,3,384]{2,1,0:T(4,128)} %get-tuple-element.7.mgrad_ref), custom_call_target="tpu_custom_call" | custom-call | tf_op jit(solution)/shard_map/pallas_call | solution.py:823

commit v5 on v3

--- a/solution.py
+++ b/solution.py
@@ -115,6 +115,9 @@
     sum2,
     s3_send,
     s3_recv,
+    sum3,
+    s4_send,
+    s4_recv,
     feat_ss,
     feat_rs,
     noise_ss,
@@ -133,6 +136,8 @@
     s2_rs,
     s3_ss,
     s3_rs,
+    s4_ss,
+    s4_rs,
 ):
     t = lax.axis_index("tile")
     s = lax.axis_index("step")
@@ -169,16 +174,10 @@
 
     barrier = pltpu.get_barrier_semaphore()
 
-    def greet_step(k, _):
+    for k in range(1, STEPS):
         pl.semaphore_signal(barrier, inc=1, device_id=(t, (s + k) % STEPS), device_id_type=MESH)
-        return 0
-
-    def greet_tile(k, _):
+    for k in range(1, TILES):
         pl.semaphore_signal(barrier, inc=1, device_id=((t + k) % TILES, s), device_id_type=MESH)
-        return 0
-
-    lax.fori_loop(1, STEPS, greet_step, 0)
-    lax.fori_loop(1, TILES, greet_tile, 0)
     for offsets in AROUND:
         if offsets[0] and offsets[1]:
             pl.semaphore_signal(barrier, inc=1, device_id=near(offsets), device_id_type=MESH)
@@ -231,15 +230,8 @@
         wide[...] = jnp.zeros_like(wide)
         for j in range(4):
             wide[LAT * j : LAT * j + LAT, columns * j : columns * j + columns] = weight[...]
-        flipped[...] = jnp.transpose(wide[...])
-
-    chosen = time_ref[0]
-    angle = ((jnp.full((8, 128), chosen, jnp.int32).astype(F32) + 1.0) / 1000.0 + 0.008) / 1.008 * (math.pi / 2.0)
-    cosine = jnp.cos(angle)[0:1, :]
-    sine = jnp.sin(angle)[0:1, :]
-    l_table.wait()
-    onehot = (lax.broadcasted_iota(jnp.int32, (16, table.shape[0]), 1) == chosen).astype(F32).astype(BF16)
-    embed[...] = dot(onehot, table[...])[0:8]
+        if flipped is latw4:
+            flipped[...] = jnp.transpose(wide[...])
 
     l_enc.wait()
 
@@ -305,19 +297,20 @@
     def lat_copy(k):
         return remote(lat_send, lat_recv.at[k - 1], lat_ss.at[k - 1], lat_rs.at[k - 1], t, (s + k) % STEPS)
 
-    def lat_start(k, _):
+    for k in range(1, STEPS):
         lat_copy(k).start()
-        return 0
-
-    lax.fori_loop(1, STEPS, lat_start, 0)
+
+    inw4_t[...] = jnp.transpose(inw4[...])
+    outw4[...] = jnp.transpose(outw4_t[...])
+    chosen = time_ref[0]
+    angle = ((jnp.full((8, 128), chosen, jnp.int32).astype(F32) + 1.0) / 1000.0 + 0.008) / 1.008 * (math.pi / 2.0)
+    cosine = jnp.cos(angle)[0:1, :]
+    sine = jnp.sin(angle)[0:1, :]
+    l_table.wait()
+    onehot = (lax.broadcasted_iota(jnp.int32, (16, table.shape[0]), 1) == chosen).astype(F32).astype(BF16)
+    embed[...] = dot(onehot, table[...])[0:8]
 
     l_midw.wait()
-
-    def flip_mid(k, _):
-        mid_t[k] = jnp.transpose(midw[k])
-        return 0
-
-    lax.fori_loop(0, 9, flip_mid, 0)
     for side in (0, 1):
         noise_copies[side].wait()
     noise_rows[576:640, :] = noise_edge_in[0].astype(F32)
@@ -325,13 +318,11 @@
 
     lat_flat[pl.ds(pl.multiple_of(s * 48, 16), 48), :] = lat_pack[...].astype(BF16).astype(F32)
 
-    def lat_take(k, _):
+    for k in range(1, STEPS):
         lat_copy(k).wait()
+    for k in range(1, STEPS):
         source = (s - k + STEPS) % STEPS
         lat_flat[pl.ds(pl.multiple_of(source * 48, 16), 48), :] = lat_recv[k - 1].astype(F32)
-        return 0
-
-    lax.fori_loop(1, STEPS, lat_take, 0)
 
     def input_rows(pair):
         first = 2 * pair
@@ -406,6 +397,16 @@
             back_ext[r + 1 + row, 320:384, :] = shift_up(own[0:64]).astype(BF16)
             back_ext[r + 1 + row, 0:64, :] = shift_down(own[192:256]).astype(BF16)
 
+    halo_copies = []
+
+    def halo_start(side):
+        tile, step = near((2 * side - 1, 0))
+        src, dst = ((1, 9), (8, 0))[side]
+        src, dst = back_ext.at[src, pl.ds(64, 256)], back_ext.at[dst, pl.ds(64, 256)]
+        copy = remote(src, dst, halo_ss.at[side], halo_rs.at[side], tile, step)
+        copy.start()
+        halo_copies.append(copy)
+
     input_rows(0)
     input_rows(1)
     for i in range(4):
@@ -415,128 +416,160 @@
         flip_rows(i)
         if i:
             forward_after(i - 1)
+        if i == 1:
+            halo_start(0)
     flip_rows(4)
     forward_after(3)
-
-    halo_copies = []
-    for side, offset in ((0, -1), (1, 1)):
-        tile, step = near((offset, 0))
-        src, dst = (1, 9) if side == 0 else (8, 0)
-        src, dst = back_ext.at[src, pl.ds(64, 256)], back_ext.at[dst, pl.ds(64, 256)]
-        copy = remote(src, dst, halo_ss.at[side], halo_rs.at[side], tile, step)
-        copy.start()
-        halo_copies.append(copy)
+    halo_start(1)
 
     def s1_copy(a):
         return remote(s1_send.at[a], s1_recv.at[a], s1_ss.at[a], s1_rs.at[a], t, s + 1 - 2 * core)
 
-    def s1_start(a):
+    def s1_pack(a):
         for n in range(9):
             first = (n // 3) * UNET + n % 3 + 3 * (1 - core)
             block = jnp.concatenate([grad[a * 3 + i, pl.ds(first, 64, stride=6), :] for i in range(3)], axis=1)
             s1_send[a, 64 * n : 64 * n + 64, :] = block.astype(BF16)
-        s1_copy(a).start()
-
-    def axis_peer(a, k):
-        if a == 0:
-            there = (z + k) % 4
-            return there, t, there * 4 + s % 4
-        if a == 1:
-            there = (x + k) % 4
-            return there, y_hi * 4 + there, s
-        there = (y + k) % 4
-        return there, (there // 2) * 4 + x, z * 4 + (there % 2) * 2 + core
-
-    def plane_rows(a, n, there):
-        base = n * 64
-        parts = []
-        for i in range(3):
-            if a == 0:
-                half = [sum1[a * 3 + i, pl.ds(base + 2 * there + low, 8, stride=8), :] for low in (0, 1)]
-                parts.append(jnp.concatenate(half, axis=0))
-            elif a == 1:
-                half = [
-                    sum1[a * 3 + i, pl.ds(base + high * 32 + pl.multiple_of(there * 8, 8), 8), :] for high in (0, 1)
-                ]
-                parts.append(jnp.concatenate(half, axis=0))
-            else:
-                first = base + (there // 2) * 32 + there % 2
-                parts.append(sum1[a * 3 + i, pl.ds(first, 16, stride=2), :])
-        return jnp.concatenate(parts, axis=1)
-
-    def s2_copy(a, k):
-        _, tile, step = axis_peer(a, k)
-        index = a * 3 + k - 1
-        return remote(s2_send.at[index], s2_recv.at[index], s2_ss.at[index], s2_rs.at[index], tile, step)
-
-    def s2_start(a):
-        s1_copy(a).wait()
-
+
+    def s1_add(a):
         for n in range(9):
             first = (n // 3) * UNET + n % 3 + 3 * core
             got = s1_recv[a, 64 * n : 64 * n + 64, :].astype(F32)
             for i in range(3):
                 own = grad[a * 3 + i, pl.ds(first, 64, stride=6), :]
                 sum1[a * 3 + i, 64 * n : 64 * n + 64, :] = own + got[:, 128 * i : 128 * i + 128]
+
+    def axis_peer(axis, k):
+        if axis == "z":
+            there = (z + k) % 4
+            return there, t, there * 4 + s % 4
+        if axis == "x":
+            there = (x + k) % 4
+            return there, y_hi * 4 + there, s
+        there = (y + k) % 4
+        return there, (there // 2) * 4 + x, z * 4 + (there % 2) * 2 + core
+
+    first_axis, second_axis, third_axis = ("z", "x", "y"), ("x", "z", "z"), ("y", "y", "x")
+
+    def plane_rows(a, b, c, there):
+        base = (3 * b + c) * 64
+        parts = []
+        for i in range(3):
+            ref = sum1.at[a * 3 + i]
+            if b == 0:
+                parts.append(
+                    jnp.concatenate([ref[pl.ds(base + 2 * there + low, 8, stride=8), :] for low in (0, 1)], axis=0)
+                )
+            elif b == 1:
+                rows = [pl.ds(pl.multiple_of(base + high * 32 + there * 8, 8), 8) for high in (0, 1)]
+                parts.append(jnp.concatenate([ref[row, :] for row in rows], axis=0))
+            else:
+                parts.append(ref[pl.ds(base + (there // 2) * 32 + there % 2, 16, stride=2), :])
+        return jnp.concatenate(parts, axis=1)
+
+    def s2_copy(a, b, k):
+        _, tile, step = axis_peer(first_axis[b], k)
+        index = (a * 3 + b) * 3 + k - 1
+        return remote(s2_send.at[index], s2_recv.at[index], s2_ss.at[index], s2_rs.at[index], tile, step)
+
+    def s2_pack(a):
+        for b in range(3):
+            for k in range(1, 4):
+                there = axis_peer(first_axis[b], k)[0]
+                for c in range(3):
+                    block = plane_rows(a, b, c, there).astype(BF16)
+                    s2_send[(a * 3 + b) * 3 + k - 1, 16 * c : 16 * c + 16, :] = block
+
+    def s2_start(a):
         for k in (2, 1, 3):
-            there = axis_peer(a, k)[0]
-            for n in range(9):
-                s2_send[a * 3 + k - 1, 16 * n : 16 * n + 16, :] = plane_rows(a, n, there).astype(BF16)
-            s2_copy(a, k).start()
-
-    def plane_peer(a, k):
-        if a == 0:
-            mine = y_lo * 8 + t
-            there = (mine + k) % 16
-            return mine, there, there % 8, z * 4 + (there // 8) * 2 + core
-        if a == 1:
-            mine = y_hi * 8 + s // 2
-            there = (mine + k) % 16
-            return mine, there, (there // 8) * 4 + x, (there % 8) * 2 + core
-        mine = x * 4 + z
-        there = (mine + k) % 16
-        return mine, there, y_hi * 4 + there // 4, (there % 4) * 4 + s % 4
-
-    def s3_copy(a, k):
-        _, _, tile, step = plane_peer(a, k)
-        index = a * 15 + k - 1
+            for b in range(3):
+                s2_copy(a, b, k).start()
+
+    def s2_wait(a):
+        for b in range(3):
+            for k in range(1, 4):
+                s2_copy(a, b, k).wait()
+
+    def s2_add(a):
+        for b in range(3):
+            mine = axis_peer(first_axis[b], 0)[0]
+            for c in range(3):
+                total = plane_rows(a, b, c, mine)
+                for k in range(3):
+                    total = total + s2_recv[(a * 3 + b) * 3 + k, 16 * c : 16 * c + 16, :].astype(F32)
+                row = 16 * (3 * a + c)
+                for i, part in enumerate(lane_tiles(total)):
+                    sum2[b * 3 + i, row : row + 16, :] = part
+
+    def line_rows(b, there):
+        parts = []
+        for i in range(3):
+            ref = sum2.at[b * 3 + i]
+            if b == 1:
+                parts.append(
+                    jnp.concatenate([ref[pl.ds(2 * there + low, 24, stride=8), :] for low in (0, 1)], axis=0)
+                )
+            else:
+                parts.append(ref[pl.ds(there, 48, stride=4), :])
+        return jnp.concatenate(parts, axis=1)
+
+    def s3_copy(b, k):
+        _, tile, step = axis_peer(second_axis[b], k)
+        index = b * 3 + k - 1
         return remote(s3_send.at[index], s3_recv.at[index], s3_ss.at[index], s3_rs.at[index], tile, step)
 
-    def s3_start(a):
-        for k in range(1, 4):
-            s2_copy(a, k).wait()
-        mine = axis_peer(a, 0)[0]
-
-        for n in range(9):
-            total = plane_rows(a, n, mine)
+    def s3_start():
+        for b in range(3):
+            for k in range(1, 4):
+                s3_send[b * 3 + k - 1] = line_rows(b, axis_peer(second_axis[b], k)[0]).astype(BF16)
+        for b in range(3):
+            for k in range(1, 4):
+                s3_copy(b, k).start()
+
+    def point_rows(b, there):
+        if b == 0:
+            rows = pl.ds((there % 2) * 2 + there // 2, 16, stride=4)
+        elif b == 1:
+            rows = pl.ds((there % 2) * 24 + there // 2, 16, stride=2)
+        else:
+            rows = pl.ds(there, 16, stride=4)
+        return jnp.concatenate([sum3[b * 3 + i, rows, :] for i in range(3)], axis=1)
+
+    def s4_copy(b, k):
+        _, tile, step = axis_peer(third_axis[b], k)
+        index = b * 3 + k - 1
+        return remote(s4_send.at[index], s4_recv.at[index], s4_ss.at[index], s4_rs.at[index], tile, step)
+
+    def s4_start():
+        for b in range(3):
+            for k in range(1, 4):
+                s3_copy(b, k).wait()
+        for b in range(3):
+            total = line_rows(b, axis_peer(second_axis[b], 0)[0])
             for k in range(3):
-                total = total + s2_recv[a * 3 + k, 16 * n : 16 * n + 16, :].astype(F32)
+                total = total + s3_recv[b * 3 + k].astype(F32)
             for i, part in enumerate(lane_tiles(total)):
-                sum2[a * 3 + i, 16 * n : 16 * n + 16, :] = part
-
-        def send(k, _):
-            there = plane_peer(a, k)[1]
-            block = jnp.concatenate([sum2[a * 3 + i, pl.ds(there, 16, stride=16), :] for i in range(3)], axis=1)
-            s3_send[a * 15 + k - 1] = block.astype(BF16)
-            s3_copy(a, k).start()
-            return 0
-
-        lax.fori_loop(1, 16, send, 0)
-
-    def finish(a):
-        mine = plane_peer(a, 0)[0]
-        own = jnp.concatenate([sum2[a * 3 + i, pl.ds(mine, 16, stride=16), :] for i in range(3)], axis=1)
-
-        def add(k, total):
-            s3_copy(a, k).wait()
-            return total + s3_recv[a * 15 + k - 1].astype(F32)
-
-        total = lax.fori_loop(1, 16, add, own) * (1.0 / math.sqrt(64 * 256))
-        for b in range(3):
-            mgrad_ref[3 * a + b] = total[3 * b : 3 * b + 3]
-
-    sum2[...] = jnp.zeros_like(sum2)
-    for a in range(3):
+                sum3[b * 3 + i, 0:48, :] = part
+        for b in range(3):
+            for k in range(1, 4):
+                s4_send[b * 3 + k - 1] = point_rows(b, axis_peer(third_axis[b], k)[0]).astype(BF16)
+        for b in range(3):
+            for k in range(1, 4):
+                s4_copy(b, k).start()
+
+    def finish():
+        for b in range(3):
+            for k in range(1, 4):
+                s4_copy(b, k).wait()
+        for b in range(3):
+            total = point_rows(b, axis_peer(third_axis[b], 0)[0])
+            for k in range(3):
+                total = total + s4_recv[b * 3 + k].astype(F32)
+            total = total * (1.0 / math.sqrt(64 * 256))
+            for a in range(3):
+                mgrad_ref[3 * a + b] = total[3 * a : 3 * a + 3]
+
+    def weight_product(a):
         taps = [
             jnp.concatenate([inner_t[r + a, :, 0:256] for r in range(8)], axis=1),
             jnp.concatenate([inner_tm[r + a] for r in range(8)], axis=1),
@@ -545,11 +578,16 @@
         result = dot(jnp.concatenate(taps, axis=0), back_ext[1:9, 64:320, :].reshape(2048, UNET))
         for i, part in enumerate(lane_tiles(result)):
             grad[a * 3 + i] = part
+
+    sum2[...] = jnp.zeros_like(sum2)
+    sum3[...] = jnp.zeros_like(sum3)
+    for a in range(3):
+        weight_product(a)
         for k in range(3 * a, 3 * a + 3):
-            enc_t[k] = jnp.transpose(enc[k])
-        s1_start(a)
+            mid_t[k] = jnp.transpose(midw[k])
         if a:
-            s2_start(a - 1)
+            s1_pack(a - 1)
+            s1_copy(a - 1).start()
 
     for row, copy in ((9, halo_copies[0]), (0, halo_copies[1])):
         copy.wait()
@@ -564,44 +602,76 @@
     def _():
         back_ext[9] = jnp.zeros_like(back_ext[9])
 
-    def backward_rows(i):
+    def backward_conv(i):
         r = 2 * i
         windows = [
             back_ext[r + 2 - a : r + 4 - a, 64 * (2 - b) : 64 * (2 - b) + 256, :].reshape(512, UNET)
             for a in range(3)
             for b in range(3)
         ]
-        through = dot(jnp.concatenate(windows, axis=1), mid_t[...].reshape(9 * UNET, UNET))
-        through = through + back_mixed[256 * r : 256 * r + 512, :]
+        pre_middle[i % 2] = dot(jnp.concatenate(windows, axis=1), mid_t[...].reshape(9 * UNET, UNET))
+
+    def backward_after(i):
+        r = 2 * i
+        through = pre_middle[i % 2] + back_mixed[256 * r : 256 * r + 512, :]
         back = (through * inner_slope[r : r + 2].reshape(512, UNET)).astype(BF16)
         back_part[64 * r : 64 * r + 128, :] = cosine * dot(by_class(back), inw4_t[...])
 
-    backward_rows(0)
+    def flip_enc(first, last):
+        for k in range(first, last):
+            enc_t[k] = jnp.transpose(enc[k])
+
+    s1_copy(0).wait()
+    backward_conv(0)
+    s1_pack(2)
+    s1_add(0)
+    s2_pack(0)
+    flip_enc(0, 3)
+    s1_copy(2).start()
+    s2_start(0)
+
+    s1_copy(1).wait()
+    backward_conv(1)
+    backward_after(0)
+    s1_add(1)
+    s2_pack(1)
+    flip_enc(3, 6)
+    s2_start(1)
+
+    s1_copy(2).wait()
+    backward_conv(2)
+    backward_after(1)
+    s1_add(2)
+    s2_pack(2)
+    flip_enc(6, 9)
     s2_start(2)
-    backward_rows(1)
-    backward_rows(2)
-    s3_start(0)
-    backward_rows(3)
+
+    s2_wait(0)
+    backward_conv(3)
+    backward_after(2)
+    s2_add(0)
+    backward_after(3)
 
     def part_copy(k):
         return remote(
             part_send.at[k - 1], part_recv.at[k - 1], part_ss.at[k - 1], part_rs.at[k - 1], t, (s + k) % STEPS
         )
 
-    def part_start(k, _):
+    for k in range(1, STEPS):
         part_send[k - 1] = back_part[pl.ds((s + k) % STEPS, 32, stride=16), :].astype(BF16)
+    for k in range(1, STEPS):
         part_copy(k).start()
-        return 0
-
-    lax.fori_loop(1, STEPS, part_start, 0)
-
-    s3_start(1)
-
-    def part_add(k, total):
+
+    for a in (1, 2):
+        s2_wait(a)
+        s2_add(a)
+    s3_start()
+
+    for k in range(1, STEPS):
         part_copy(k).wait()
-        return total + part_recv[k - 1].astype(F32)
-
-    latent_round = lax.fori_loop(1, STEPS, part_add, back_part[pl.ds(s, 32, stride=16), :])
+    latent_round = back_part[pl.ds(s, 32, stride=16), :]
+    for k in range(1, STEPS):
+        latent_round = latent_round + part_recv[k - 1].astype(F32)
     round_send[...] = latent_round.astype(BF16)
     round_copies = []
     for d, offsets in enumerate(AROUND):
@@ -610,7 +680,7 @@
         copy.start()
         round_copies.append(copy)
 
-    s3_start(2)
+    s4_start()
 
     round_grid[...] = jnp.zeros_like(round_grid)
     round_pack[...] = round_send[...].astype(F32)
@@ -660,8 +730,7 @@
         for i in range(2):
             fgrad_ref[r, :, 128 * i : 128 * i + 128] = out_grid[i, r * 32 + 8 : r * 32 + 24, :]
 
-    for a in range(3):
-        finish(a)
+    finish()
 
 
 def hand_over(fgrad_ref, mgrad_ref, fgrad_out, mgrad_out):
@@ -748,11 +817,14 @@
         pltpu.VMEM((3, 576, UNET), BF16),
         pltpu.VMEM((3, 576, UNET), BF16),
         pltpu.VMEM((9, 576, 128), F32),
-        pltpu.VMEM((9, 144, UNET), BF16),
-        pltpu.VMEM((9, 144, UNET), BF16),
+        pltpu.VMEM((27, 48, UNET), BF16),
+        pltpu.VMEM((27, 48, UNET), BF16),
         pltpu.VMEM((9, 256, 128), F32),
-        pltpu.VMEM((45, 16, UNET), BF16),
-        pltpu.VMEM((45, 16, UNET), BF16),
+        pltpu.VMEM((9, 48, UNET), BF16),
+        pltpu.VMEM((9, 48, UNET), BF16),
+        pltpu.VMEM((9, 64, 128), F32),
+        pltpu.VMEM((9, 16, UNET), BF16),
+        pltpu.VMEM((9, 16, UNET), BF16),
         dma((8,)),
         dma((8,)),
         dma((2,)),
@@ -767,10 +839,12 @@
         dma((8,)),
         dma((3,)),
         dma((3,)),
+        dma((27,)),
+        dma((27,)),
         dma((9,)),
         dma((9,)),
-        dma((45,)),
-        dma((45,)),
+        dma((9,)),
+        dma((9,)),
     ]
     shapes = (
         jax.ShapeDtypeStruct((8, 16, FEAT), F32),

time: 68.5 us -> 65.8 us (0.961)
  Pallas kernels: 66.1 us -> 63.4 us
    pallas_call x1, Pallas kernels: 64.5 us -> 61.9 us  [per_device(): pl.pallas_call(kernel, out_shape=shapes, in_specs=[pl.BlockSpec(memory_sp...]
where the time goes in v5:
time: 65.8 us; the launch traced here: 64.7 us
  Pallas kernels  63.4 us (96%)
  between operations  1.29 us (2%)
    pallas_call x1, Pallas kernels, per_device(): pl.pallas_call(kernel, out_shape=shapes, in_specs=[pl.BlockSpec(memory_sp...  61.9 us
    pallas_call x1, Pallas kernels, per_device(): pl.pallas_call(hand_over, out_shape=shapes, in_specs=[vmem, vmem], out_sp...  1.59 us

profile of v5, /device:TPU:0, one launch (start us, length us, event | category | flops | bytes accessed | tf_op | source)
XLA Modules:
  0.0 64.7 jit_solution(2955778301188283313)
XLA Ops:
  1.3 61.9 %shard_map.104 = (f32[8,16,256]{2,1,0:T(8,128)}, f32[9,3,384]{2,1,0:T(4,128)}) custom-call(s32[1]{0:T(128)S(6)} %copy.11.time_ref, bf16[8,16,256]{2,1,0:T(8,128)(2,1)} %feat_hbm.1, bf16[9,256,512]{2,1,0:T(8,128)(2,1)} %enc_hbm.1, bf16[32,512]{1,0:T(8,128)(2,1)} %bitcast.4, bf16[1,8,8192]{2,1,0:T(8,128)(2,1)} %noise_hbm.1, bf16[1000,384]{1,0:T(8,128)(2,1)} %table_hbm.1, ...), custom_call_target="tpu_custom_call" | custom-call | flops 17999998976 | bytes 8000000 | tf_op jit(solution)/shard_map/pallas_call | solution.py:853
  63.1 1.6 %shard_map.105 = (f32[8,16,256]{2,1,0:T(8,128)}, f32[9,3,384]{2,1,0:T(4,128)}) custom-call(f32[8,16,256]{2,1,0:T(8,128)} %get-tuple-element.6.fgrad_ref, f32[9,3,384]{2,1,0:T(4,128)} %get-tuple-element.7.mgrad_ref), custom_call_target="tpu_custom_call" | custom-call | tf_op jit(solution)/shard_map/pallas_call | solution.py:864

commit v6 on v5

--- a/solution.py
+++ b/solution.py
@@ -324,17 +324,16 @@
         source = (s - k + STEPS) % STEPS
         lat_flat[pl.ds(pl.multiple_of(source * 48, 16), 48), :] = lat_recv[k - 1].astype(F32)
 
-    def input_rows(pair):
-        first = 2 * pair
-        latent = [lat_flat[pl.ds((first + r) * 4 + q, 16, stride=48), :] for r in range(2) for q in range(4)]
-        noisy = cosine * jnp.concatenate(latent, axis=0) + sine * noise_rows[64 * first : 64 * first + 128, :]
-        noisy = noisy.astype(BF16)
+    def input_rows(first, count):
+        latent = [lat_flat[pl.ds((first + r) * 4 + q, 16, stride=48), :] for r in range(count) for q in range(4)]
+        noisy = sine * noise_rows[64 * first : 64 * (first + count), :]
+        noisy = (cosine * jnp.concatenate(latent, axis=0) + noisy).astype(BF16)
         for j in range(4):
             pre = dot(noisy, inw4[:, UNET * j : UNET * j + UNET]) + embed[0:1, :]
             sigma = sigmoid(pre)
             inner = pre * sigma
             slope = slope_of(pre, sigma)
-            for r in range(2):
+            for r in range(count):
                 row = first + r
                 own = inner[64 * r : 64 * r + 64]
                 if row == 0:
@@ -349,8 +348,8 @@
                 if 0 < row < 9:
                     inner_slope[row - 1, 64 * j : 64 * j + 64, :] = slope[64 * r : 64 * r + 64]
 
-    def flip_rows(pair):
-        for row in (2 * pair, 2 * pair + 1):
+    def flip_rows(first, last):
+        for row in range(first, last):
             flipped = jnp.transpose(inner_ext[row])
             inner_t[row] = flipped
             inner_tm[row] = flipped[:, 64:320]
@@ -373,25 +372,25 @@
 
     def forward_conv(i):
         windows = [
-            inner_ext[2 * i + a : 2 * i + a + 2, 64 * b : 64 * b + 256, :].reshape(512, UNET)
+            inner_ext[4 * i + a : 4 * i + a + 4, 64 * b : 64 * b + 256, :].reshape(1024, UNET)
             for a in range(3)
             for b in range(3)
         ]
-        pre_middle[i % 2] = dot(jnp.concatenate(windows, axis=1), midw[...].reshape(9 * UNET, UNET))
+        pre_middle[i] = dot(jnp.concatenate(windows, axis=1), midw[...].reshape(9 * UNET, UNET))
 
     def forward_after(i):
-        r = 2 * i
-        pre = pre_middle[i % 2]
+        r = 4 * i
+        pre = pre_middle[i]
         sigma = sigmoid(pre)
-        own = inner_ext[r + 1 : r + 3, 64:320, :].reshape(512, UNET)
+        own = inner_ext[r + 1 : r + 5, 64:320, :].reshape(1024, UNET)
         mixed = (own.astype(F32) + pre * sigma).astype(BF16)
         prediction = dot(by_class(mixed), outw4[...])
-        own_noise = noise_rows[64 + r * 64 : 192 + r * 64, :]
+        own_noise = noise_rows[64 + r * 64 : 320 + r * 64, :]
         error = ((prediction - own_noise) * (1.0 / math.sqrt(STEPS))).astype(BF16)
         pulled = by_position(dot(error, outw4_t[...]))
-        back_mixed[256 * r : 256 * r + 512, :] = pulled
+        back_mixed[256 * r : 256 * r + 1024, :] = pulled
         back = pulled * slope_of(pre, sigma)
-        for row in range(2):
+        for row in range(4):
             own = back[256 * row : 256 * row + 256]
             back_ext[r + 1 + row, 64:320, :] = own.astype(BF16)
             back_ext[r + 1 + row, 320:384, :] = shift_up(own[0:64]).astype(BF16)
@@ -407,19 +406,15 @@
         copy.start()
         halo_copies.append(copy)
 
-    input_rows(0)
-    input_rows(1)
-    for i in range(4):
-        forward_conv(i)
-        if i < 3:
-            input_rows(i + 2)
-        flip_rows(i)
-        if i:
-            forward_after(i - 1)
-        if i == 1:
-            halo_start(0)
-    flip_rows(4)
-    forward_after(3)
+    input_rows(0, 6)
+    forward_conv(0)
+    input_rows(6, 4)
+    flip_rows(0, 5)
+    forward_conv(1)
+    forward_after(0)
+    flip_rows(5, 10)
+    halo_start(0)
+    forward_after(1)
     halo_start(1)
 
     def s1_copy(a):
@@ -585,9 +580,14 @@
         weight_product(a)
         for k in range(3 * a, 3 * a + 3):
             mid_t[k] = jnp.transpose(midw[k])
-        if a:
-            s1_pack(a - 1)
-            s1_copy(a - 1).start()
+        if a == 2:
+            s1_add(0)
+            s2_pack(0)
+            s2_start(0)
+        s1_pack(a)
+        s1_copy(a).start()
+        if a == 1:
+            s1_copy(0).wait()
 
     for row, copy in ((9, halo_copies[0]), (0, halo_copies[1])):
         copy.wait()
@@ -603,54 +603,39 @@
         back_ext[9] = jnp.zeros_like(back_ext[9])
 
     def backward_conv(i):
-        r = 2 * i
+        r = 4 * i
         windows = [
-            back_ext[r + 2 - a : r + 4 - a, 64 * (2 - b) : 64 * (2 - b) + 256, :].reshape(512, UNET)
+            back_ext[r + 2 - a : r + 6 - a, 64 * (2 - b) : 64 * (2 - b) + 256, :].reshape(1024, UNET)
             for a in range(3)
             for b in range(3)
         ]
-        pre_middle[i % 2] = dot(jnp.concatenate(windows, axis=1), mid_t[...].reshape(9 * UNET, UNET))
+        pre_middle[i] = dot(jnp.concatenate(windows, axis=1), mid_t[...].reshape(9 * UNET, UNET))
 
     def backward_after(i):
-        r = 2 * i
-        through = pre_middle[i % 2] + back_mixed[256 * r : 256 * r + 512, :]
-        back = (through * inner_slope[r : r + 2].reshape(512, UNET)).astype(BF16)
-        back_part[64 * r : 64 * r + 128, :] = cosine * dot(by_class(back), inw4_t[...])
+        r = 4 * i
+        through = pre_middle[i] + back_mixed[256 * r : 256 * r + 1024, :]
+        back = (through * inner_slope[r : r + 4].reshape(1024, UNET)).astype(BF16)
+        back_part[64 * r : 64 * r + 256, :] = cosine * dot(by_class(back), inw4_t[...])
 
     def flip_enc(first, last):
         for k in range(first, last):
             enc_t[k] = jnp.transpose(enc[k])
 
-    s1_copy(0).wait()
+    s1_copy(1).wait()
     backward_conv(0)
-    s1_pack(2)
-    s1_add(0)
-    s2_pack(0)
-    flip_enc(0, 3)
-    s1_copy(2).start()
-    s2_start(0)
-
-    s1_copy(1).wait()
+    s1_add(1)
+    s2_pack(1)
+    flip_enc(0, 5)
+    s2_start(1)
+
+    s1_copy(2).wait()
     backward_conv(1)
     backward_after(0)
-    s1_add(1)
-    s2_pack(1)
-    flip_enc(3, 6)
-    s2_start(1)
-
-    s1_copy(2).wait()
-    backward_conv(2)
-    backward_after(1)
     s1_add(2)
     s2_pack(2)
-    flip_enc(6, 9)
+    flip_enc(5, 9)
     s2_start(2)
-
-    s2_wait(0)
-    backward_conv(3)
-    backward_after(2)
-    s2_add(0)
-    backward_after(3)
+    backward_after(1)
 
     def part_copy(k):
         return remote(
@@ -662,7 +647,7 @@
     for k in range(1, STEPS):
         part_copy(k).start()
 
-    for a in (1, 2):
+    for a in range(3):
         s2_wait(a)
         s2_add(a)
     s3_start()
@@ -800,7 +785,7 @@
         pltpu.VMEM((8, 256, UNET), F32),
         pltpu.VMEM((10, UNET, 384), BF16),
         pltpu.VMEM((10, UNET, 256), BF16),
-        pltpu.VMEM((2, 512, UNET), F32),
+        pltpu.VMEM((2, 1024, UNET), F32),
         pltpu.VMEM((2048, UNET), F32),
         pltpu.VMEM((10, 384, UNET), BF16),
         pltpu.VMEM((512, 128), F32),

time: 65.8 us -> 66.4 us (level); the launches traced: 64.7 us -> 66.1 us
  Pallas kernels: 63.4 us -> 64.8 us
    pallas_call x1, Pallas kernels: 61.9 us -> 63.3 us  [per_device(): pl.pallas_call(kernel, out_shape=shapes, in_specs=[pl.BlockSpec(memory_sp...]
where the time goes in v6:
time: 66.4 us; the launch traced here: 66.1 us
  Pallas kernels  64.8 us (98%)
  between operations  1.29 us (2%)
    pallas_call x1, Pallas kernels, per_device(): pl.pallas_call(kernel, out_shape=shapes, in_specs=[pl.BlockSpec(memory_sp...  63.3 us
    pallas_call x1, Pallas kernels, per_device(): pl.pallas_call(hand_over, out_shape=shapes, in_specs=[vmem, vmem], out_sp...  1.59 us

profile of v6, /device:TPU:0, one launch (start us, length us, event | category | flops | bytes accessed | tf_op | source)
XLA Modules:
  0.0 66.1 jit_solution(7911637507401645909)
XLA Ops:
  1.3 63.3 %shard_map.104 = (f32[8,16,256]{2,1,0:T(8,128)}, f32[9,3,384]{2,1,0:T(4,128)}) custom-call(s32[1]{0:T(128)S(6)} %copy.11.time_ref, bf16[8,16,256]{2,1,0:T(8,128)(2,1)} %feat_hbm.1, bf16[9,256,512]{2,1,0:T(8,128)(2,1)} %enc_hbm.1, bf16[32,512]{1,0:T(8,128)(2,1)} %bitcast.4, bf16[1,8,8192]{2,1,0:T(8,128)(2,1)} %noise_hbm.1, bf16[1000,384]{1,0:T(8,128)(2,1)} %table_hbm.1, ...), custom_call_target="tpu_custom_call" | custom-call | flops 17999998976 | bytes 8000000 | tf_op jit(solution)/shard_map/pallas_call | solution.py:838
  64.5 1.6 %shard_map.105 = (f32[8,16,256]{2,1,0:T(8,128)}, f32[9,3,384]{2,1,0:T(4,128)}) custom-call(f32[8,16,256]{2,1,0:T(8,128)} %get-tuple-element.6.fgrad_ref, f32[9,3,384]{2,1,0:T(4,128)} %get-tuple-element.7.mgrad_ref), custom_call_target="tpu_custom_call" | custom-call | tf_op jit(solution)/shard_map/pallas_call | solution.py:849

commit v7 on v5

--- a/solution.py
+++ b/solution.py
@@ -99,9 +99,9 @@
     back_part,
     part_send,
     part_recv,
-    round_pack,
-    round_send,
-    round_recv,
+    rim_send,
+    rim_recv,
+    part_sum,
     round_grid,
     hidden_even,
     hidden_odd,
@@ -128,8 +128,8 @@
     halo_rs,
     part_ss,
     part_rs,
-    round_ss,
-    round_rs,
+    rim_ss,
+    rim_rs,
     s1_ss,
     s1_rs,
     s2_ss,
@@ -585,9 +585,14 @@
         weight_product(a)
         for k in range(3 * a, 3 * a + 3):
             mid_t[k] = jnp.transpose(midw[k])
-        if a:
-            s1_pack(a - 1)
-            s1_copy(a - 1).start()
+        if a == 2:
+            s1_add(0)
+            s2_pack(0)
+            s2_start(0)
+        s1_pack(a)
+        s1_copy(a).start()
+        if a == 1:
+            s1_copy(0).wait()
 
     for row, copy in ((9, halo_copies[0]), (0, halo_copies[1])):
         copy.wait()
@@ -615,96 +620,100 @@
         r = 2 * i
         through = pre_middle[i % 2] + back_mixed[256 * r : 256 * r + 512, :]
         back = (through * inner_slope[r : r + 2].reshape(512, UNET)).astype(BF16)
-        back_part[64 * r : 64 * r + 128, :] = cosine * dot(by_class(back), inw4_t[...])
+        back_part[64 * r + 64 : 64 * r + 192, :] = cosine * dot(by_class(back), inw4_t[...])
 
     def flip_enc(first, last):
         for k in range(first, last):
             enc_t[k] = jnp.transpose(enc[k])
 
-    s1_copy(0).wait()
+    back_part[640:1024, :] = jnp.zeros((384, 128), F32)
+    s1_copy(1).wait()
     backward_conv(0)
-    s1_pack(2)
-    s1_add(0)
-    s2_pack(0)
-    flip_enc(0, 3)
-    s1_copy(2).start()
-    s2_start(0)
-
-    s1_copy(1).wait()
-    backward_conv(1)
-    backward_after(0)
     s1_add(1)
     s2_pack(1)
+    flip_enc(0, 3)
+    s2_start(1)
+
+    s1_copy(2).wait()
+    backward_conv(3)
+    backward_after(0)
+    s1_add(2)
+    s2_pack(2)
     flip_enc(3, 6)
-    s2_start(1)
-
-    s1_copy(2).wait()
+    s2_start(2)
+
+    backward_after(3)
+    rim_copies = []
+    for side, row in ((0, 1), (1, 8)):
+        rim_send[side] = back_part[64 * row : 64 * row + 64, :].astype(BF16)
+        tile, step = near((2 * side - 1, 0))
+        copy = remote(rim_send.at[side], rim_recv.at[side], rim_ss.at[side], rim_rs.at[side], tile, step)
+        copy.start()
+        rim_copies.append(copy)
+
+    backward_conv(1)
+    flip_enc(6, 9)
     backward_conv(2)
     backward_after(1)
-    s1_add(2)
-    s2_pack(2)
-    flip_enc(6, 9)
-    s2_start(2)
-
-    s2_wait(0)
-    backward_conv(3)
     backward_after(2)
-    s2_add(0)
-    backward_after(3)
+
+    for copy in rim_copies:
+        copy.wait()
+    back_part[576:640, :] = jnp.where(t < TILES - 1, rim_recv[0].astype(F32), 0.0)
+    back_part[0:64, :] = jnp.where(t > 0, rim_recv[1].astype(F32), 0.0)
+
+    lane = lax.broadcasted_iota(jnp.int32, (16, 128), 1)
+
+    def part_of(step):
+        beside = jnp.where(
+            lane < 64, back_part[pl.ds(step + 1, 16, stride=64), :], back_part[pl.ds(step + 47, 16, stride=64), :]
+        )
+        return jnp.concatenate([back_part[pl.ds(step, 40, stride=16), :], beside], axis=0)
 
     def part_copy(k):
         return remote(
             part_send.at[k - 1], part_recv.at[k - 1], part_ss.at[k - 1], part_rs.at[k - 1], t, (s + k) % STEPS
         )
 
+    part_blank = jnp.zeros((8, 128), F32)
     for k in range(1, STEPS):
-        part_send[k - 1] = back_part[pl.ds((s + k) % STEPS, 32, stride=16), :].astype(BF16)
+        block = jnp.concatenate([part_of((s + k) % STEPS), part_blank], axis=0)
+        part_send[k - 1] = block.astype(BF16)
     for k in range(1, STEPS):
         part_copy(k).start()
 
-    for a in (1, 2):
+    for a in range(3):
         s2_wait(a)
         s2_add(a)
     s3_start()
 
     for k in range(1, STEPS):
         part_copy(k).wait()
-    latent_round = back_part[pl.ds(s, 32, stride=16), :]
+    total = part_of(s)
     for k in range(1, STEPS):
-        latent_round = latent_round + part_recv[k - 1].astype(F32)
-    round_send[...] = latent_round.astype(BF16)
-    round_copies = []
-    for d, offsets in enumerate(AROUND):
-        tile, step = near(offsets)
-        copy = remote(round_send, round_recv.at[d], round_ss.at[d], round_rs.at[d], tile, step)
-        copy.start()
-        round_copies.append(copy)
+        total = total + part_recv[k - 1].astype(F32)[0:56]
+    part_sum[0:56, :] = total
 
     s4_start()
 
     round_grid[...] = jnp.zeros_like(round_grid)
-    round_pack[...] = round_send[...].astype(F32)
     for q in range(4):
-        round_grid[pl.ds(10 + q, 8, stride=8), :] = round_pack[pl.ds(q, 8, stride=4), :]
-    for d, (dt, ds) in enumerate(AROUND):
-        round_copies[d].wait()
-        valid = jnp.bool_(True)
-        if dt:
-            valid = (t < TILES - 1) if dt < 0 else (t > 0)
-        if ds:
-            beside = (s < STEPS - 1) if ds < 0 else (s > 0)
-            valid = jnp.logical_and(valid, beside) if dt else beside
-        round_pack[...] = jnp.where(valid, round_recv[d].astype(F32), 0.0)
-        if dt == 0:
-            q, place = (0, 6) if ds < 0 else (3, 1)
-            round_grid[pl.ds(8 + place, 8, stride=8), :] = round_pack[pl.ds(q, 8, stride=4), :]
-        else:
-            source, row = (0, 72) if dt < 0 else (28, 0)
-            if ds == 0:
-                round_grid[row + 2 : row + 6, :] = round_pack[source : source + 4, :]
-            else:
-                q, place = (0, 6) if ds < 0 else (3, 1)
-                round_grid[row + place : row + place + 1, :] = round_pack[source + q : source + q + 1, :]
+        round_grid[pl.ds(2 + q, 10, stride=8), :] = part_sum[pl.ds(q, 10, stride=4), :]
+    beside = part_sum[40:50, :]
+    lane = lax.broadcasted_iota(jnp.int32, (10, 128), 1)
+    left = jnp.logical_and(s > 0, lane >= 3 * LAT)
+    right = jnp.logical_and(s < STEPS - 1, lane < LAT)
+    round_grid[pl.ds(1, 10, stride=8), :] = jnp.where(left, beside, 0.0)
+    round_grid[pl.ds(6, 10, stride=8), :] = jnp.where(right, beside, 0.0)
+
+    @pl.when(t == 0)
+    def _():
+        round_grid[0:8, :] = jnp.zeros((8, 128), F32)
+
+    @pl.when(t == TILES - 1)
+    def _():
+        round_grid[72:80, :] = jnp.zeros((8, 128), F32)
+
     pulled = dot(round_grid[...].astype(BF16), latw4_t[...])
     for j in range(4):
         pre = pre_hidden[80 * j : 80 * j + 80, :]
@@ -803,12 +812,12 @@
         pltpu.VMEM((2, 512, UNET), F32),
         pltpu.VMEM((2048, UNET), F32),
         pltpu.VMEM((10, 384, UNET), BF16),
-        pltpu.VMEM((512, 128), F32),
-        pltpu.VMEM((15, 32, 128), BF16),
-        pltpu.VMEM((15, 32, 128), BF16),
-        pltpu.VMEM((32, 128), F32),
-        pltpu.VMEM((32, 128), BF16),
-        pltpu.VMEM((8, 32, 128), BF16),
+        pltpu.VMEM((1024, 128), F32),
+        pltpu.VMEM((15, 64, 128), BF16),
+        pltpu.VMEM((15, 64, 128), BF16),
+        pltpu.VMEM((2, 64, 128), BF16),
+        pltpu.VMEM((2, 64, 128), BF16),
+        pltpu.VMEM((64, 128), F32),
         pltpu.VMEM((80, 128), F32),
         pltpu.VMEM((6, 80, HID), BF16),
         pltpu.VMEM((6, 72, HID), BF16),
@@ -835,8 +844,8 @@
         dma((2,)),
         dma((15,)),
         dma((15,)),
-        dma((8,)),
-        dma((8,)),
+        dma((2,)),
+        dma((2,)),
         dma((3,)),
         dma((3,)),
         dma((27,)),

time: 65.8 us -> 66.2 us (level); the launches traced: 64.7 us -> 66 us
  Pallas kernels: 63.4 us -> 64.8 us
    pallas_call x1, Pallas kernels: 61.9 us -> 63.2 us  [per_device(): pl.pallas_call(kernel, out_shape=shapes, in_specs=[pl.BlockSpec(memory_sp...]
where the time goes in v7:
time: 66.2 us; the launch traced here: 66 us
  Pallas kernels  64.8 us (98%)
  between operations  1.29 us (2%)
    pallas_call x1, Pallas kernels, per_device(): pl.pallas_call(kernel, out_shape=shapes, in_specs=[pl.BlockSpec(memory_sp...  63.2 us
    pallas_call x1, Pallas kernels, per_device(): pl.pallas_call(hand_over, out_shape=shapes, in_specs=[vmem, vmem], out_sp...  1.59 us

profile of v7, /device:TPU:0, one launch (start us, length us, event | category | flops | bytes accessed | tf_op | source)
XLA Modules:
  0.0 66.0 jit_solution(2115056191387161082)
XLA Ops:
  1.3 63.2 %shard_map.104 = (f32[8,16,256]{2,1,0:T(8,128)}, f32[9,3,384]{2,1,0:T(4,128)}) custom-call(s32[1]{0:T(128)S(6)} %copy.11.time_ref, bf16[8,16,256]{2,1,0:T(8,128)(2,1)} %feat_hbm.1, bf16[9,256,512]{2,1,0:T(8,128)(2,1)} %enc_hbm.1, bf16[32,512]{1,0:T(8,128)(2,1)} %bitcast.4, bf16[1,8,8192]{2,1,0:T(8,128)(2,1)} %noise_hbm.1, bf16[1000,384]{1,0:T(8,128)(2,1)} %table_hbm.1, ...), custom_call_target="tpu_custom_call" | custom-call | flops 17999998976 | bytes 8000000 | tf_op jit(solution)/shard_map/pallas_call | solution.py:862
  64.5 1.6 %shard_map.105 = (f32[8,16,256]{2,1,0:T(8,128)}, f32[9,3,384]{2,1,0:T(4,128)}) custom-call(f32[8,16,256]{2,1,0:T(8,128)} %get-tuple-element.6.fgrad_ref, f32[9,3,384]{2,1,0:T(4,128)} %get-tuple-element.7.mgrad_ref), custom_call_target="tpu_custom_call" | custom-call | tf_op jit(solution)/shard_map/pallas_call | solution.py:873

commit v8 on v7

--- a/solution.py
+++ b/solution.py
@@ -153,24 +153,18 @@
     def near(offsets):
         return (t + offsets[0] + TILES) % TILES, (s + offsets[1] + STEPS) % STEPS
 
+    small = ((feat_hbm, feat), (noise_hbm, noise), (latw_hbm, latw), (inw_hbm, inw), (outw_hbm, outw), (table_hbm, table))
+    large = [
+        (src.at[pl.ds(3 * i, 3)], dst.at[pl.ds(3 * i, 3)]) for src, dst in ((enc_hbm, enc), (midw_hbm, midw)) for i in range(3)
+    ]
     loads = [
-        pltpu.make_async_copy(src, dst, in_sem.at[i])
-        for i, (src, dst) in enumerate(
-            (
-                (feat_hbm, feat),
-                (noise_hbm, noise),
-                (enc_hbm, enc),
-                (latw_hbm, latw),
-                (inw_hbm, inw),
-                (outw_hbm, outw),
-                (table_hbm, table),
-                (midw_hbm, midw),
-            )
-        )
+        pltpu.make_async_copy(src, dst, in_sem.at[i]) for i, (src, dst) in enumerate((*small[:2], *large, *small[2:]))
     ]
     for load in loads:
         load.start()
-    l_feat, l_noise, l_enc, l_latw, l_inw, l_outw, l_table, l_midw = loads
+    l_feat, l_noise = loads[:2]
+    l_enc, l_midw = loads[2:5], loads[5:8]
+    l_latw, l_inw, l_outw, l_table = loads[8:]
 
     barrier = pltpu.get_barrier_semaphore()
 
@@ -233,7 +227,8 @@
         if flipped is latw4:
             flipped[...] = jnp.transpose(wide[...])
 
-    l_enc.wait()
+    for load in l_enc:
+        load.wait()
 
     for d, copy in enumerate(feat_copies):
         copy.wait()
@@ -310,7 +305,8 @@
     onehot = (lax.broadcasted_iota(jnp.int32, (16, table.shape[0]), 1) == chosen).astype(F32).astype(BF16)
     embed[...] = dot(onehot, table[...])[0:8]
 
-    l_midw.wait()
+    for load in l_midw:
+        load.wait()
     for side in (0, 1):
         noise_copies[side].wait()
     noise_rows[576:640, :] = noise_edge_in[0].astype(F32)
@@ -585,14 +581,8 @@
         weight_product(a)
         for k in range(3 * a, 3 * a + 3):
             mid_t[k] = jnp.transpose(midw[k])
-        if a == 2:
-            s1_add(0)
-            s2_pack(0)
-            s2_start(0)
         s1_pack(a)
         s1_copy(a).start()
-        if a == 1:
-            s1_copy(0).wait()
 
     for row, copy in ((9, halo_copies[0]), (0, halo_copies[1])):
         copy.wait()
@@ -627,20 +617,18 @@
             enc_t[k] = jnp.transpose(enc[k])
 
     back_part[640:1024, :] = jnp.zeros((384, 128), F32)
+    backward_conv(0)
+    flip_enc(0, 4)
+
+    s1_copy(0).wait()
     s1_copy(1).wait()
-    backward_conv(0)
-    s1_add(1)
-    s2_pack(1)
-    flip_enc(0, 3)
-    s2_start(1)
-
-    s1_copy(2).wait()
     backward_conv(3)
     backward_after(0)
-    s1_add(2)
-    s2_pack(2)
-    flip_enc(3, 6)
-    s2_start(2)
+    for a in (0, 1):
+        s1_add(a)
+        s2_pack(a)
+    s2_start(0)
+    s2_start(1)
 
     backward_after(3)
     rim_copies = []
@@ -651,10 +639,15 @@
         copy.start()
         rim_copies.append(copy)
 
+    s1_copy(2).wait()
     backward_conv(1)
-    flip_enc(6, 9)
+    s1_add(2)
+    s2_pack(2)
+    flip_enc(4, 6)
+    s2_start(2)
     backward_conv(2)
     backward_after(1)
+    flip_enc(6, 9)
     backward_after(2)
 
     for copy in rim_copies:
@@ -780,7 +773,7 @@
         pltpu.VMEM((LAT, UNET), BF16),
         pltpu.VMEM((9, UNET, UNET), BF16),
         pltpu.VMEM((LAT, UNET), BF16),
-        dma((8,)),
+        dma((12,)),
         pltpu.VMEM((9, HID, FEAT), BF16),
         pltpu.VMEM((9, UNET, UNET), BF16),
         pltpu.VMEM((4 * HID, 128), BF16),

time: 66.2 us -> 67.7 us (1.023)
  Pallas kernels: 64.8 us -> 66.3 us
    pallas_call x1, Pallas kernels: 63.2 us -> 64.7 us  [per_device(): pl.pallas_call(kernel, out_shape=shapes, in_specs=[pl.BlockSpec(memory_sp...]
where the time goes in v8:
time: 67.7 us; the launch traced here: 67.6 us
  Pallas kernels  66.3 us (98%)
  between operations  1.29 us (2%)
    pallas_call x1, Pallas kernels, per_device(): pl.pallas_call(kernel, out_shape=shapes, in_specs=[pl.BlockSpec(memory_sp...  64.7 us
    pallas_call x1, Pallas kernels, per_device(): pl.pallas_call(hand_over, out_shape=shapes, in_specs=[vmem, vmem], out_sp...  1.59 us

profile of v8, /device:TPU:0, one launch (start us, length us, event | category | flops | bytes accessed | tf_op | source)
XLA Modules:
  0.0 67.6 jit_solution(6358711589075154461)
XLA Ops:
  1.3 64.7 %shard_map.104 = (f32[8,16,256]{2,1,0:T(8,128)}, f32[9,3,384]{2,1,0:T(4,128)}) custom-call(s32[1]{0:T(128)S(6)} %copy.11.time_ref, bf16[8,16,256]{2,1,0:T(8,128)(2,1)} %feat_hbm.1, bf16[9,256,512]{2,1,0:T(8,128)(2,1)} %enc_hbm.1, bf16[32,512]{1,0:T(8,128)(2,1)} %bitcast.4, bf16[1,8,8192]{2,1,0:T(8,128)(2,1)} %noise_hbm.1, bf16[1000,384]{1,0:T(8,128)(2,1)} %table_hbm.1, ...), custom_call_target="tpu_custom_call" | custom-call | flops 17999998976 | bytes 8000000 | tf_op jit(solution)/shard_map/pallas_call | solution.py:855
  66.0 1.6 %shard_map.105 = (f32[8,16,256]{2,1,0:T(8,128)}, f32[9,3,384]{2,1,0:T(4,128)}) custom-call(f32[8,16,256]{2,1,0:T(8,128)} %get-tuple-element.6.fgrad_ref, f32[9,3,384]{2,1,0:T(4,128)} %get-tuple-element.7.mgrad_ref), custom_call_target="tpu_custom_call" | custom-call | tf_op jit(solution)/shard_map/pallas_call | solution.py:866

commit v9 on v5

--- a/solution.py
+++ b/solution.py
@@ -467,36 +467,61 @@
                 parts.append(ref[pl.ds(base + (there // 2) * 32 + there % 2, 16, stride=2), :])
         return jnp.concatenate(parts, axis=1)
 
-    def s2_copy(a, b, k):
-        _, tile, step = axis_peer(first_axis[b], k)
-        index = (a * 3 + b) * 3 + k - 1
+    onward = (3, 1)
+
+    def s2_offset(a, slot):
+        if a == 2:
+            return slot + 1
+        return onward[a] if slot else 4 - onward[a]
+
+    def s2_copy(a, b, slot):
+        _, tile, step = axis_peer(first_axis[b], s2_offset(a, slot))
+        index = (a * 3 + b) * 3 + slot
         return remote(s2_send.at[index], s2_recv.at[index], s2_ss.at[index], s2_rs.at[index], tile, step)
 
     def s2_pack(a):
         for b in range(3):
-            for k in range(1, 4):
-                there = axis_peer(first_axis[b], k)[0]
+            for slot in range(3 if a == 2 else 2):
+                away = 2 if a < 2 and slot else s2_offset(a, slot)
+                there = axis_peer(first_axis[b], away)[0]
                 for c in range(3):
                     block = plane_rows(a, b, c, there).astype(BF16)
-                    s2_send[(a * 3 + b) * 3 + k - 1, 16 * c : 16 * c + 16, :] = block
+                    s2_send[(a * 3 + b) * 3 + slot, 16 * c : 16 * c + 16, :] = block
 
     def s2_start(a):
-        for k in (2, 1, 3):
+        for slot in (1, 0, 2) if a == 2 else (1, 0):
             for b in range(3):
-                s2_copy(a, b, k).start()
+                s2_copy(a, b, slot).start()
+
+    def s2_hand_wait(a):
+        for b in range(3):
+            s2_copy(a, b, 1).wait()
+
+    def s2_hand_pack(a):
+        for b in range(3):
+            there = axis_peer(first_axis[b], onward[a])[0]
+            index = (a * 3 + b) * 3
+            for c in range(3):
+                rows = slice(16 * c, 16 * c + 16)
+                block = plane_rows(a, b, c, there) + s2_recv[index + 1, rows, :].astype(F32)
+                s2_send[index + 2, rows, :] = block.astype(BF16)
+
+    def s2_hand_start(a):
+        for b in range(3):
+            s2_copy(a, b, 2).start()
 
     def s2_wait(a):
         for b in range(3):
-            for k in range(1, 4):
-                s2_copy(a, b, k).wait()
+            for slot in range(3) if a == 2 else (0, 2):
+                s2_copy(a, b, slot).wait()
 
     def s2_add(a):
         for b in range(3):
             mine = axis_peer(first_axis[b], 0)[0]
             for c in range(3):
                 total = plane_rows(a, b, c, mine)
-                for k in range(3):
-                    total = total + s2_recv[(a * 3 + b) * 3 + k, 16 * c : 16 * c + 16, :].astype(F32)
+                for slot in range(3) if a == 2 else (0, 2):
+                    total = total + s2_recv[(a * 3 + b) * 3 + slot, 16 * c : 16 * c + 16, :].astype(F32)
                 row = 16 * (3 * a + c)
                 for i, part in enumerate(lane_tiles(total)):
                     sum2[b * 3 + i, row : row + 16, :] = part
@@ -585,9 +610,14 @@
         weight_product(a)
         for k in range(3 * a, 3 * a + 3):
             mid_t[k] = jnp.transpose(midw[k])
-        if a:
-            s1_pack(a - 1)
-            s1_copy(a - 1).start()
+        if a == 2:
+            s1_add(0)
+            s2_pack(0)
+            s2_start(0)
+        s1_pack(a)
+        s1_copy(a).start()
+        if a == 1:
+            s1_copy(0).wait()
 
     for row, copy in ((9, halo_copies[0]), (0, halo_copies[1])):
         copy.wait()
@@ -621,35 +651,33 @@
         for k in range(first, last):
             enc_t[k] = jnp.transpose(enc[k])
 
-    s1_copy(0).wait()
+    s1_copy(1).wait()
     backward_conv(0)
-    s1_pack(2)
-    s1_add(0)
-    s2_pack(0)
+    s1_add(1)
+    s2_pack(1)
     flip_enc(0, 3)
-    s1_copy(2).start()
-    s2_start(0)
-
-    s1_copy(1).wait()
+    s2_start(1)
+
+    s1_copy(2).wait()
+    s2_hand_wait(0)
     backward_conv(1)
     backward_after(0)
-    s1_add(1)
-    s2_pack(1)
+    s1_add(2)
+    s2_pack(2)
+    s2_hand_pack(0)
     flip_enc(3, 6)
-    s2_start(1)
-
-    s1_copy(2).wait()
+    s2_start(2)
+    s2_hand_start(0)
+
+    s2_hand_wait(1)
     backward_conv(2)
     backward_after(1)
-    s1_add(2)
-    s2_pack(2)
+    s2_hand_pack(1)
     flip_enc(6, 9)
-    s2_start(2)
-
-    s2_wait(0)
+    s2_hand_start(1)
+
     backward_conv(3)
     backward_after(2)
-    s2_add(0)
     backward_after(3)
 
     def part_copy(k):
@@ -662,7 +690,7 @@
     for k in range(1, STEPS):
         part_copy(k).start()
 
-    for a in (1, 2):
+    for a in range(3):
         s2_wait(a)
         s2_add(a)
     s3_start()

time: 65.8 us -> 66.7 us (1.014)
  Pallas kernels: 63.4 us -> 64.3 us
    pallas_call x1, Pallas kernels: 61.9 us -> 62.8 us  [per_device(): pl.pallas_call(kernel, out_shape=shapes, in_specs=[pl.BlockSpec(memory_sp...]
where the time goes in v9:
time: 66.7 us; the launch traced here: 65.6 us
  Pallas kernels  64.3 us (96%)
  between operations  1.29 us (2%)
    pallas_call x1, Pallas kernels, per_device(): pl.pallas_call(kernel, out_shape=shapes, in_specs=[pl.BlockSpec(memory_sp...  62.8 us
    pallas_call x1, Pallas kernels, per_device(): pl.pallas_call(hand_over, out_shape=shapes, in_specs=[vmem, vmem], out_sp...  1.59 us

profile of v9, /device:TPU:0, one launch (start us, length us, event | category | flops | bytes accessed | tf_op | source)
XLA Modules:
  0.0 65.6 jit_solution(7420104727938200870)
XLA Ops:
  1.3 62.8 %shard_map.104 = (f32[8,16,256]{2,1,0:T(8,128)}, f32[9,3,384]{2,1,0:T(4,128)}) custom-call(s32[1]{0:T(128)S(6)} %copy.11.time_ref, bf16[8,16,256]{2,1,0:T(8,128)(2,1)} %feat_hbm.1, bf16[9,256,512]{2,1,0:T(8,128)(2,1)} %enc_hbm.1, bf16[32,512]{1,0:T(8,128)(2,1)} %bitcast.4, bf16[1,8,8192]{2,1,0:T(8,128)(2,1)} %noise_hbm.1, bf16[1000,384]{1,0:T(8,128)(2,1)} %table_hbm.1, ...), custom_call_target="tpu_custom_call" | custom-call | flops 17999998976 | bytes 8000000 | tf_op jit(solution)/shard_map/pallas_call | solution.py:881
  64.0 1.6 %shard_map.105 = (f32[8,16,256]{2,1,0:T(8,128)}, f32[9,3,384]{2,1,0:T(4,128)}) custom-call(f32[8,16,256]{2,1,0:T(8,128)} %get-tuple-element.6.fgrad_ref, f32[9,3,384]{2,1,0:T(4,128)} %get-tuple-element.7.mgrad_ref), custom_call_target="tpu_custom_call" | custom-call | tf_op jit(solution)/shard_map/pallas_call | solution.py:892

commit v10 on v5

--- a/solution.py
+++ b/solution.py
@@ -106,10 +106,9 @@
     hidden_even,
     hidden_odd,
     out_grid,
+    order,
     grad,
-    s1_send,
     s1_recv,
-    sum1,
     s2_send,
     s2_recv,
     sum2,
@@ -300,6 +299,19 @@
     for k in range(1, STEPS):
         lat_copy(k).start()
 
+    place = lax.broadcasted_iota(jnp.int32, (16, UNET), 0)
+    channel = lax.broadcasted_iota(jnp.int32, (16, UNET), 1)
+    planes = (
+        ((place >> 2) & 1) * 64 + (place & 3) * 16 + (place >> 3) * 2,
+        (place >> 3) * 64 + ((place >> 1) & 3) * 4 + (place & 1) * 2,
+        (place >> 2) * 16 + (place & 3) * 4,
+    )
+    for b in range(3):
+        for block in range(24):
+            half, f, c = block // 12, block // 3 % 4, block % 3
+            along = (f * 4, f * 16, (f // 2) * 64 + (f % 2) * 2)[b]
+            picked = channel == (planes[b] + (along + half)) * 3 + c
+            order[b, 16 * block : 16 * block + 16, :] = jnp.where(picked, 1.0, 0.0).astype(BF16)
     inw4_t[...] = jnp.transpose(inw4[...])
     outw4[...] = jnp.transpose(outw4_t[...])
     chosen = time_ref[0]
@@ -423,21 +435,7 @@
     halo_start(1)
 
     def s1_copy(a):
-        return remote(s1_send.at[a], s1_recv.at[a], s1_ss.at[a], s1_rs.at[a], t, s + 1 - 2 * core)
-
-    def s1_pack(a):
-        for n in range(9):
-            first = (n // 3) * UNET + n % 3 + 3 * (1 - core)
-            block = jnp.concatenate([grad[a * 3 + i, pl.ds(first, 64, stride=6), :] for i in range(3)], axis=1)
-            s1_send[a, 64 * n : 64 * n + 64, :] = block.astype(BF16)
-
-    def s1_add(a):
-        for n in range(9):
-            first = (n // 3) * UNET + n % 3 + 3 * core
-            got = s1_recv[a, 64 * n : 64 * n + 64, :].astype(F32)
-            for i in range(3):
-                own = grad[a * 3 + i, pl.ds(first, 64, stride=6), :]
-                sum1[a * 3 + i, 64 * n : 64 * n + 64, :] = own + got[:, 128 * i : 128 * i + 128]
+        return remote(grad.at[a, 1 - core], s1_recv.at[a], s1_ss.at[a], s1_rs.at[a], t, s + 1 - 2 * core)
 
     def axis_peer(axis, k):
         if axis == "z":
@@ -451,21 +449,9 @@
 
     first_axis, second_axis, third_axis = ("z", "x", "y"), ("x", "z", "z"), ("y", "y", "x")
 
-    def plane_rows(a, b, c, there):
-        base = (3 * b + c) * 64
-        parts = []
-        for i in range(3):
-            ref = sum1.at[a * 3 + i]
-            if b == 0:
-                parts.append(
-                    jnp.concatenate([ref[pl.ds(base + 2 * there + low, 8, stride=8), :] for low in (0, 1)], axis=0)
-                )
-            elif b == 1:
-                rows = [pl.ds(pl.multiple_of(base + high * 32 + there * 8, 8), 8) for high in (0, 1)]
-                parts.append(jnp.concatenate([ref[row, :] for row in rows], axis=0))
-            else:
-                parts.append(ref[pl.ds(base + (there // 2) * 32 + there % 2, 16, stride=2), :])
-        return jnp.concatenate(parts, axis=1)
+    def plane_rows(a, b, there):
+        rows = pl.ds(pl.multiple_of(there * 48, 16), 48)
+        return grad[a, core, b, rows, :].astype(F32) + s1_recv[a, b, rows, :].astype(F32)
 
     def s2_copy(a, b, k):
         _, tile, step = axis_peer(first_axis[b], k)
@@ -476,9 +462,7 @@
         for b in range(3):
             for k in range(1, 4):
                 there = axis_peer(first_axis[b], k)[0]
-                for c in range(3):
-                    block = plane_rows(a, b, c, there).astype(BF16)
-                    s2_send[(a * 3 + b) * 3 + k - 1, 16 * c : 16 * c + 16, :] = block
+                s2_send[(a * 3 + b) * 3 + k - 1] = plane_rows(a, b, there).astype(BF16)
 
     def s2_start(a):
         for k in (2, 1, 3):
@@ -493,13 +477,11 @@
     def s2_add(a):
         for b in range(3):
             mine = axis_peer(first_axis[b], 0)[0]
-            for c in range(3):
-                total = plane_rows(a, b, c, mine)
-                for k in range(3):
-                    total = total + s2_recv[(a * 3 + b) * 3 + k, 16 * c : 16 * c + 16, :].astype(F32)
-                row = 16 * (3 * a + c)
-                for i, part in enumerate(lane_tiles(total)):
-                    sum2[b * 3 + i, row : row + 16, :] = part
+            total = plane_rows(a, b, mine)
+            for k in range(3):
+                total = total + s2_recv[(a * 3 + b) * 3 + k].astype(F32)
+            for i, part in enumerate(lane_tiles(total)):
+                sum2[b * 3 + i, 48 * a : 48 * a + 48, :] = part
 
     def line_rows(b, there):
         parts = []
@@ -576,8 +558,10 @@
             jnp.concatenate([inner_t[r + a, :, 128:384] for r in range(8)], axis=1),
         ]
         result = dot(jnp.concatenate(taps, axis=0), back_ext[1:9, 64:320, :].reshape(2048, UNET))
-        for i, part in enumerate(lane_tiles(result)):
-            grad[a * 3 + i] = part
+        for b in range(3):
+            ordered = dot(order[b], result[UNET * b : UNET * b + UNET].astype(BF16)).astype(BF16)
+            grad[a, 0, b] = ordered[0:192]
+            grad[a, 1, b] = ordered[192:384]
 
     sum2[...] = jnp.zeros_like(sum2)
     sum3[...] = jnp.zeros_like(sum3)
@@ -585,9 +569,7 @@
         weight_product(a)
         for k in range(3 * a, 3 * a + 3):
             mid_t[k] = jnp.transpose(midw[k])
-        if a:
-            s1_pack(a - 1)
-            s1_copy(a - 1).start()
+        s1_copy(a).start()
 
     for row, copy in ((9, halo_copies[0]), (0, halo_copies[1])):
         copy.wait()
@@ -622,29 +604,24 @@
             enc_t[k] = jnp.transpose(enc[k])
 
     s1_copy(0).wait()
+    s1_copy(1).wait()
     backward_conv(0)
-    s1_pack(2)
-    s1_add(0)
     s2_pack(0)
+    s2_pack(1)
     flip_enc(0, 3)
-    s1_copy(2).start()
     s2_start(0)
-
-    s1_copy(1).wait()
+    s2_start(1)
+
+    s1_copy(2).wait()
     backward_conv(1)
     backward_after(0)
-    s1_add(1)
-    s2_pack(1)
+    s2_pack(2)
     flip_enc(3, 6)
-    s2_start(1)
-
-    s1_copy(2).wait()
+    s2_start(2)
+
     backward_conv(2)
     backward_after(1)
-    s1_add(2)
-    s2_pack(2)
     flip_enc(6, 9)
-    s2_start(2)
 
     s2_wait(0)
     backward_conv(3)
@@ -813,10 +790,9 @@
         pltpu.VMEM((6, 80, HID), BF16),
         pltpu.VMEM((6, 72, HID), BF16),
         pltpu.VMEM((2, 256, 128), F32),
-        pltpu.VMEM((9, 3 * UNET, 128), F32),
-        pltpu.VMEM((3, 576, UNET), BF16),
-        pltpu.VMEM((3, 576, UNET), BF16),
-        pltpu.VMEM((9, 576, 128), F32),
+        pltpu.VMEM((3, UNET, UNET), BF16),
+        pltpu.VMEM((3, 2, 3, 192, UNET), BF16),
+        pltpu.VMEM((3, 3, 192, UNET), BF16),
         pltpu.VMEM((27, 48, UNET), BF16),
         pltpu.VMEM((27, 48, UNET), BF16),
         pltpu.VMEM((9, 256, 128), F32),

time: 65.8 us -> 67.2 us (1.021)
  Pallas kernels: 63.4 us -> 64.8 us
    pallas_call x1, Pallas kernels: 61.9 us -> 63.2 us  [per_device(): pl.pallas_call(kernel, out_shape=shapes, in_specs=[pl.BlockSpec(memory_sp...]
where the time goes in v10:
time: 67.2 us; the launch traced here: 66 us
  Pallas kernels  64.8 us (96%)
  between operations  1.29 us (2%)
    pallas_call x1, Pallas kernels, per_device(): pl.pallas_call(kernel, out_shape=shapes, in_specs=[pl.BlockSpec(memory_sp...  63.2 us
    pallas_call x1, Pallas kernels, per_device(): pl.pallas_call(hand_over, out_shape=shapes, in_specs=[vmem, vmem], out_sp...  1.59 us

profile of v10, /device:TPU:0, one launch (start us, length us, event | category | flops | bytes accessed | tf_op | source)
XLA Modules:
  0.0 66.0 jit_solution(7313833814833158848)
XLA Ops:
  1.3 63.2 %shard_map.104 = (f32[8,16,256]{2,1,0:T(8,128)}, f32[9,3,384]{2,1,0:T(4,128)}) custom-call(s32[1]{0:T(128)S(6)} %copy.11.time_ref, bf16[8,16,256]{2,1,0:T(8,128)(2,1)} %feat_hbm.1, bf16[9,256,512]{2,1,0:T(8,128)(2,1)} %enc_hbm.1, bf16[32,512]{1,0:T(8,128)(2,1)} %bitcast.4, bf16[1,8,8192]{2,1,0:T(8,128)(2,1)} %noise_hbm.1, bf16[1000,384]{1,0:T(8,128)(2,1)} %table_hbm.1, ...), custom_call_target="tpu_custom_call" | custom-call | flops 17999998976 | bytes 8000000 | tf_op jit(solution)/shard_map/pallas_call | solution.py:829
  64.5 1.6 %shard_map.105 = (f32[8,16,256]{2,1,0:T(8,128)}, f32[9,3,384]{2,1,0:T(4,128)}) custom-call(f32[8,16,256]{2,1,0:T(8,128)} %get-tuple-element.6.fgrad_ref, f32[9,3,384]{2,1,0:T(4,128)} %get-tuple-element.7.mgrad_ref), custom_call_target="tpu_custom_call" | custom-call | tf_op jit(solution)/shard_map/pallas_call | solution.py:840

commit v11 on v6

--- a/solution.py
+++ b/solution.py
@@ -65,8 +65,7 @@
     midw,
     outw,
     in_sem,
-    enc_t,
-    mid_t,
+    mid_sums,
     latw4,
     latw4_t,
     inw4,
@@ -91,8 +90,10 @@
     noise_edge_in,
     inner_ext,
     inner_slope,
-    inner_t,
-    inner_tm,
+    mixes,
+    mixes_t,
+    mixes_tm,
+    back_mixes,
     pre_middle,
     back_mixed,
     back_ext,
@@ -311,6 +312,11 @@
     embed[...] = dot(onehot, table[...])[0:8]
 
     l_midw.wait()
+    for b in range(3):
+        ends = midw[b].astype(F32) + midw[6 + b].astype(F32)
+        centre = midw[3 + b].astype(F32)
+        mid_sums[0, b] = (0.5 * (ends + centre)).astype(BF16)
+        mid_sums[1, b] = (0.5 * (ends - centre)).astype(BF16)
     for side in (0, 1):
         noise_copies[side].wait()
     noise_rows[576:640, :] = noise_edge_in[0].astype(F32)
@@ -346,13 +352,39 @@
                 if j == 3:
                     inner_ext[row, 0:64, :] = shift_down(own).astype(BF16)
                 if 0 < row < 9:
-                    inner_slope[row - 1, 64 * j : 64 * j + 64, :] = slope[64 * r : 64 * r + 64]
-
-    def flip_rows(first, last):
-        for row in range(first, last):
-            flipped = jnp.transpose(inner_ext[row])
-            inner_t[row] = flipped
-            inner_tm[row] = flipped[:, 64:320]
+                    inner_slope[row - 1, 64 * j : 64 * j + 64, :] = slope[64 * r : 64 * r + 64].astype(BF16)
+
+    def mix_rows(ref, pair):
+        d = [ref[2 * pair + r] for r in range(4)]
+        mixes[pair, 0] = d[0] - d[2]
+        mixes[pair, 1] = d[1] + d[2]
+        mixes[pair, 2] = d[2] - d[1]
+        mixes[pair, 3] = d[1] - d[3]
+
+    def flip_mixes(pair):
+        for k in range(4):
+            flipped = jnp.transpose(mixes[pair, k])
+            mixes_t[pair, k] = flipped
+            mixes_tm[UNET * (4 * pair + k) : UNET * (4 * pair + k + 1), :] = flipped[:, 64:320]
+
+    def mixed_conv(i, weights):
+        for k in (1, 2, 0, 3):
+            windows = [mixes[2 * i : 2 * i + 2, k, 64 * b : 64 * b + 256, :].reshape(512, UNET) for b in range(3)]
+            part = dot(jnp.concatenate(windows, axis=1), weights[k])
+            for pair in range(2):
+                own = part[256 * pair : 256 * pair + 256]
+                even = slice(512 * pair, 512 * pair + 256)
+                odd = slice(512 * pair + 256, 512 * pair + 512)
+                if k == 1:
+                    pre_middle[i, even, :] = own
+                    pre_middle[i, odd, :] = own
+                elif k == 2:
+                    pre_middle[i, even, :] += own
+                    pre_middle[i, odd, :] -= own
+                elif k == 0:
+                    pre_middle[i, even, :] += own
+                else:
+                    pre_middle[i, odd, :] -= own
 
     def by_class(value):
         rows = value.shape[0] // 256
@@ -371,12 +403,8 @@
         )
 
     def forward_conv(i):
-        windows = [
-            inner_ext[4 * i + a : 4 * i + a + 4, 64 * b : 64 * b + 256, :].reshape(1024, UNET)
-            for a in range(3)
-            for b in range(3)
-        ]
-        pre_middle[i] = dot(jnp.concatenate(windows, axis=1), midw[...].reshape(9 * UNET, UNET))
+        weights = [midw[0:3], mid_sums[0], mid_sums[1], midw[6:9]]
+        mixed_conv(i, [weight.reshape(3 * UNET, UNET) for weight in weights])
 
     def forward_after(i):
         r = 4 * i
@@ -395,6 +423,10 @@
             back_ext[r + 1 + row, 64:320, :] = own.astype(BF16)
             back_ext[r + 1 + row, 320:384, :] = shift_up(own[0:64]).astype(BF16)
             back_ext[r + 1 + row, 0:64, :] = shift_down(own[192:256]).astype(BF16)
+        for pair in range(2):
+            first, second = back[512 * pair : 512 * pair + 256], back[512 * pair + 256 : 512 * pair + 512]
+            back_mixes[2 * i + pair, 0] = (0.5 * (first + second)).astype(BF16)
+            back_mixes[2 * i + pair, 1] = (0.5 * (first - second)).astype(BF16)
 
     halo_copies = []
 
@@ -407,12 +439,18 @@
         halo_copies.append(copy)
 
     input_rows(0, 6)
+    mix_rows(inner_ext, 0)
+    mix_rows(inner_ext, 1)
     forward_conv(0)
     input_rows(6, 4)
-    flip_rows(0, 5)
+    mix_rows(inner_ext, 2)
+    mix_rows(inner_ext, 3)
+    flip_mixes(0)
+    flip_mixes(1)
     forward_conv(1)
     forward_after(0)
-    flip_rows(5, 10)
+    flip_mixes(2)
+    flip_mixes(3)
     halo_start(0)
     forward_after(1)
     halo_start(1)
@@ -564,30 +602,51 @@
             for a in range(3):
                 mgrad_ref[3 * a + b] = total[3 * a : 3 * a + 3]
 
-    def weight_product(a):
+    def weight_product(k):
         taps = [
-            jnp.concatenate([inner_t[r + a, :, 0:256] for r in range(8)], axis=1),
-            jnp.concatenate([inner_tm[r + a] for r in range(8)], axis=1),
-            jnp.concatenate([inner_t[r + a, :, 128:384] for r in range(8)], axis=1),
+            jnp.concatenate([mixes_t[pair, k, :, 0:256] for pair in range(4)], axis=1),
+            jnp.concatenate(
+                [mixes_tm[UNET * (4 * pair + k) : UNET * (4 * pair + k + 1), :] for pair in range(4)], axis=1
+            ),
+            jnp.concatenate([mixes_t[pair, k, :, 128:384] for pair in range(4)], axis=1),
         ]
-        result = dot(jnp.concatenate(taps, axis=0), back_ext[1:9, 64:320, :].reshape(2048, UNET))
-        for i, part in enumerate(lane_tiles(result)):
-            grad[a * 3 + i] = part
+        if k in (0, 3):
+            right = [back_ext[1 + 2 * pair + k // 3, 64:320, :] for pair in range(4)]
+        else:
+            right = [back_mixes[pair, k - 1] for pair in range(4)]
+        return lane_tiles(dot(jnp.concatenate(taps, axis=0), jnp.concatenate(right, axis=0)))
+
+    def flip_mid(k):
+        for b in range(3):
+            source = (midw.at[8 - b], mid_sums.at[0, 2 - b], mid_sums.at[1, 2 - b], midw.at[2 - b])[k]
+            inner_ext[3 * k + b] = jnp.transpose(source[...])
 
     sum2[...] = jnp.zeros_like(sum2)
     sum3[...] = jnp.zeros_like(sum3)
-    for a in range(3):
-        weight_product(a)
-        for k in range(3 * a, 3 * a + 3):
-            mid_t[k] = jnp.transpose(midw[k])
-        if a == 2:
-            s1_add(0)
-            s2_pack(0)
-            s2_start(0)
-        s1_pack(a)
-        s1_copy(a).start()
-        if a == 1:
-            s1_copy(0).wait()
+    for i, part in enumerate(weight_product(1)):
+        grad[i] = part
+        grad[3 + i] = part
+        grad[6 + i] = part
+    flip_mid(0)
+    for i, part in enumerate(weight_product(2)):
+        grad[i] += part
+        grad[3 + i] -= part
+        grad[6 + i] += part
+    flip_mid(1)
+    s1_pack(1)
+    s1_copy(1).start()
+    for i, part in enumerate(weight_product(0)):
+        grad[i] += part
+    flip_mid(2)
+    mix_rows(back_ext, 1)
+    s1_pack(0)
+    s1_copy(0).start()
+    for i, part in enumerate(weight_product(3)):
+        grad[6 + i] -= part
+    flip_mid(3)
+    mix_rows(back_ext, 2)
+    s1_pack(2)
+    s1_copy(2).start()
 
     for row, copy in ((9, halo_copies[0]), (0, halo_copies[1])):
         copy.wait()
@@ -603,30 +662,29 @@
         back_ext[9] = jnp.zeros_like(back_ext[9])
 
     def backward_conv(i):
-        r = 4 * i
-        windows = [
-            back_ext[r + 2 - a : r + 6 - a, 64 * (2 - b) : 64 * (2 - b) + 256, :].reshape(1024, UNET)
-            for a in range(3)
-            for b in range(3)
-        ]
-        pre_middle[i] = dot(jnp.concatenate(windows, axis=1), mid_t[...].reshape(9 * UNET, UNET))
+        mixed_conv(i, [inner_ext[3 * k : 3 * k + 3].reshape(3 * UNET, UNET) for k in range(4)])
 
     def backward_after(i):
         r = 4 * i
         through = pre_middle[i] + back_mixed[256 * r : 256 * r + 1024, :]
-        back = (through * inner_slope[r : r + 4].reshape(1024, UNET)).astype(BF16)
+        back = (through * inner_slope[r : r + 4].reshape(1024, UNET).astype(F32)).astype(BF16)
         back_part[64 * r : 64 * r + 256, :] = cosine * dot(by_class(back), inw4_t[...])
 
     def flip_enc(first, last):
         for k in range(first, last):
-            enc_t[k] = jnp.transpose(enc[k])
-
+            mixes_tm[HID * k : HID * k + HID, :] = jnp.transpose(enc[k])
+
+    mix_rows(back_ext, 0)
+    mix_rows(back_ext, 3)
     s1_copy(1).wait()
+    s1_copy(0).wait()
     backward_conv(0)
-    s1_add(1)
-    s2_pack(1)
+    for a in (1, 0):
+        s1_add(a)
+        s2_pack(a)
     flip_enc(0, 5)
     s2_start(1)
+    s2_start(0)
 
     s1_copy(2).wait()
     backward_conv(1)
@@ -707,7 +765,7 @@
             else:
                 window = hidden_even[2 - b : 6 - b, 8 * (2 - a) : 8 * (2 - a) + 64, :]
             pieces.append(window.reshape(256, HID))
-    result = dot(jnp.concatenate(pieces, axis=1), enc_t[...].reshape(9 * HID, FEAT))
+    result = dot(jnp.concatenate(pieces, axis=1), mixes_tm[0 : 9 * HID, :])
     for j in range(4):
         for i, part in enumerate(lane_tiles(result[64 * j : 64 * j + 64])):
             out_grid[i, pl.ds(j, 64, stride=4), :] = part
@@ -757,8 +815,7 @@
         pltpu.VMEM((9, UNET, UNET), BF16),
         pltpu.VMEM((LAT, UNET), BF16),
         dma((8,)),
-        pltpu.VMEM((9, HID, FEAT), BF16),
-        pltpu.VMEM((9, UNET, UNET), BF16),
+        pltpu.VMEM((2, 3, UNET, UNET), BF16),
         pltpu.VMEM((4 * HID, 128), BF16),
         pltpu.VMEM((128, 4 * HID), BF16),
         pltpu.VMEM((128, 4 * UNET), BF16),
@@ -781,10 +838,12 @@
         pltpu.VMEM((640, 128), F32),
         pltpu.VMEM((2, 64, 128), BF16),
         pltpu.VMEM((2, 64, 128), BF16),
-        pltpu.VMEM((10, 384, UNET), BF16),
-        pltpu.VMEM((8, 256, UNET), F32),
-        pltpu.VMEM((10, UNET, 384), BF16),
-        pltpu.VMEM((10, UNET, 256), BF16),
+        pltpu.VMEM((12, 384, UNET), BF16),
+        pltpu.VMEM((8, 256, UNET), BF16),
+        pltpu.VMEM((4, 4, 384, UNET), BF16),
+        pltpu.VMEM((4, 4, UNET, 384), BF16),
+        pltpu.VMEM((16 * UNET, 256), BF16),
+        pltpu.VMEM((4, 2, 256, UNET), BF16),
         pltpu.VMEM((2, 1024, UNET), F32),
         pltpu.VMEM((2048, UNET), F32),
         pltpu.VMEM((10, 384, UNET), BF16),

time: 66.4 us -> 62 us (0.934)
  Pallas kernels: 64.8 us -> 60.6 us
    pallas_call x1, Pallas kernels: 63.3 us -> 59 us  [per_device(): pl.pallas_call(kernel, out_shape=shapes, in_specs=[pl.BlockSpec(memory_sp...]
where the time goes in v11:
time: 62 us; the launch traced here: 61.9 us
  Pallas kernels  60.6 us (98%)
  between operations  1.29 us (2%)
    pallas_call x1, Pallas kernels, per_device(): pl.pallas_call(kernel, out_shape=shapes, in_specs=[pl.BlockSpec(memory_sp...  59 us
    pallas_call x1, Pallas kernels, per_device(): pl.pallas_call(hand_over, out_shape=shapes, in_specs=[vmem, vmem], out_sp...  1.59 us

profile of v11, /device:TPU:0, one launch (start us, length us, event | category | flops | bytes accessed | tf_op | source)
XLA Modules:
  0.0 61.9 jit_solution(758230982350971958)
XLA Ops:
  1.3 59.0 %shard_map.104 = (f32[8,16,256]{2,1,0:T(8,128)}, f32[9,3,384]{2,1,0:T(4,128)}) custom-call(s32[1]{0:T(128)S(6)} %copy.11.time_ref, bf16[8,16,256]{2,1,0:T(8,128)(2,1)} %feat_hbm.1, bf16[9,256,512]{2,1,0:T(8,128)(2,1)} %enc_hbm.1, bf16[32,512]{1,0:T(8,128)(2,1)} %bitcast.4, bf16[1,8,8192]{2,1,0:T(8,128)(2,1)} %noise_hbm.1, bf16[1000,384]{1,0:T(8,128)(2,1)} %table_hbm.1, ...), custom_call_target="tpu_custom_call" | custom-call | flops 17999998976 | bytes 8000000 | tf_op jit(solution)/shard_map/pallas_call | solution.py:897
  60.3 1.6 %shard_map.105 = (f32[8,16,256]{2,1,0:T(8,128)}, f32[9,3,384]{2,1,0:T(4,128)}) custom-call(f32[8,16,256]{2,1,0:T(8,128)} %get-tuple-element.6.fgrad_ref, f32[9,3,384]{2,1,0:T(4,128)} %get-tuple-element.7.mgrad_ref), custom_call_target="tpu_custom_call" | custom-call | tf_op jit(solution)/shard_map/pallas_call | solution.py:908

commit v12 on v11

--- a/solution.py
+++ b/solution.py
@@ -438,6 +438,20 @@
         copy.start()
         halo_copies.append(copy)
 
+    def weight_product(k, pairs):
+        taps = [
+            jnp.concatenate([mixes_t[pair, k, :, 0:256] for pair in pairs], axis=1),
+            jnp.concatenate(
+                [mixes_tm[UNET * (4 * pair + k) : UNET * (4 * pair + k + 1), :] for pair in pairs], axis=1
+            ),
+            jnp.concatenate([mixes_t[pair, k, :, 128:384] for pair in pairs], axis=1),
+        ]
+        if k in (0, 3):
+            right = [back_ext[1 + 2 * pair + k // 3, 64:320, :] for pair in pairs]
+        else:
+            right = [back_mixes[pair, k - 1] for pair in pairs]
+        return lane_tiles(dot(jnp.concatenate(taps, axis=0), jnp.concatenate(right, axis=0)))
+
     input_rows(0, 6)
     mix_rows(inner_ext, 0)
     mix_rows(inner_ext, 1)
@@ -452,6 +466,10 @@
     flip_mixes(2)
     flip_mixes(3)
     halo_start(0)
+    for i, part in enumerate(weight_product(0, (0, 1))):
+        grad[i] = part
+    for i, part in enumerate(weight_product(3, (0, 1))):
+        grad[6 + i] = -part
     forward_after(1)
     halo_start(1)
 
@@ -602,20 +620,6 @@
             for a in range(3):
                 mgrad_ref[3 * a + b] = total[3 * a : 3 * a + 3]
 
-    def weight_product(k):
-        taps = [
-            jnp.concatenate([mixes_t[pair, k, :, 0:256] for pair in range(4)], axis=1),
-            jnp.concatenate(
-                [mixes_tm[UNET * (4 * pair + k) : UNET * (4 * pair + k + 1), :] for pair in range(4)], axis=1
-            ),
-            jnp.concatenate([mixes_t[pair, k, :, 128:384] for pair in range(4)], axis=1),
-        ]
-        if k in (0, 3):
-            right = [back_ext[1 + 2 * pair + k // 3, 64:320, :] for pair in range(4)]
-        else:
-            right = [back_mixes[pair, k - 1] for pair in range(4)]
-        return lane_tiles(dot(jnp.concatenate(taps, axis=0), jnp.concatenate(right, axis=0)))
-
     def flip_mid(k):
         for b in range(3):
             source = (midw.at[8 - b], mid_sums.at[0, 2 - b], mid_sums.at[1, 2 - b], midw.at[2 - b])[k]
@@ -623,25 +627,25 @@
 
     sum2[...] = jnp.zeros_like(sum2)
     sum3[...] = jnp.zeros_like(sum3)
-    for i, part in enumerate(weight_product(1)):
-        grad[i] = part
+    for i, part in enumerate(weight_product(1, range(4))):
+        grad[i] += part
         grad[3 + i] = part
-        grad[6 + i] = part
+        grad[6 + i] += part
     flip_mid(0)
-    for i, part in enumerate(weight_product(2)):
+    for i, part in enumerate(weight_product(2, range(4))):
         grad[i] += part
         grad[3 + i] -= part
         grad[6 + i] += part
     flip_mid(1)
     s1_pack(1)
     s1_copy(1).start()
-    for i, part in enumerate(weight_product(0)):
+    for i, part in enumerate(weight_product(0, (2, 3))):
         grad[i] += part
     flip_mid(2)
     mix_rows(back_ext, 1)
     s1_pack(0)
     s1_copy(0).start()
-    for i, part in enumerate(weight_product(3)):
+    for i, part in enumerate(weight_product(3, (2, 3))):
         grad[6 + i] -= part
     flip_mid(3)
     mix_rows(back_ext, 2)

time: 62 us -> 64.1 us (1.034)
  Pallas kernels: 60.6 us -> 62.6 us
    pallas_call x1, Pallas kernels: 59 us -> 61.1 us  [per_device(): pl.pallas_call(kernel, out_shape=shapes, in_specs=[pl.BlockSpec(memory_sp...]
where the time goes in v12:
time: 64.1 us; the launch traced here: 63.9 us
  Pallas kernels  62.6 us (98%)
  between operations  1.29 us (2%)
    pallas_call x1, Pallas kernels, per_device(): pl.pallas_call(kernel, out_shape=shapes, in_specs=[pl.BlockSpec(memory_sp...  61.1 us
    pallas_call x1, Pallas kernels, per_device(): pl.pallas_call(hand_over, out_shape=shapes, in_specs=[vmem, vmem], out_sp...  1.59 us

profile of v12, /device:TPU:0, one launch (start us, length us, event | category | flops | bytes accessed | tf_op | source)
XLA Modules:
  0.0 63.9 jit_solution(10920572414464492510)
XLA Ops:
  1.3 61.1 %shard_map.104 = (f32[8,16,256]{2,1,0:T(8,128)}, f32[9,3,384]{2,1,0:T(4,128)}) custom-call(s32[1]{0:T(128)S(6)} %copy.11.time_ref, bf16[8,16,256]{2,1,0:T(8,128)(2,1)} %feat_hbm.1, bf16[9,256,512]{2,1,0:T(8,128)(2,1)} %enc_hbm.1, bf16[32,512]{1,0:T(8,128)(2,1)} %bitcast.4, bf16[1,8,8192]{2,1,0:T(8,128)(2,1)} %noise_hbm.1, bf16[1000,384]{1,0:T(8,128)(2,1)} %table_hbm.1, ...), custom_call_target="tpu_custom_call" | custom-call | flops 17999998976 | bytes 8000000 | tf_op jit(solution)/shard_map/pallas_call | solution.py:901
  62.3 1.6 %shard_map.105 = (f32[8,16,256]{2,1,0:T(8,128)}, f32[9,3,384]{2,1,0:T(4,128)}) custom-call(f32[8,16,256]{2,1,0:T(8,128)} %get-tuple-element.6.fgrad_ref, f32[9,3,384]{2,1,0:T(4,128)} %get-tuple-element.7.mgrad_ref), custom_call_target="tpu_custom_call" | custom-call | tf_op jit(solution)/shard_map/pallas_call | solution.py:912
